TPU v7x, 512 devices: a whole 4x4x16 slice. The times are simulated.
512 devices in a mesh: chan: 32 (over z_lo, x), win: 16 (over z_hi, y, core).
Axes of the slice: x: 4, y: 4, z: 16 (z_hi: 2, z_lo: 8; z = z_hi * 8 + z_lo), core: 2. Of those that a mesh axis runs over, the one named last changes fastest.
Arguments:
- records: bfloat16 [96, 256, 32, 1024], P('chan', None, 'win'), may hold values from -20 to 20
- pairs: int32 [80, 2], replicated, may hold values from 0 to 95, as said below
- owner: int32 [80], replicated, may hold values from 0 to 31, as said below
Outputs:
- cross_spectra: float32 [128, 256, 1024], P('chan', 'win')
Inputs may be any that keep to these rules, and one draw needn't show every extreme that they name: `pairs`: each row holds two channel blocks a < b with b - a from 1 to 3. owner[p] is the chan index of a device holding some block from pairs[p, 0] to pairs[p, 1]; every owner has 2 to 4 pairs.
All inputs are finite; a program needn't handle non-finite values.
Results may differ from a plain program's by a relative error of at most 0.0055.
Values may be sent and summed in bfloat16 or wider, within the bound.
No kernel may reach another device: no remote copies, remote signals or barrier semaphores. Data moves between devices by JAX's collectives and lax.ppermute only.
A program may use at most 64 MiB of HBM per device.

v0:
```python
import math

import jax
import jax.numpy as jnp
from jax import lax
from jax.sharding import PartitionSpec as P

REACH = 3
PCAP = 4


def padded(block, sides, width):
    for axis, dim in sides:
        count = lax.axis_size(axis)
        forward = [(i, i + 1) for i in range(count - 1)]
        backward = [(target, source) for source, target in forward]
        low = lax.ppermute(
            lax.slice_in_dim(block, block.shape[dim] - width, None, axis=dim), axis, forward
        )
        high = lax.ppermute(lax.slice_in_dim(block, 0, width, axis=dim), axis, backward)
        block = jnp.concatenate([low, block, high], axis=dim)
    return block


def basis_table(length, bin_count):
    sample_ids = jnp.arange(length, dtype=jnp.int32)
    bin_ids = jnp.arange(bin_count, dtype=jnp.int32)
    phases = (sample_ids[:, None] * bin_ids[None, :] % length).astype(jnp.float32) * (
        2.0 * math.pi / length
    )
    hann_taper = 0.5 - 0.5 * jnp.cos(sample_ids.astype(jnp.float32) * (2.0 * math.pi / length))
    return jnp.concatenate(
        [hann_taper[:, None] * jnp.cos(phases), -hann_taper[:, None] * jnp.sin(phases)], axis=1
    ).astype(jnp.bfloat16)


def whitened(row_data, basis):
    lead_shape = row_data.shape[:-1]
    flat_rows = row_data.reshape(-1, row_data.shape[-1])
    spectrum = jnp.dot(flat_rows, basis, preferred_element_type=jnp.float32)
    power_mean = jnp.mean(spectrum * spectrum, axis=-1, keepdims=True)
    scaled = (spectrum * lax.rsqrt(power_mean + 1e-06)).astype(jnp.bfloat16)
    return scaled.reshape(lead_shape + (basis.shape[1],))


def cross_sum(first_spec, second_spec, bin_count):
    first_spec = first_spec.astype(jnp.float32)
    second_spec = second_spec.astype(jnp.float32)
    first_real = first_spec[..., :bin_count]
    first_imag = first_spec[..., bin_count:]
    second_real = second_spec[..., :bin_count]
    second_imag = second_spec[..., bin_count:]
    real_part = jnp.sum(first_real * second_real + first_imag * second_imag, axis=-2)
    imag_part = jnp.sum(first_imag * second_real - first_real * second_imag, axis=-2)
    return jnp.concatenate([real_part, imag_part], axis=-1)


def local(records, pairs, owner):
    length = records.shape[-1]
    bin_count = length // 2
    blocks = records.shape[0]
    basis = basis_table(length, bin_count)
    local_rows = lax.all_to_all(records, "win", split_axis=1, concat_axis=2, tiled=True)
    own_spectra = whitened(local_rows, basis)
    nearby = padded(own_spectra, (("chan", 0),), REACH)
    device_at = lax.axis_index("chan")
    is_mine = (owner == device_at).astype(jnp.int32)
    ranking = jnp.cumsum(is_mine) - is_mine
    slot_ids = jnp.arange(PCAP, dtype=jnp.int32)
    picked = is_mine[None, :] * (ranking[None, :] == slot_ids[:, None]).astype(jnp.int32)
    in_use = jnp.sum(picked, axis=1) > 0
    offset_block = device_at * blocks - REACH
    first_at = jnp.where(in_use, jnp.sum(picked * pairs[:, 0][None, :], axis=1) - offset_block, 0)
    second_at = jnp.where(in_use, jnp.sum(picked * pairs[:, 1][None, :], axis=1) - offset_block, 0)
    first_spec = jnp.take(nearby, first_at, axis=0)
    second_spec = jnp.take(nearby, second_at, axis=0)
    partials = cross_sum(first_spec, second_spec, bin_count)
    partials = jnp.where(in_use[:, None, None], partials, jnp.zeros_like(partials))
    return partials


def solution(mesh):
    return jax.shard_map(
        local,
        mesh=mesh,
        in_specs=(P("chan", None, "win", None), P(), P()),
        out_specs=P("chan", "win", None),
        check_vma=False,
    )
```

profile of v0, /device:TPU:152, one launch (start us, length us, event | category | flops | bytes accessed | tf_op | source)
XLA Modules:
  0.0 302.9 jit_solution(13136065880829868010)
XLA Ops:
  0.0 5.7 %copy.13 = bf16[3,256,2,1024]{3,2,0,1:T(2,128)(2,1)} copy(bf16[3,256,2,1024]{3,2,1,0:T(2,128)(2,1)} %param.5) | data formatting | bytes 6291456 | tf_op args[0]
  5.7 13.2 %all-to-all-start = ((bf16[3,256,2,1024]{3,2,0,1:T(2,128)(2,1)}), bf16[3,256,2,1024]{3,2,0,1:T(2,128)(2,1)S(1)}, u32[]{:S(2)}, u32[]{:S(2)}) async-start(bf16[3,256,2,1024]{3,2,0,1:T(2,128)(2,1)} %copy.13), calls=%async_computation | async-start | bytes 6291456 | tf_op jit(solution)/shard_map/all_to_all | solution.py:63
  19.0 9.7 %multiply_convert_fusion.1 = (bf16[1024,512]{1,0:T(8,128)(2,1)}, bf16[1024,512]{1,0:T(8,128)(2,1)}) fusion(f32[1024]{0:T(1024)S(1)} %fusion.13, f32[1024]{0:T(1024)S(1)} %multiply_subtract_fusion), kind=kLoop, calls=%fused_computation.21 | loop fusion | flops 9437184 | bytes 2105344 | tf_op jit(solution)/shard_map/convert.1
  28.7 118.1 %all-to-all-done = bf16[3,256,2,1024]{3,2,0,1:T(2,128)(2,1)S(1)} async-done(((bf16[3,256,2,1024]{3,2,0,1:T(2,128)(2,1)}), bf16[3,256,2,1024]{3,2,0,1:T(2,128)(2,1)S(1)}, u32[]{:S(2)}, u32[]{:S(2)}) %all-to-all-start) | async-done | bytes 3145760 | tf_op jit(solution)/shard_map/all_to_all | solution.py:63
  146.8 5.1 %copy.17 = bf16[3,16,16,2,1024]{4,3,1,2,0:T(2,128)(2,1)} copy(bf16[3,16,16,2,1024]{4,3,0,2,1:T(2,128)(2,1)S(1)} %bitcast.17) | data formatting | bytes 6291456 | tf_op jit(solution)/shard_map/all_to_all | solution.py:63
  151.9 4.0 %reshape.67 = bf16[1536,1024]{1,0:T(8,128)(2,1)S(1)} reshape(bf16[3,16,16,2,1024]{4,3,2,1,0:T(2,128)(2,1)} %bitcast.18) | data formatting | bytes 6291456 | tf_op jit(solution)/shard_map/reshape | solution.py:39
  155.9 5.0 %multiply_reduce_fusion = (f32[1536]{0:T(1024)S(1)}, f32[1024,1536]{1,0:T(8,128)S(1)}) fusion(bf16[1536,1024]{1,0:T(8,128)(2,1)S(1)} %reshape.67, bf16[1024,512]{1,0:T(8,128)(2,1)} %get-tuple-element.22, bf16[1024,512]{1,0:T(8,128)(2,1)} %get-tuple-element.23), kind=kOutput, calls=%fused_computation.4 | convolution fusion | flops 3228563968 | bytes 11540480 | tf_op jit(solution)/shard_map/dot_general | solution.py:40
  161.0 2.5 fusion
  163.5 0.0 copy-start.2
  163.5 0.0 copy-start.1
  163.5 3.2 %copy.15 = bf16[1536,1024]{1,0:T(8,128)(2,1)S(1)} copy(bf16[1536,1024]{0,1:T(8,128)(2,1)} %fusion) | data formatting | bytes 6291456 | tf_op jit(solution)/shard_map/convert_element_type | solution.py:42
  166.7 33.3 %collective-permute-start.1 = (bf16[3,16,32,1024]{3,2,1,0:T(8,128)(2,1)S(1)}, bf16[3,16,32,1024]{3,2,1,0:T(8,128)(2,1)}, u32[]{:S(2)}, u32[]{:S(2)}) collective-permute-start(bf16[3,16,32,1024]{3,2,1,0:T(8,128)(2,1)S(1)} %bitcast.14), channel_id=1, source_target_pairs={{16,0},{32,16},{48,32},{64,48},{80,64},{96,80},{112,96},{128,112},... | collective-permute-start | bytes 9437192 | tf_op jit(solution)/shard_map/ppermute | solution.py:20
  200.0 2.1 collective-permute-start
  202.1 0.0 copy-done.2
  202.2 0.1 copy.12
  202.3 0.1 reduce-window.9
  202.4 0.1 reduce.1
  202.5 0.0 copy-done.1
  202.5 0.2 fusion.11
  202.7 65.0 %collective-permute-done.1 = bf16[3,16,32,1024]{3,2,1,0:T(8,128)(2,1)} collective-permute-done((bf16[3,16,32,1024]{3,2,1,0:T(8,128)(2,1)S(1)}, bf16[3,16,32,1024]{3,2,1,0:T(8,128)(2,1)}, u32[]{:S(2)}, u32[]{:S(2)}) %collective-permute-start.1) | collective-permute-done | bytes 3145760 | tf_op jit(solution)/shard_map/ppermute | solution.py:20
  267.7 7.5 %collective-permute-done = bf16[3,16,32,1024]{3,2,1,0:T(8,128)(2,1)} collective-permute-done((bf16[3,16,32,1024]{3,2,1,0:T(8,128)(2,1)S(1)}, bf16[3,16,32,1024]{3,2,1,0:T(8,128)(2,1)}, u32[]{:S(2)}, u32[]{:S(2)}) %collective-permute-start) | collective-permute-done | bytes 3145760 | tf_op jit(solution)/shard_map/ppermute | solution.py:17
  275.3 6.9 %pad_maximum_fusion = bf16[9,16,32,1024]{3,2,1,0:T(8,128)(2,1)} fusion(bf16[3,16,32,1024]{3,2,1,0:T(8,128)(2,1)} %collective-permute-done.1, bf16[3,16,32,1024]{3,2,1,0:T(8,128)(2,1)S(1)} %bitcast.16, bf16[3,16,32,1024]{3,2,1,0:T(8,128)(2,1)} %collective-permute-done), kind=kLoop, calls=%fused_computation.2 | loop fusion | flops 9437184 | bytes 18874368 | tf_op jit(solution)/shard_map/concatenate | solution.py:21
  282.2 6.6 %gather_fusion.1 = bf16[4,16,32,1024]{3,2,1,0:T(8,128)(2,1)} fusion(bf16[9,16,32,1024]{3,2,1,0:T(8,128)(2,1)} %pad_maximum_fusion, s32[1024]{0:T(1024)S(1)} %get-tuple-element.24), kind=kCustom, calls=%fused_computation.1.clone | custom fusion | bytes 8388624 | tf_op jit(solution)/shard_map/jit(_take)/gather | solution.py:76
  288.8 6.4 %gather_fusion = bf16[4,16,32,1024]{3,2,1,0:T(8,128)(2,1)} fusion(bf16[9,16,32,1024]{3,2,1,0:T(8,128)(2,1)} %pad_maximum_fusion, s32[1024]{0:T(1024)S(1)} %get-tuple-element.25), kind=kCustom, calls=%fused_computation.clone | custom fusion | bytes 8388624 | tf_op jit(solution)/shard_map/jit(_take)/gather | solution.py:75
  295.2 0.0 copy-start
  295.2 2.9 select_convert_fusion.1
  298.2 0.5 copy-done
  298.7 0.6 select_convert_fusion
  299.3 2.8 add_reduce_fusion
  302.1 0.8 maximum_select_fusion
  (9 shorter events, 0.1 us)
Async XLA Ops:
  5.7 141.1 %all-to-all-start = ((bf16[3,256,2,1024]{3,2,0,1:T(2,128)(2,1)}), bf16[3,256,2,1024]{3,2,0,1:T(2,128)(2,1)S(1)}, u32[]{:S(2)}, u32[]{:S(2)}) async-start(bf16[3,256,2,1024]{3,2,0,1:T(2,128)(2,1)} %copy.13), calls=%async_computation | async-start | bytes 6291456 | tf_op jit(solution)/shard_map/all_to_all | solution.py:63
  163.5 38.7 %copy-start.2 = (s32[80]{0:T(128)S(1)}, s32[80]{0:T(128)}, u32[]{:S(2)}) copy-start(s32[80]{0:T(128)} %param.7) | copy-start | bytes 964
  163.5 39.1 %copy-start.1 = (s32[80,2]{0,1:T(2,128)S(1)}, s32[80,2]{0,1:T(2,128)}, u32[]{:S(2)}) copy-start(s32[80,2]{0,1:T(2,128)} %param.6) | copy-start | bytes 1924
  166.7 101.0 %collective-permute-start.1 = (bf16[3,16,32,1024]{3,2,1,0:T(8,128)(2,1)S(1)}, bf16[3,16,32,1024]{3,2,1,0:T(8,128)(2,1)}, u32[]{:S(2)}, u32[]{:S(2)}) collective-permute-start(bf16[3,16,32,1024]{3,2,1,0:T(8,128)(2,1)S(1)} %bitcast.14), channel_id=1, source_target_pairs={{16,0},{32,16},{48,32},{64,48},{80,64},{96,80},{112,96},{128,112},... | collective-permute-start | bytes 9437192 | tf_op jit(solution)/shard_map/ppermute | solution.py:20
  200.0 75.2 %collective-permute-start = (bf16[3,16,32,1024]{3,2,1,0:T(8,128)(2,1)S(1)}, bf16[3,16,32,1024]{3,2,1,0:T(8,128)(2,1)}, u32[]{:S(2)}, u32[]{:S(2)}) collective-permute-start(bf16[3,16,32,1024]{3,2,1,0:T(8,128)(2,1)S(1)} %bitcast.15), channel_id=1, source_target_pairs={{0,16},{16,32},{32,48},{48,64},{64,80},{80,96},{96,112},{112,128},... | collective-permute-start | bytes 9437192 | tf_op jit(solution)/shard_map/ppermute | solution.py:17
  295.2 3.4 %copy-start = (bf16[4,16,32,1024]{3,2,1,0:T(8,128)(2,1)S(1)}, bf16[4,16,32,1024]{3,2,1,0:T(8,128)(2,1)}, u32[]{:S(2)}) copy-start(bf16[4,16,32,1024]{3,2,1,0:T(8,128)(2,1)} %gather_fusion.1) | copy-start | bytes 12582916
where the time goes:
time: 303 us
  waiting for transfers between devices  191 us (63%)
  starting transfers between devices  48.6 us (16%)
  local copies, waits for them, and re-layouts  31.6 us (10%)
  other arithmetic  26.8 us (9%)
  matrix products  5.02 us (2%)
    all_to_all x1, waiting for transfers between devices, local(): lax.all_to_all(records, 'win', split_axis=1, concat_axis=2, tiled=True)  118 us
    ppermute x1, waiting for transfers between devices, padded(): lax.ppermute(lax.slice_in_dim(block, 0, width, axis=dim), axis, backward)  65 us
    ppermute x1, starting transfers between devices, padded(): lax.ppermute(lax.slice_in_dim(block, 0, width, axis=dim), axis, backward)  33.3 us
    all_to_all x1, starting transfers between devices, local(): lax.all_to_all(records, 'win', split_axis=1, concat_axis=2, tiled=True)  13.2 us
    another operation x4, other arithmetic  9.94 us
    ppermute x1, waiting for transfers between devices, padded(): lax.ppermute(lax.slice_in_dim(block, block.shape[dim] - width, None, axis...  7.54 us
    concatenate x1, other arithmetic, padded(): block = jnp.concatenate([low, block, high], axis=dim)  6.94 us
    gather x1, local copies, waits for them, and re-layouts, local(): second_spec = jnp.take(nearby, second_at, axis=0)  6.56 us
  transfers between devices with their start and end apart: 3, of which 3 were waited for; matrix products, arithmetic and copies ran while one was open for 3% of the time, Pallas kernels for 0%

commit v1 on v0

v1 whole, which is shorter than its diff:
```python
import math

import jax
import jax.numpy as jnp
import ml_dtypes
import numpy as np
from jax import lax
from jax.experimental import pallas as pl
from jax.experimental.pallas import tpu as pltpu
from jax.sharding import PartitionSpec as P

PCAP = 4
BLOCKS = 3
CHAN = 32
CHUNKS = 2
LENGTH = 1024
BINS = 512
ROWS = 256 // CHUNKS
VMEM = pl.BlockSpec(memory_space=pltpu.VMEM)
SMEM = pl.BlockSpec(memory_space=pltpu.SMEM)
ANY = pl.BlockSpec(memory_space=pl.ANY)
PARAMS = pltpu.CompilerParams(vmem_limit_bytes=40 << 20)


def basis_table():
    sample_ids = np.arange(LENGTH, dtype=np.int32)
    bin_ids = np.arange(BINS, dtype=np.int32)
    step = np.float32(2.0 * math.pi / LENGTH)
    phases = (sample_ids[:, None] * bin_ids[None, :] % LENGTH).astype(np.float32) * step
    taper = np.float32(0.5) - np.float32(0.5) * np.cos(sample_ids.astype(np.float32) * step)
    table = np.concatenate([taper[:, None] * np.cos(phases), -taper[:, None] * np.sin(phases)], axis=1)
    return table.astype(ml_dtypes.bfloat16)


def lanes(pairs, owner):
    first, second = pairs[:, 0], pairs[:, 1]
    ids = jnp.arange(BLOCKS * CHAN, dtype=jnp.int32)
    right = jnp.any((first[None, :] == ids[:, None]) & (owner[None, :] == ids[:, None] // BLOCKS + 1), axis=1)
    left = jnp.any((second[None, :] == ids[:, None]) & (owner[None, :] == ids[:, None] // BLOCKS - 1), axis=1)
    right = right.astype(jnp.int32).reshape(CHAN, BLOCKS)
    left = left.astype(jnp.int32).reshape(CHAN, BLOCKS)
    most = jnp.maximum(jnp.max(jnp.sum(right, axis=1)), jnp.max(jnp.sum(left, axis=1)))
    return right, left, most


def tables(pairs, owner, right, left, width):
    me = lax.axis_index("chan")
    if width < BLOCKS:
        place_right = jnp.cumsum(right, axis=1) - right
        place_left = jnp.cumsum(left, axis=1) - left
    else:
        place_right = place_left = jnp.broadcast_to(jnp.arange(BLOCKS, dtype=jnp.int32), (CHAN, BLOCKS))
        right = left = jnp.ones((CHAN, BLOCKS), jnp.int32)
    spots = jnp.arange(width, dtype=jnp.int32)
    block_ids = jnp.arange(BLOCKS, dtype=jnp.int32)

    def row(table, at):
        return jnp.sum(jnp.where(jnp.arange(CHAN)[:, None] == at, table, 0), axis=0)

    def chosen(need, place):
        hit = (row(need, me)[None, :] > 0) & (row(place, me)[None, :] == spots[:, None])
        return jnp.sum(jnp.where(hit, block_ids[None, :], 0), axis=1)

    send = jnp.concatenate([chosen(right, place_right), chosen(left, place_left)])
    mine = (owner == me).astype(jnp.int32)
    ranking = jnp.cumsum(mine) - mine
    slots = jnp.arange(PCAP, dtype=jnp.int32)
    picked = mine[None, :] * (ranking[None, :] == slots[:, None]).astype(jnp.int32)
    used = jnp.sum(picked, axis=1)
    first = jnp.sum(picked * pairs[:, 0][None, :], axis=1) - me * BLOCKS
    second = jnp.sum(picked * pairs[:, 1][None, :], axis=1) - me * BLOCKS

    def look(table, index):
        return jnp.sum(jnp.where(index[:, None] == block_ids[None, :], table[None, :], 0), axis=1)

    from_left = BLOCKS + look(row(place_right, me - 1), first + BLOCKS)
    from_right = BLOCKS + width + look(row(place_left, me + 1), second - BLOCKS)
    a = jnp.where(first < 0, from_left, first)
    b = jnp.where(second >= BLOCKS, from_right, second)
    a = jnp.where(used > 0, jnp.clip(a, 0, BLOCKS + 2 * width - 1), 0)
    b = jnp.where(used > 0, jnp.clip(b, 0, BLOCKS + 2 * width - 1), 0)
    return send.astype(jnp.int32), jnp.concatenate([a, b, used]).astype(jnp.int32)


def spectra_kernel(chunk, width, info, x, basis, own0, own1, right0, right1, left0, left1, xbuf, bbuf, spec, xsem, bsem, osem, lsem):
    core = info[2 * width]

    def load(side, block):
        at = (core + side) % 2
        return pltpu.make_async_copy(x.at[block, :, at, chunk], xbuf.at[side, block], xsem.at[side, block])

    table = pltpu.make_async_copy(basis, bbuf, bsem)
    load(0, 0).start()
    table.start()
    for side in range(2):
        for block in range(BLOCKS):
            if (side, block) != (0, 0):
                load(side, block).start()
    table.wait()
    owns = (own0, own1)
    lane_refs = ((right0, right1), (left0, left1))
    for side in range(2):
        for block in range(BLOCKS):
            load(side, block).wait()
            rows = xbuf[side, block].reshape(ROWS, LENGTH)
            spectrum = jnp.dot(rows, bbuf[...], preferred_element_type=jnp.float32)
            power_mean = jnp.mean(spectrum * spectrum, axis=-1, keepdims=True)
            spec[side, block] = (spectrum * lax.rsqrt(power_mean + 1e-06)).astype(jnp.bfloat16)
            pltpu.make_async_copy(spec.at[side, block], owns[side].at[block], osem.at[side, block]).start()
            for way in range(2):
                for spot in range(width):

                    @pl.when(info[way * width + spot] == block)
                    def _(side=side, block=block, way=way, spot=spot):
                        pltpu.make_async_copy(
                            spec.at[side, block], lane_refs[way][side].at[spot], lsem.at[side, way, spot]
                        ).start()

    for side in range(2):
        for block in range(BLOCKS):
            pltpu.make_async_copy(spec.at[side, block], owns[side].at[block], osem.at[side, block]).wait()
        for way in range(2):
            for spot in range(width):
                pltpu.make_async_copy(
                    spec.at[side, 0], lane_refs[way][side].at[spot], lsem.at[side, way, spot]
                ).wait()


def spectra(chunk, width, info, x, basis):
    own = jax.ShapeDtypeStruct((BLOCKS, ROWS, LENGTH), jnp.bfloat16)
    lane = jax.ShapeDtypeStruct((width, ROWS, LENGTH), jnp.bfloat16)
    return pl.pallas_call(
        lambda *refs: spectra_kernel(chunk, width, *refs),
        out_shape=(own, own, lane, lane, lane, lane),
        in_specs=[SMEM, ANY, ANY],
        out_specs=[ANY] * 6,
        scratch_shapes=[
            pltpu.VMEM((2, BLOCKS, 8, 16 // CHUNKS, 2, LENGTH), jnp.bfloat16),
            pltpu.VMEM((LENGTH, LENGTH), jnp.bfloat16),
            pltpu.VMEM((2, BLOCKS, ROWS, LENGTH), jnp.bfloat16),
            pltpu.SemaphoreType.DMA((2, BLOCKS)),
            pltpu.SemaphoreType.DMA,
            pltpu.SemaphoreType.DMA((2, BLOCKS)),
            pltpu.SemaphoreType.DMA((2, 2, width)),
        ],
        compiler_params=PARAMS,
        cost_estimate=pl.CostEstimate(flops=2 * 6 * ROWS * LENGTH * LENGTH, bytes_accessed=8 << 20, transcendentals=0),
        name="spectra",
    )(info, x, basis)


def products_kernel(width, info, own0, own1, l0, l1, r0, r1, out, buf, acc, sems):
    copies = []
    for side, (own, low, high) in enumerate(((own0, l0, r0), (own1, l1, r1))):
        for part, (ref, start, count) in enumerate(
            ((own, 0, BLOCKS), (low, BLOCKS, width), (high, BLOCKS + width, width))
        ):
            copies.append(pltpu.make_async_copy(ref, buf.at[side, pl.ds(start, count)], sems.at[side, part]))
    for copy in copies:
        copy.start()
    for copy in copies:
        copy.wait()
    half = 16 // CHUNKS

    @pl.loop(0, PCAP)
    def _(slot):
        a, b, used = info[slot], info[PCAP + slot], info[2 * PCAP + slot]

        @pl.when(used > 0)
        def _():
            @pl.loop(0, 4)
            def _(y):
                for lane in range(BINS // 128):
                    re_lanes = pl.ds(lane * 128, 128)
                    im_lanes = pl.ds(BINS + lane * 128, 128)
                    for z in range(2):
                        at = pl.ds(pl.multiple_of((z * 4 + y) * 2 * half, 2 * half), 2 * half)
                        real = imag = None
                        for side in range(2):
                            a_re = buf[side, a, at, re_lanes].astype(jnp.float32)
                            a_im = buf[side, a, at, im_lanes].astype(jnp.float32)
                            b_re = buf[side, b, at, re_lanes].astype(jnp.float32)
                            b_im = buf[side, b, at, im_lanes].astype(jnp.float32)
                            re = a_re * b_re + a_im * b_im
                            im = a_im * b_re - a_re * b_im
                            real = re if real is None else real + re
                            imag = im if imag is None else imag + im
                        acc[lane, z, 0] = real
                        acc[lane, z, 1] = imag
                    for part, lanes_at in ((0, re_lanes), (1, im_lanes)):
                        sums = [
                            acc[lane, z, part, pl.ds(0, half, 2), :] + acc[lane, z, part, pl.ds(1, half, 2), :]
                            for z in range(2)
                        ]
                        out[y, slot, :, lanes_at] = jnp.concatenate(sums, axis=0).astype(jnp.bfloat16)

        @pl.when(used == 0)
        def _():
            @pl.loop(0, 4)
            def _(y):
                out[y, slot] = jnp.zeros((2 * half, LENGTH), jnp.bfloat16)


def products(width, info, *arrays):
    half = 16 // CHUNKS
    return pl.pallas_call(
        lambda *refs: products_kernel(width, *refs),
        out_shape=jax.ShapeDtypeStruct((4, PCAP, 2 * half, LENGTH), jnp.bfloat16),
        in_specs=[SMEM] + [ANY] * 6,
        out_specs=VMEM,
        scratch_shapes=[
            pltpu.VMEM((2, BLOCKS + 2 * width, ROWS, LENGTH), jnp.bfloat16),
            pltpu.VMEM((BINS // 128, 2, 2, 2 * half, 128), jnp.float32),
            pltpu.SemaphoreType.DMA((2, 3)),
        ],
        compiler_params=PARAMS,
        cost_estimate=pl.CostEstimate(flops=1 << 25, bytes_accessed=8 << 20, transcendentals=0),
        name="products",
    )(info, *arrays)


def routes():
    def both(step, flip):
        out = []
        for chan in range(CHAN):
            if 0 <= chan + step < CHAN:
                out += [(chan * 16 + win, (chan + step) * 16 + (win ^ flip)) for win in range(16)]
        return out

    return both


def path(records, pairs, owner, right, left, width):
    route = routes()
    axes = ("chan", "win")
    win = lax.axis_index("win")
    core = win % 2
    far = win // 8
    send, slots = tables(pairs, owner, right, left, width)
    send = jnp.concatenate([send, core[None].astype(jnp.int32)])
    basis = jnp.asarray(basis_table())
    x = records.reshape(BLOCKS, 8, 2, CHUNKS, 16 // CHUNKS, 2, LENGTH)
    half = 16 // CHUNKS
    ready = []
    for chunk in range(CHUNKS):
        own0, own1, r0, r1, l0, l1 = spectra(chunk, width, send, x, basis)
        low0 = lax.ppermute(r0, axes, route(1, 0))
        low1 = lax.ppermute(r1, axes, route(1, 1))
        high0 = lax.ppermute(l0, axes, route(-1, 0))
        high1 = lax.ppermute(l1, axes, route(-1, 1))
        other = lax.ppermute(own1, axes, route(0, 1))
        ready.append((own0, other, low0, low1, high0, high1))
    y_groups = [[z * 8 + y * 2 + c for y in range(4)] for z in range(2) for c in range(2)]
    z_groups = [[z * 8 + y * 2 + c for z in range(2)] for y in range(4) for c in range(2)]
    keep, give = [], []
    for chunk in range(CHUNKS):
        part = products(width, slots, *ready[chunk])
        part = lax.all_to_all(part, "win", 0, 0, tiled=True, axis_index_groups=y_groups)
        total = jnp.sum(part.astype(jnp.float32), axis=0).reshape(PCAP, 2, half, LENGTH)
        keep.append(lax.dynamic_index_in_dim(total, far, axis=1, keepdims=False))
        give.append(lax.dynamic_index_in_dim(total, 1 - far, axis=1, keepdims=False).astype(jnp.bfloat16))
    keep = jnp.concatenate(keep, axis=1)
    give = jnp.concatenate(give, axis=1)
    got = lax.all_gather(give, "win", axis=0, tiled=False, axis_index_groups=z_groups)
    got = lax.dynamic_index_in_dim(got, 1 - far, axis=0, keepdims=False)
    return keep + got.astype(jnp.float32)


def local(records, pairs, owner):
    right, left, most = lanes(pairs, owner)
    return lax.cond(
        most <= 2,
        lambda: path(records, pairs, owner, right, left, 2),
        lambda: path(records, pairs, owner, right, left, 3),
    )


def solution(mesh):
    return jax.shard_map(
        local,
        mesh=mesh,
        in_specs=(P("chan", None, "win", None), P(), P()),
        out_specs=P("chan", "win", None),
        check_vma=False,
    )
```

time: 303 us -> 122 us (0.40)
  the two profiles are of different devices: /device:TPU:152 before, /device:TPU:102 now
where the time goes in v1:
time: 122 us; the launch traced here: 121 us
  starting transfers between devices  38.7 us (32%)
  waiting for transfers between devices  31.5 us (26%)
  Pallas kernels  21.1 us (17%)
  blocking collectives  20 us (16%)
  local copies, waits for them, and re-layouts  3.84 us (3%)
  other arithmetic  3.81 us (3%)
  between operations  1.4 us (1%)
    all_gather x1, blocking collectives, path(): lax.all_gather(give, 'win', axis=0, tiled=False, axis_index_groups=z_groups)  20 us
    pallas_call x2, Pallas kernels, spectra(): pl.pallas_call(lambda *refs: spectra_kernel(chunk, width, *refs), out_sha...  13.9 us
    ppermute x2, waiting for transfers between devices, path(): high1 = lax.ppermute(l1, axes, route(-1, 1))  12.2 us
    ppermute x2, starting transfers between devices, path(): low0 = lax.ppermute(r0, axes, route(1, 0))  11.4 us
    all_to_all x2, waiting for transfers between devices, path(): lax.all_to_all(part, 'win', 0, 0, tiled=True, axis_index_groups=y_groups)  10.2 us
    all_to_all x2, starting transfers between devices, path(): lax.all_to_all(part, 'win', 0, 0, tiled=True, axis_index_groups=y_groups)  8.98 us
    ppermute x2, waiting for transfers between devices, path(): low1 = lax.ppermute(r1, axes, route(1, 1))  7.55 us
    pallas_call x2, Pallas kernels, products(): pl.pallas_call(lambda *refs: products_kernel(width, *refs), out_shape=jax...  7.17 us
  transfers between devices with their start and end apart: 12, of which 6 were waited for; matrix products, arithmetic and copies ran while one was open for 1% of the time, Pallas kernels for 12%

profile of v1, /device:TPU:102, one launch (start us, length us, event | category | flops | bytes accessed | tf_op | source)
XLA Modules:
  0.0 121.0 jit_solution(10364758145807466958)
XLA Ops:
  0.0 0.8 slice_bitcast_fusion.5
  0.8 0.8 fusion.18
  1.6 0.1 reshape.188
  1.7 0.1 reduce_sum.273
  1.8 0.6 reduce_max.18
  2.4 0.1 reshape.189
  2.5 0.1 reduce_sum.274
  2.6 0.7 reduce_max.19
  4.7 115.5 %conditional.1 = (f32[4,16,1024]{2,1,0:T(8,128)S(1)}) conditional(s32[]{:T(128)} %convert_element_type.77, (s32[80]{0:T(128)}, s32[80,2]{0,1:T(2,128)}, bf16[3,256,2,1024]{3,2,1,0:T(2,128)(2,1)}, bf16[1024,1024]{1,0:T(8,128)(2,1)}) %tuple.11, (s32[80]{0:T(128)}, s32[80,2]{0,1:T(2,128)}, s32[32,3]{1,0:T(8,128)S(1)}, s32[32,3]{1,0:T(8,128)S(1)}, ...), branch_computations={%region_6.20_spmd, %region_20.39_spmd} | conditional | flops 3289721856 | bytes 78131224 | solution.py:271
  4.7 0.0 copy-start.8
  4.7 0.0 copy-start.6
  4.8 0.1 copy.29
  4.9 0.1 copy.28
  5.0 0.2 select_reduce_fusion.11
  5.3 0.1 fusion.11
  5.4 0.1 pad_add_fusion.3.refs_0_
  5.5 7.0 %spectra.7 = (bf16[3,128,1024]{2,1,0:T(8,128)(2,1)S(1)}, bf16[3,128,1024]{2,1,0:T(8,128)(2,1)}, bf16[2,128,1024]{2,1,0:T(8,128)(2,1)S(1)}, bf16[2,128,1024]{2,1,...) custom-call(s32[5]{0:T(128)S(1)} %pad_add_fusion.3.refs_0_, ...), custom_call_target="tpu_custom_call" | custom-call | flops 1610612736 | bytes 8388608 | tf_op jit(solution)/shard_map/cond/branch_1_fun/spectra/pallas_call | solution.py:132
  12.5 4.9 %collective-permute-start.16 = (bf16[2,128,1024]{2,1,0:T(8,128)(2,1)S(1)}, bf16[2,128,1024]{2,1,0:T(8,128)(2,1)S(1)}, u32[]{:S(2)}, u32[]{:S(2)}) collective-permute-start(bf16[2,128,1024]{2,1,0:T(8,128)(2,1)S(1)} %get-tuple-element.58), channel_id=1, source_target_pairs={{0,16},{1,17},{2,18},{3,19},{4,20},{5,21},{6,22},{7,23},{8,24},{9,... | collective-permute-start | bytes 1572872 | tf_op jit(solution)/shard_map/cond/branch_1_fun/ppermute | solution.py:247
  17.4 2.6 %collective-permute-start.17 = (bf16[2,128,1024]{2,1,0:T(8,128)(2,1)}, bf16[2,128,1024]{2,1,0:T(8,128)(2,1)}, u32[]{:S(2)}, u32[]{:S(2)}) collective-permute-start(bf16[2,128,1024]{2,1,0:T(8,128)(2,1)} %get-tuple-element.59), channel_id=1, source_target_pairs={{0,17},{1,16},{2,19},{3,18},{4,21},{5,20},{6,23},{7,22},{8,25},{9,... | collective-permute-start | bytes 1572872 | tf_op jit(solution)/shard_map/cond/branch_1_fun/ppermute | solution.py:248
  20.0 2.4 %collective-permute-start.18 = (bf16[2,128,1024]{2,1,0:T(8,128)(2,1)}, bf16[2,128,1024]{2,1,0:T(8,128)(2,1)}, u32[]{:S(2)}, u32[]{:S(2)}) collective-permute-start(bf16[2,128,1024]{2,1,0:T(8,128)(2,1)} %get-tuple-element.60), channel_id=1, source_target_pairs={{16,0},{17,1},{18,2},{19,3},{20,4},{21,5},{22,6},{23,7},{24,8},{25... | collective-permute-start | bytes 1572872 | tf_op jit(solution)/shard_map/cond/branch_1_fun/ppermute | solution.py:249
  22.4 2.5 %collective-permute-start.19 = (bf16[2,128,1024]{2,1,0:T(8,128)(2,1)}, bf16[2,128,1024]{2,1,0:T(8,128)(2,1)}, u32[]{:S(2)}, u32[]{:S(2)}) collective-permute-start(bf16[2,128,1024]{2,1,0:T(8,128)(2,1)} %get-tuple-element.61), channel_id=1, source_target_pairs={{16,1},{17,0},{18,3},{19,2},{20,5},{21,4},{22,7},{23,6},{24,9},{25... | collective-permute-start | bytes 1572872 | tf_op jit(solution)/shard_map/cond/branch_1_fun/ppermute | solution.py:250
  24.9 2.2 %collective-permute-start.15 = (bf16[3,128,1024]{2,1,0:T(8,128)(2,1)}, bf16[3,128,1024]{2,1,0:T(8,128)(2,1)S(1)}, u32[]{:S(2)}, u32[]{:S(2)}) collective-permute-start(bf16[3,128,1024]{2,1,0:T(8,128)(2,1)} %get-tuple-element.57), channel_id=1, source_target_pairs={{0,1},{1,0},{2,3},{3,2},{4,5},{5,4},{6,7},{7,6},{8,9},{9,8},{10,11... | collective-permute-start | bytes 2359304 | tf_op jit(solution)/shard_map/cond/branch_1_fun/ppermute | solution.py:251
  27.1 0.0 copy-done.8
  27.2 0.0 copy-done.6
  27.2 0.1 copy.26
  27.3 0.1 reduce-window.17
  27.4 0.1 reduce.2
  27.5 0.2 fusion.9
  27.7 6.9 %spectra.6 = (bf16[3,128,1024]{2,1,0:T(8,128)(2,1)S(1)}, bf16[3,128,1024]{2,1,0:T(8,128)(2,1)}, bf16[2,128,1024]{2,1,0:T(8,128)(2,1)}, bf16[2,128,1024]{2,1,0:T(...) custom-call(s32[5]{0:T(128)S(1)} %pad_add_fusion.3.refs_0_, ...), custom_call_target="tpu_custom_call" | custom-call | flops 1610612736 | bytes 8388608 | tf_op jit(solution)/shard_map/cond/branch_1_fun/spectra/pallas_call | solution.py:132
  34.6 0.0 collective-permute-done.16.refs_3_
  34.6 0.0 copy-start.2
  34.6 0.8 copy-done.2
  35.5 2.3 %collective-permute-start.10 = (bf16[3,128,1024]{2,1,0:T(8,128)(2,1)}, bf16[3,128,1024]{2,1,0:T(8,128)(2,1)S(1)}, u32[]{:S(2)}, u32[]{:S(2)}) collective-permute-start(bf16[3,128,1024]{2,1,0:T(8,128)(2,1)} %get-tuple-element.51), channel_id=1, source_target_pairs={{0,1},{1,0},{2,3},{3,2},{4,5},{5,4},{6,7},{7,6},{8,9},{9,8},{10,11... | collective-permute-start | bytes 2359304 | tf_op jit(solution)/shard_map/cond/branch_1_fun/ppermute | solution.py:251
  37.8 0.2 select_reduce_fusion.13
  38.0 1.9 %collective-permute-done.17.refs_4_ = bf16[2,128,1024]{2,1,0:T(8,128)(2,1)} collective-permute-done((bf16[2,128,1024]{2,1,0:T(8,128)(2,1)}, bf16[2,128,1024]{2,1,0:T(8,128)(2,1)}, u32[]{:S(2)}, u32[]{:S(2)}) %collective-permute-start.17) | collective-permute-done | bytes 524320 | tf_op jit(solution)/shard_map/cond/branch_1_fun/ppermute | solution.py:248
  39.9 6.5 %collective-permute-start.11 = (bf16[2,128,1024]{2,1,0:T(8,128)(2,1)}, bf16[2,128,1024]{2,1,0:T(8,128)(2,1)}, u32[]{:S(2)}, u32[]{:S(2)}) collective-permute-start(bf16[2,128,1024]{2,1,0:T(8,128)(2,1)} %get-tuple-element.52), channel_id=1, source_target_pairs={{0,16},{1,17},{2,18},{3,19},{4,20},{5,21},{6,22},{7,23},{8,24},{9,... | collective-permute-start | bytes 1572872 | tf_op jit(solution)/shard_map/cond/branch_1_fun/ppermute | solution.py:247
  46.4 0.0 collective-permute-done.18.refs_5_
  46.4 2.5 %collective-permute-start.12 = (bf16[2,128,1024]{2,1,0:T(8,128)(2,1)}, bf16[2,128,1024]{2,1,0:T(8,128)(2,1)}, u32[]{:S(2)}, u32[]{:S(2)}) collective-permute-start(bf16[2,128,1024]{2,1,0:T(8,128)(2,1)} %get-tuple-element.53), channel_id=1, source_target_pairs={{0,17},{1,16},{2,19},{3,18},{4,21},{5,20},{6,23},{7,22},{8,25},{9,... | collective-permute-start | bytes 1572872 | tf_op jit(solution)/shard_map/cond/branch_1_fun/ppermute | solution.py:248
  49.0 2.6 %collective-permute-done.19.refs_6_ = bf16[2,128,1024]{2,1,0:T(8,128)(2,1)} collective-permute-done((bf16[2,128,1024]{2,1,0:T(8,128)(2,1)}, bf16[2,128,1024]{2,1,0:T(8,128)(2,1)}, u32[]{:S(2)}, u32[]{:S(2)}) %collective-permute-start.19) | collective-permute-done | bytes 524320 | tf_op jit(solution)/shard_map/cond/branch_1_fun/ppermute | solution.py:250
  51.6 1.9 %collective-permute-start.13 = (bf16[2,128,1024]{2,1,0:T(8,128)(2,1)}, bf16[2,128,1024]{2,1,0:T(8,128)(2,1)}, u32[]{:S(2)}, u32[]{:S(2)}) collective-permute-start(bf16[2,128,1024]{2,1,0:T(8,128)(2,1)} %get-tuple-element.54), channel_id=1, source_target_pairs={{16,0},{17,1},{18,2},{19,3},{20,4},{21,5},{22,6},{23,7},{24,8},{25... | collective-permute-start | bytes 1572872 | tf_op jit(solution)/shard_map/cond/branch_1_fun/ppermute | solution.py:249
  53.5 0.0 collective-permute-done.15.refs_2_
  53.5 1.9 %collective-permute-start.14 = (bf16[2,128,1024]{2,1,0:T(8,128)(2,1)}, bf16[2,128,1024]{2,1,0:T(8,128)(2,1)}, u32[]{:S(2)}, u32[]{:S(2)}) collective-permute-start(bf16[2,128,1024]{2,1,0:T(8,128)(2,1)} %get-tuple-element.55), channel_id=1, source_target_pairs={{16,1},{17,0},{18,3},{19,2},{20,5},{21,4},{22,7},{23,6},{24,9},{25... | collective-permute-start | bytes 1572872 | tf_op jit(solution)/shard_map/cond/branch_1_fun/ppermute | solution.py:250
  55.4 0.1 pad_add_fusion.2.refs_0_
  55.5 0.0 copy-start.3
  55.5 1.0 copy-done.3
  56.6 3.5 %products.7 = bf16[4,4,16,1024]{3,2,1,0:T(8,128)(2,1)} custom-call(s32[12]{0:T(128)S(1)} %pad_add_fusion.2.refs_0_, bf16[3,128,1024]{2,1,0:T(8,128)(2,1)S(1)} %get-tuple-element.56.refs_1_, bf16[3,128,1024]{2,1,0:T(8,128)(2,1)S(1)} %collective-permute-done.15.refs_2_, bf16[2,128,1024]{2,1,0:T(8,128)(2,1)S(1)} %copy-done.3, ...), custom_call_target="tpu_custom_call" | custom-call | flops 33554432 | bytes 8388608 | tf_op jit(solution)/shard_map/cond/branch_1_fun/products/pallas_call | solution.py:206
  60.1 4.5 %all-to-all-start.3 = ((bf16[4,4,16,1024]{3,2,1,0:T(8,128)(2,1)}), bf16[4,4,16,1024]{3,2,1,0:T(8,128)(2,1)S(1)}, u32[]{:S(2)}, u32[]{:S(2)}) async-start(bf16[4,4,16,1024]{3,2,1,0:T(8,128)(2,1)} %products.7), calls=%async_computation.3 | async-start | bytes 1048576 | tf_op jit(solution)/shard_map/cond/branch_1_fun/all_to_all | solution.py:258
  64.6 0.0 collective-permute-done.11.refs_3_
  64.6 5.6 %collective-permute-done.12.refs_4_ = bf16[2,128,1024]{2,1,0:T(8,128)(2,1)} collective-permute-done((bf16[2,128,1024]{2,1,0:T(8,128)(2,1)}, bf16[2,128,1024]{2,1,0:T(8,128)(2,1)}, u32[]{:S(2)}, u32[]{:S(2)}) %collective-permute-start.12) | collective-permute-done | bytes 524320 | tf_op jit(solution)/shard_map/cond/branch_1_fun/ppermute | solution.py:248
  70.3 1.6 %collective-permute-done.13.refs_5_ = bf16[2,128,1024]{2,1,0:T(8,128)(2,1)} collective-permute-done((bf16[2,128,1024]{2,1,0:T(8,128)(2,1)}, bf16[2,128,1024]{2,1,0:T(8,128)(2,1)}, u32[]{:S(2)}, u32[]{:S(2)}) %collective-permute-start.13) | collective-permute-done | bytes 524320 | tf_op jit(solution)/shard_map/cond/branch_1_fun/ppermute | solution.py:249
  71.9 9.6 %collective-permute-done.14.refs_6_ = bf16[2,128,1024]{2,1,0:T(8,128)(2,1)} collective-permute-done((bf16[2,128,1024]{2,1,0:T(8,128)(2,1)}, bf16[2,128,1024]{2,1,0:T(8,128)(2,1)}, u32[]{:S(2)}, u32[]{:S(2)}) %collective-permute-start.14) | collective-permute-done | bytes 524320 | tf_op jit(solution)/shard_map/cond/branch_1_fun/ppermute | solution.py:250
  81.4 0.0 collective-permute-done.10.refs_2_
  81.4 3.6 %products.6 = bf16[4,4,16,1024]{3,2,1,0:T(8,128)(2,1)} custom-call(s32[12]{0:T(128)S(1)} %pad_add_fusion.2.refs_0_, bf16[3,128,1024]{2,1,0:T(8,128)(2,1)S(1)} %get-tuple-element.50.refs_1_, bf16[3,128,1024]{2,1,0:T(8,128)(2,1)S(1)} %collective-permute-done.10.refs_2_, bf16[2,128,1024]{2,1,0:T(8,128)(2,1)} %collective-permute-done.11.refs_3_, ...), custom_call_target="tpu_custom_call" | custom-call | flops 33554432 | bytes 8388608 | tf_op jit(solution)/shard_map/cond/branch_1_fun/products/pallas_call | solution.py:206
  85.1 0.0 all-to-all-done.3
  85.1 4.5 %all-to-all-start.2 = ((bf16[4,4,16,1024]{3,2,1,0:T(8,128)(2,1)}), bf16[4,4,16,1024]{3,2,1,0:T(8,128)(2,1)S(1)}, u32[]{:S(2)}, u32[]{:S(2)}) async-start(bf16[4,4,16,1024]{3,2,1,0:T(8,128)(2,1)} %products.6), calls=%async_computation.2 | async-start | bytes 1048576 | tf_op jit(solution)/shard_map/cond/branch_1_fun/all_to_all | solution.py:258
  89.6 0.1 convert_reduce_fusion.2
  89.7 10.2 %all-to-all-done.2 = bf16[4,4,16,1024]{3,2,1,0:T(8,128)(2,1)S(1)} async-done(((bf16[4,4,16,1024]{3,2,1,0:T(8,128)(2,1)}), bf16[4,4,16,1024]{3,2,1,0:T(8,128)(2,1)S(1)}, u32[]{:S(2)}, u32[]{:S(2)}) %all-to-all-start.2) | async-done | bytes 524320 | tf_op jit(solution)/shard_map/cond/branch_1_fun/all_to_all | solution.py:258
  99.9 0.1 convert_reduce_fusion.3
  100.0 20.0 %all-gather.1 = bf16[8,16,1024]{2,1,0:T(8,128)(2,1)S(1)} all-gather(bf16[4,16,1024]{2,1,0:T(8,128)(2,1)S(1)} %pad_maximum_fusion.1), channel_id=3, replica_groups={{0,8},{1,9},{2,10},{3,11},{4,12},{5,13},{6,14},{7,15},{16,24},{17,25},{..., dimensions={0}, use_global_device_ids=true | all-gather | bytes 393216 | tf_op jit(solution)/shard_map/cond/branch_1_fun/all_gather | solution.py:264
  120.2 0.0 copy-start.4
  120.3 0.7 copy-done.4
  (23 shorter events, 0.3 us)
Async XLA Ops:
  4.7 22.4 %copy-start.8 = (s32[80]{0:T(128)S(1)}, s32[80]{0:T(128)}, u32[]{:S(2)}) copy-start(s32[80]{0:T(128)} %get-tuple-element.44) | copy-start | bytes 964 | tf_op jit(solution)/shard_map/cond
  4.7 22.4 %copy-start.6 = (s32[80,2]{0,1:T(2,128)S(1)}, s32[80,2]{0,1:T(2,128)}, u32[]{:S(2)}) copy-start(s32[80,2]{0,1:T(2,128)} %get-tuple-element.45) | copy-start | bytes 1924 | tf_op jit(solution)/shard_map/cond
  12.5 22.1 %collective-permute-start.16 = (bf16[2,128,1024]{2,1,0:T(8,128)(2,1)S(1)}, bf16[2,128,1024]{2,1,0:T(8,128)(2,1)S(1)}, u32[]{:S(2)}, u32[]{:S(2)}) collective-permute-start(bf16[2,128,1024]{2,1,0:T(8,128)(2,1)S(1)} %get-tuple-element.58), channel_id=1, source_target_pairs={{0,16},{1,17},{2,18},{3,19},{4,20},{5,21},{6,22},{7,23},{8,24},{9,... | collective-permute-start | bytes 1572872 | tf_op jit(solution)/shard_map/cond/branch_1_fun/ppermute | solution.py:247
  17.4 22.5 %collective-permute-start.17 = (bf16[2,128,1024]{2,1,0:T(8,128)(2,1)}, bf16[2,128,1024]{2,1,0:T(8,128)(2,1)}, u32[]{:S(2)}, u32[]{:S(2)}) collective-permute-start(bf16[2,128,1024]{2,1,0:T(8,128)(2,1)} %get-tuple-element.59), channel_id=1, source_target_pairs={{0,17},{1,16},{2,19},{3,18},{4,21},{5,20},{6,23},{7,22},{8,25},{9,... | collective-permute-start | bytes 1572872 | tf_op jit(solution)/shard_map/cond/branch_1_fun/ppermute | solution.py:248
  20.0 26.4 %collective-permute-start.18 = (bf16[2,128,1024]{2,1,0:T(8,128)(2,1)}, bf16[2,128,1024]{2,1,0:T(8,128)(2,1)}, u32[]{:S(2)}, u32[]{:S(2)}) collective-permute-start(bf16[2,128,1024]{2,1,0:T(8,128)(2,1)} %get-tuple-element.60), channel_id=1, source_target_pairs={{16,0},{17,1},{18,2},{19,3},{20,4},{21,5},{22,6},{23,7},{24,8},{25... | collective-permute-start | bytes 1572872 | tf_op jit(solution)/shard_map/cond/branch_1_fun/ppermute | solution.py:249
  22.4 29.2 %collective-permute-start.19 = (bf16[2,128,1024]{2,1,0:T(8,128)(2,1)}, bf16[2,128,1024]{2,1,0:T(8,128)(2,1)}, u32[]{:S(2)}, u32[]{:S(2)}) collective-permute-start(bf16[2,128,1024]{2,1,0:T(8,128)(2,1)} %get-tuple-element.61), channel_id=1, source_target_pairs={{16,1},{17,0},{18,3},{19,2},{20,5},{21,4},{22,7},{23,6},{24,9},{25... | collective-permute-start | bytes 1572872 | tf_op jit(solution)/shard_map/cond/branch_1_fun/ppermute | solution.py:250
  24.9 28.6 %collective-permute-start.15 = (bf16[3,128,1024]{2,1,0:T(8,128)(2,1)}, bf16[3,128,1024]{2,1,0:T(8,128)(2,1)S(1)}, u32[]{:S(2)}, u32[]{:S(2)}) collective-permute-start(bf16[3,128,1024]{2,1,0:T(8,128)(2,1)} %get-tuple-element.57), channel_id=1, source_target_pairs={{0,1},{1,0},{2,3},{3,2},{4,5},{5,4},{6,7},{7,6},{8,9},{9,8},{10,11... | collective-permute-start | bytes 2359304 | tf_op jit(solution)/shard_map/cond/branch_1_fun/ppermute | solution.py:251
  34.6 0.8 copy-start.2
  35.5 46.0 %collective-permute-start.10 = (bf16[3,128,1024]{2,1,0:T(8,128)(2,1)}, bf16[3,128,1024]{2,1,0:T(8,128)(2,1)S(1)}, u32[]{:S(2)}, u32[]{:S(2)}) collective-permute-start(bf16[3,128,1024]{2,1,0:T(8,128)(2,1)} %get-tuple-element.51), channel_id=1, source_target_pairs={{0,1},{1,0},{2,3},{3,2},{4,5},{5,4},{6,7},{7,6},{8,9},{9,8},{10,11... | collective-permute-start | bytes 2359304 | tf_op jit(solution)/shard_map/cond/branch_1_fun/ppermute | solution.py:251
  39.9 24.7 %collective-permute-start.11 = (bf16[2,128,1024]{2,1,0:T(8,128)(2,1)}, bf16[2,128,1024]{2,1,0:T(8,128)(2,1)}, u32[]{:S(2)}, u32[]{:S(2)}) collective-permute-start(bf16[2,128,1024]{2,1,0:T(8,128)(2,1)} %get-tuple-element.52), channel_id=1, source_target_pairs={{0,16},{1,17},{2,18},{3,19},{4,20},{5,21},{6,22},{7,23},{8,24},{9,... | collective-permute-start | bytes 1572872 | tf_op jit(solution)/shard_map/cond/branch_1_fun/ppermute | solution.py:247
  46.4 23.8 %collective-permute-start.12 = (bf16[2,128,1024]{2,1,0:T(8,128)(2,1)}, bf16[2,128,1024]{2,1,0:T(8,128)(2,1)}, u32[]{:S(2)}, u32[]{:S(2)}) collective-permute-start(bf16[2,128,1024]{2,1,0:T(8,128)(2,1)} %get-tuple-element.53), channel_id=1, source_target_pairs={{0,17},{1,16},{2,19},{3,18},{4,21},{5,20},{6,23},{7,22},{8,25},{9,... | collective-permute-start | bytes 1572872 | tf_op jit(solution)/shard_map/cond/branch_1_fun/ppermute | solution.py:248
  51.6 20.3 %collective-permute-start.13 = (bf16[2,128,1024]{2,1,0:T(8,128)(2,1)}, bf16[2,128,1024]{2,1,0:T(8,128)(2,1)}, u32[]{:S(2)}, u32[]{:S(2)}) collective-permute-start(bf16[2,128,1024]{2,1,0:T(8,128)(2,1)} %get-tuple-element.54), channel_id=1, source_target_pairs={{16,0},{17,1},{18,2},{19,3},{20,4},{21,5},{22,6},{23,7},{24,8},{25... | collective-permute-start | bytes 1572872 | tf_op jit(solution)/shard_map/cond/branch_1_fun/ppermute | solution.py:249
  53.5 27.9 %collective-permute-start.14 = (bf16[2,128,1024]{2,1,0:T(8,128)(2,1)}, bf16[2,128,1024]{2,1,0:T(8,128)(2,1)}, u32[]{:S(2)}, u32[]{:S(2)}) collective-permute-start(bf16[2,128,1024]{2,1,0:T(8,128)(2,1)} %get-tuple-element.55), channel_id=1, source_target_pairs={{16,1},{17,0},{18,3},{19,2},{20,5},{21,4},{22,7},{23,6},{24,9},{25... | collective-permute-start | bytes 1572872 | tf_op jit(solution)/shard_map/cond/branch_1_fun/ppermute | solution.py:250
  55.5 1.0 copy-start.3
  60.1 25.0 %all-to-all-start.3 = ((bf16[4,4,16,1024]{3,2,1,0:T(8,128)(2,1)}), bf16[4,4,16,1024]{3,2,1,0:T(8,128)(2,1)S(1)}, u32[]{:S(2)}, u32[]{:S(2)}) async-start(bf16[4,4,16,1024]{3,2,1,0:T(8,128)(2,1)} %products.7), calls=%async_computation.3 | async-start | bytes 1048576 | tf_op jit(solution)/shard_map/cond/branch_1_fun/all_to_all | solution.py:258
  85.1 14.8 %all-to-all-start.2 = ((bf16[4,4,16,1024]{3,2,1,0:T(8,128)(2,1)}), bf16[4,4,16,1024]{3,2,1,0:T(8,128)(2,1)S(1)}, u32[]{:S(2)}, u32[]{:S(2)}) async-start(bf16[4,4,16,1024]{3,2,1,0:T(8,128)(2,1)} %products.6), calls=%async_computation.2 | async-start | bytes 1048576 | tf_op jit(solution)/shard_map/cond/branch_1_fun/all_to_all | solution.py:258
  120.2 0.7 copy-start.4

commit v2 on v0

v2 whole, which is shorter than its diff:
```python
import math

import jax
import jax.numpy as jnp
import ml_dtypes
import numpy as np
from jax import lax
from jax.experimental import pallas as pl
from jax.experimental.pallas import tpu as pltpu
from jax.sharding import PartitionSpec as P

PCAP = 4
BLOCKS = 3
CHAN = 32
CHUNKS = 2
LENGTH = 1024
BINS = 512
HALF = 16 // CHUNKS
ROWS = 512 // CHUNKS
SIDE = ROWS // 2
VMEM = pl.BlockSpec(memory_space=pltpu.VMEM)
SMEM = pl.BlockSpec(memory_space=pltpu.SMEM)
ANY = pl.BlockSpec(memory_space=pl.ANY)
PARAMS = pltpu.CompilerParams(vmem_limit_bytes=40 << 20)


def basis_table():
    sample_ids = np.arange(LENGTH, dtype=np.int32)
    bin_ids = np.arange(BINS, dtype=np.int32)
    step = np.float32(2.0 * math.pi / LENGTH)
    phases = (sample_ids[:, None] * bin_ids[None, :] % LENGTH).astype(np.float32) * step
    taper = np.float32(0.5) - np.float32(0.5) * np.cos(sample_ids.astype(np.float32) * step)
    table = np.concatenate([taper[:, None] * np.cos(phases), -taper[:, None] * np.sin(phases)], axis=1)
    return table.astype(ml_dtypes.bfloat16)


def most_needed(pairs, owner):
    first, second = pairs[:, 0], pairs[:, 1]
    ids = jnp.arange(BLOCKS * CHAN, dtype=jnp.int32)
    right = (first[None, :] == ids[:, None]) & (owner[None, :] == ids[:, None] // BLOCKS + 1)
    left = (second[None, :] == ids[:, None]) & (owner[None, :] == ids[:, None] // BLOCKS - 1)
    need = jnp.stack([jnp.any(right, axis=1), jnp.any(left, axis=1)]).astype(jnp.int32)
    return jnp.max(jnp.sum(need.reshape(2, CHAN, BLOCKS), axis=2))


RIGHT, LEFT, FIRST, SECOND, USED, TABLE = 0, 3, 6, 10, 14, 18


def fill_table(width, where, pairs, owner, info, seen):
    me = where[0]

    def bit(block):
        return jnp.where(block == 0, 1, jnp.where(block == 1, 2, jnp.where(block == 2, 4, 0)))

    def step(p, carry):
        to_right, to_left, of_left, of_right, count = carry
        first = pairs[0, p] - me * BLOCKS
        second = pairs[1, p] - me * BLOCKS
        apart = owner[p] - me
        to_right |= jnp.where(apart == 1, bit(first), 0)
        to_left |= jnp.where(apart == -1, bit(second), 0)
        mine = apart == 0
        of_left |= jnp.where(mine, bit(first + BLOCKS), 0)
        of_right |= jnp.where(mine, bit(second - BLOCKS), 0)

        @pl.when(mine & (count < PCAP))
        def _():
            seen[0, count] = first
            seen[1, count] = second

        return to_right, to_left, of_left, of_right, count + mine.astype(jnp.int32)

    zero = jnp.int32(0)
    for slot in range(PCAP):
        seen[0, slot] = zero
        seen[1, slot] = zero
    to_right, to_left, of_left, of_right, count = lax.fori_loop(
        0, owner.shape[0], step, (zero, zero, zero, zero, zero), unroll=4
    )

    def spot(mask, block):
        if width == BLOCKS:
            return block
        low = mask & 1
        return jnp.where(block == 0, 0, jnp.where(block == 1, low, jnp.minimum(low + ((mask >> 1) & 1), width - 1)))

    for base, mask in ((RIGHT, to_right), (LEFT, to_left)):
        if width == BLOCKS:
            picks = (0, 1, 2)
        else:
            lowest = jnp.where((mask & 1) > 0, 0, jnp.where((mask & 2) > 0, 1, jnp.where((mask & 4) > 0, 2, 0)))
            next_one = jnp.where((mask & 3) == 3, 1, jnp.where((mask == 5) | (mask == 6), 2, 0))
            picks = (lowest, next_one, 0)
        for i in range(3):
            info[base + i] = jnp.int32(picks[i])
    for slot in range(PCAP):
        used = count > slot
        first = jnp.where(used, seen[0, slot], 0)
        second = jnp.where(used, seen[1, slot], 0)
        info[FIRST + slot] = jnp.where(first < 0, BLOCKS + spot(of_left, first + BLOCKS), first)
        info[SECOND + slot] = jnp.where(
            second >= BLOCKS, BLOCKS + width + spot(of_right, second - BLOCKS), second
        )
        info[USED + slot] = used.astype(jnp.int32)


def load_and_whiten(load, basis, xbuf, bbuf, bsem, spec, meanwhile, done):
    table = pltpu.make_async_copy(basis, bbuf, bsem)
    for copy in load(0):
        copy.start()
    table.start()
    for block in range(1, BLOCKS):
        for copy in load(block):
            copy.start()
    meanwhile()
    for block in range(BLOCKS):
        for copy in load(block):
            copy.wait()
        if block == 0:
            table.wait()
        rows = xbuf[block].reshape(ROWS, LENGTH)
        spectrum = jnp.dot(rows, bbuf[...], preferred_element_type=jnp.float32)
        power_mean = jnp.mean(spectrum * spectrum, axis=-1, keepdims=True)
        spec[block] = (spectrum * lax.rsqrt(power_mean + 1e-06)).astype(jnp.bfloat16)
        done(block)


def spectra_kernel(chunk, width, where, pairs, owner, x, basis, own, right, left, info, xbuf, bbuf, spec, xsem, bsem, osem, lsem, seen):
    def load(block):
        return [pltpu.make_async_copy(x.at[block, :, chunk], xbuf.at[block], xsem.at[block])]

    def lane_copy(way, spot, block):
        return pltpu.make_async_copy(spec.at[block], (right, left)[way].at[spot], lsem.at[way, spot])

    def own_copy(block):
        return pltpu.make_async_copy(spec.at[block], own.at[block], osem.at[block])

    load_and_whiten(
        load, basis, xbuf, bbuf, bsem, spec,
        lambda: fill_table(width, where, pairs, owner, info, seen),
        lambda block: own_copy(block).start(),
    )
    for way in range(2):
        for spot in range(width):
            lane_copy(way, spot, info[way * 3 + spot]).start()
    for block in range(BLOCKS):
        own_copy(block).wait()
    for way in range(2):
        for spot in range(width):
            lane_copy(way, spot, 0).wait()


COST = pl.CostEstimate(flops=2 * 3 * ROWS * LENGTH * LENGTH, bytes_accessed=8 << 20, transcendentals=0)


def spectra(chunk, width, where, pairs, owner, x, basis):
    own = jax.ShapeDtypeStruct((BLOCKS, ROWS, LENGTH), jnp.bfloat16)
    lane = jax.ShapeDtypeStruct((width, ROWS, LENGTH), jnp.bfloat16)
    return pl.pallas_call(
        lambda *refs: spectra_kernel(chunk, width, *refs),
        out_shape=(own, lane, lane, jax.ShapeDtypeStruct((TABLE,), jnp.int32)),
        in_specs=[SMEM] * 3 + [ANY, ANY],
        out_specs=[ANY] * 3 + [SMEM],
        scratch_shapes=[
            pltpu.VMEM((BLOCKS, 16, HALF, 2, LENGTH), jnp.bfloat16),
            pltpu.VMEM((LENGTH, LENGTH), jnp.bfloat16),
            pltpu.VMEM((BLOCKS, ROWS, LENGTH), jnp.bfloat16),
            pltpu.SemaphoreType.DMA((BLOCKS,)),
            pltpu.SemaphoreType.DMA,
            pltpu.SemaphoreType.DMA((BLOCKS,)),
            pltpu.SemaphoreType.DMA((2, width)),
            pltpu.SMEM((2, PCAP), jnp.int32),
        ],
        compiler_params=PARAMS,
        cost_estimate=COST,
        name="spectra",
    )(where, pairs, owner, x, basis)


def split_kernel(chunk, where, x, basis, same, other, xbuf, bbuf, spec, xsem, bsem, osem):
    core = where[1]

    def load(block):
        return [
            pltpu.make_async_copy(x.at[block, :, (core + side) % 2, chunk], xbuf.at[block, side], xsem.at[block, side])
            for side in range(2)
        ]

    def own_copies(block):
        return [
            pltpu.make_async_copy(spec.at[block, pl.ds(side * SIDE, SIDE)], ref.at[block], osem.at[block, side])
            for side, ref in enumerate((same, other))
        ]

    def done(block):
        for copy in own_copies(block):
            copy.start()

    load_and_whiten(load, basis, xbuf, bbuf, bsem, spec, lambda: None, done)
    for block in range(BLOCKS):
        for copy in own_copies(block):
            copy.wait()


def split_spectra(chunk, where, x, basis):
    own = jax.ShapeDtypeStruct((BLOCKS, SIDE, LENGTH), jnp.bfloat16)
    return pl.pallas_call(
        lambda *refs: split_kernel(chunk, *refs),
        out_shape=(own, own),
        in_specs=[SMEM] + [ANY, ANY],
        out_specs=[ANY] * 2,
        scratch_shapes=[
            pltpu.VMEM((BLOCKS, 2, 8, HALF, 2, LENGTH), jnp.bfloat16),
            pltpu.VMEM((LENGTH, LENGTH), jnp.bfloat16),
            pltpu.VMEM((BLOCKS, ROWS, LENGTH), jnp.bfloat16),
            pltpu.SemaphoreType.DMA((BLOCKS, 2)),
            pltpu.SemaphoreType.DMA,
            pltpu.SemaphoreType.DMA((BLOCKS, 2)),
        ],
        compiler_params=PARAMS,
        cost_estimate=COST,
        name="split_spectra",
    )(where, x, basis)


def lanes_kernel(width, info, same, other, right, left, sems):
    def copies(block_of):
        return [
            pltpu.make_async_copy(ref.at[block_of(way, spot)], lane.at[side, spot], sems.at[way, spot, side])
            for way, lane in enumerate((right, left))
            for spot in range(width)
            for side, ref in enumerate((same, other))
        ]

    for copy in copies(lambda way, spot: info[way * 3 + spot]):
        copy.start()
    for copy in copies(lambda way, spot: 0):
        copy.wait()


def lanes(width, info, same, other):
    lane = jax.ShapeDtypeStruct((2, width, SIDE, LENGTH), jnp.bfloat16)
    return pl.pallas_call(
        lambda *refs: lanes_kernel(width, *refs),
        out_shape=(lane, lane),
        in_specs=[SMEM] + [ANY, ANY],
        out_specs=[ANY] * 2,
        scratch_shapes=[pltpu.SemaphoreType.DMA((2, width, 2))],
        compiler_params=PARAMS,
        cost_estimate=pl.CostEstimate(flops=0, bytes_accessed=4 << 20, transcendentals=0),
        name="lanes",
    )(info, same, other)


def products_kernel(width, sides, *refs):
    info, owns, (low, high, out, buf, acc, sems) = refs[0], refs[1 : 1 + sides], refs[1 + sides :]
    peers = 8 // sides
    copies = []
    for side in range(sides):
        parts = (
            (owns[side], 0, BLOCKS),
            (low.at[side], BLOCKS, width),
            (high.at[side], BLOCKS + width, width),
        )
        for part, (ref, start, count) in enumerate(parts):
            copies.append(pltpu.make_async_copy(ref, buf.at[side, pl.ds(start, count)], sems.at[side, part]))
    for copy in copies:
        copy.start()
    for copy in copies:
        copy.wait()

    @pl.loop(0, PCAP)
    def _(slot):
        a, b, used = info[FIRST + slot], info[SECOND + slot], info[USED + slot]

        @pl.when(used > 0)
        def _():
            @pl.loop(0, peers)
            def _(peer):
                for lane in range(BINS // 128):
                    re_lanes = pl.ds(lane * 128, 128)
                    im_lanes = pl.ds(BINS + lane * 128, 128)
                    for z in range(2):
                        at = pl.ds(pl.multiple_of((z * peers + peer) * 2 * HALF, 2 * HALF), 2 * HALF)
                        real, imag = [], []
                        for side in range(sides):
                            a_re = buf[side, a, at, re_lanes].astype(jnp.float32)
                            a_im = buf[side, a, at, im_lanes].astype(jnp.float32)
                            b_re = buf[side, b, at, re_lanes].astype(jnp.float32)
                            b_im = buf[side, b, at, im_lanes].astype(jnp.float32)
                            real.append(a_re * b_re + a_im * b_im)
                            imag.append(a_im * b_re - a_re * b_im)
                        acc[lane, z, 0] = sum(real[1:], real[0])
                        acc[lane, z, 1] = sum(imag[1:], imag[0])
                    for part, lanes_at in ((0, re_lanes), (1, im_lanes)):
                        sums = [
                            acc[lane, z, part, pl.ds(0, HALF, 2), :] + acc[lane, z, part, pl.ds(1, HALF, 2), :]
                            for z in range(2)
                        ]
                        out[peer, slot, :, lanes_at] = jnp.concatenate(sums, axis=0).astype(jnp.bfloat16)

        @pl.when(used == 0)
        def _():
            @pl.loop(0, peers)
            def _(peer):
                out[peer, slot] = jnp.zeros((2 * HALF, LENGTH), jnp.bfloat16)


def products(width, info, owns, low, high):
    sides = len(owns)
    return pl.pallas_call(
        lambda *refs: products_kernel(width, sides, *refs),
        out_shape=jax.ShapeDtypeStruct((8 // sides, PCAP, 2 * HALF, LENGTH), jnp.bfloat16),
        in_specs=[SMEM] + [ANY] * (sides + 2),
        out_specs=VMEM,
        scratch_shapes=[
            pltpu.VMEM((sides, BLOCKS + 2 * width, ROWS // sides, LENGTH), jnp.bfloat16),
            pltpu.VMEM((BINS // 128, 2, 2, 2 * HALF, 128), jnp.float32),
            pltpu.SemaphoreType.DMA((sides, 3)),
        ],
        compiler_params=PARAMS,
        cost_estimate=pl.CostEstimate(flops=1 << 25, bytes_accessed=8 << 20, transcendentals=0),
        name="products",
    )(info, *owns, low, high)


def path(records, pairs, owner, width):
    win = lax.axis_index("win")
    far = win // 8
    where = jnp.stack([lax.axis_index("chan"), win % 2]).astype(jnp.int32)
    basis = jnp.asarray(basis_table())
    forward = [(i, i + 1) for i in range(CHAN - 1)]
    backward = [(i + 1, i) for i in range(CHAN - 1)]

    x = records.reshape(BLOCKS, 16, CHUNKS, HALF, 2, LENGTH)
    own, right, left, info = spectra(0, width, where, pairs.T, owner, x, basis)
    low = lax.ppermute(right[None], "chan", forward)
    high = lax.ppermute(left[None], "chan", backward)

    x = records.reshape(BLOCKS, 8, 2, CHUNKS, HALF, 2, LENGTH)
    same, other = split_spectra(1, where, x, basis)
    other = lax.ppermute(other, "win", [(i, i ^ 1) for i in range(16)])
    right, left = lanes(width, info, same, other)
    own, right = lax.optimization_barrier((own, right))
    low_split = lax.ppermute(right, "chan", forward)
    high_split = lax.ppermute(left, "chan", backward)

    chip_groups = [[z * 8 + j for j in range(8)] for z in range(2)]
    core_groups = [[z * 8 + y * 2 + core for y in range(4)] for z in range(2) for core in range(2)]
    far_groups = [[z * 8 + j for z in range(2)] for j in range(8)]

    def near(part):
        total = jnp.sum(part.astype(jnp.float32), axis=0).reshape(PCAP, 2, HALF, LENGTH)
        keep = lax.dynamic_index_in_dim(total, far, axis=1, keepdims=False)
        give = lax.dynamic_index_in_dim(total, 1 - far, axis=1, keepdims=False).astype(jnp.bfloat16)
        return keep, give

    part0 = products(width, info, (own,), low, high)
    part0 = lax.all_to_all(part0, "win", 0, 0, tiled=True, axis_index_groups=chip_groups)
    part1 = products(width, info, (same, other), low_split, high_split)
    part0, _ = lax.optimization_barrier((part0, part1))
    part1 = lax.all_to_all(part1, "win", 0, 0, tiled=True, axis_index_groups=core_groups)
    keep0, give0 = near(part0)
    keep1, give1 = near(part1)
    give = jnp.concatenate([give0, give1], axis=1)
    got = lax.all_gather(give, "win", axis=0, tiled=False, axis_index_groups=far_groups)
    got = lax.dynamic_index_in_dim(got, 1 - far, axis=0, keepdims=False)
    return jnp.concatenate([keep0, keep1], axis=1) + got.astype(jnp.float32), keep0


def local(records, pairs, owner):
    fast, late = path(records, pairs, owner, 2)
    pairs_late, owner_late, _ = lax.optimization_barrier((pairs, owner, late))
    return lax.cond(
        most_needed(pairs_late, owner_late) <= 2,
        lambda fast: fast,
        lambda fast: path(records, pairs, owner, BLOCKS)[0],
        fast,
    )


def solution(mesh):
    return jax.shard_map(
        local,
        mesh=mesh,
        in_specs=(P("chan", None, "win", None), P(), P()),
        out_specs=P("chan", "win", None),
        check_vma=False,
    )
```

time: 303 us -> 103 us (0.34)
  the two profiles are of different devices: /device:TPU:152 before, /device:TPU:38 now
where the time goes in v2:
time: 103 us
  waiting for transfers between devices  33.5 us (33%)
  starting transfers between devices  24.5 us (24%)
  blocking collectives  22.1 us (21%)
  Pallas kernels  18 us (17%)
  other arithmetic  2.44 us (2%)
  local copies, waits for them, and re-layouts  1.2 us (1%)
    all_gather x1, blocking collectives, path(): lax.all_gather(give, 'win', axis=0, tiled=False, axis_index_groups=far_gr...  22.1 us
    ppermute x1, waiting for transfers between devices, path(): low_split = lax.ppermute(right, 'chan', forward)  8.26 us
    all_to_all x1, waiting for transfers between devices, path(): lax.all_to_all(part1, 'win', 0, 0, tiled=True, axis_index_groups=core_gro...  6.79 us
    pallas_call x1, Pallas kernels, spectra(): pl.pallas_call(lambda *refs: spectra_kernel(chunk, width, *refs), out_sha...  6.56 us
    pallas_call x2, Pallas kernels, products(): pl.pallas_call(lambda *refs: products_kernel(width, sides, *refs), out_sh...  6.02 us
    ppermute x1, waiting for transfers between devices, path(): high = lax.ppermute(left[None], 'chan', backward)  5.92 us
    ppermute x1, starting transfers between devices, path(): low_split = lax.ppermute(right, 'chan', forward)  5.86 us
    ppermute x1, waiting for transfers between devices, path(): high_split = lax.ppermute(left, 'chan', backward)  5.66 us
  transfers between devices with their start and end apart: 7, of which 6 were waited for; matrix products, arithmetic and copies ran while one was open for 1% of the time, Pallas kernels for 11%

profile of v2, /device:TPU:38, one launch (start us, length us, event | category | flops | bytes accessed | tf_op | source)
XLA Modules:
  0.0 102.7 jit_solution(3355309159474398854)
XLA Ops:
  0.0 0.1 pad_add_fusion.1.refs_0_
  0.1 0.0 copy-start.3
  0.1 0.0 copy-start.5
  0.1 6.6 %spectra.3 = (bf16[3,256,1024]{2,1,0:T(8,128)(2,1)S(1)}, bf16[2,256,1024]{2,1,0:T(8,128)(2,1)S(1)}, bf16[2,256,1024]{2,1,0:T(8,128)(2,1)S(1)}, s32[18]{0:T(128)S(1)}) custom-call(s32[2]{0:T(128)S(1)} %pad_add_fusion.1.refs_0_, s32[2,80]{1,0:T(2,128)} %bitcast.68, s32[80]{0:T(128)} %refs_2_.2, bf16[3,16,2,8,2,1024]{5,4,3,2,1,0:T(2,128)(2,1)} %bitcast.70, ...), custom_call_target="tpu_custom_call" | custom-call | flops 1610612736 | bytes 8388608 | tf_op jit(solution)/shard_map/spectra/pallas_call | solution.py:159
  6.6 3.8 %collective-permute-start.6 = (bf16[1,2,256,1024]{3,2,1,0:T(8,128)(2,1)S(1)}, bf16[1,2,256,1024]{3,2,1,0:T(8,128)(2,1)S(1)}, u32[]{:S(2)}, u32[]{:S(2)}) collective-permute-start(bf16[1,2,256,1024]{3,2,1,0:T(8,128)(2,1)S(1)} %bitcast.57), channel_id=1, source_target_pairs={{0,16},{16,32},{32,48},{48,64},{64,80},{80,96},{96,112},{112,128},... | collective-permute-start | bytes 3145736 | tf_op jit(solution)/shard_map/ppermute | solution.py:337
  10.4 2.1 %collective-permute-start.7 = (bf16[1,2,256,1024]{3,2,1,0:T(8,128)(2,1)S(1)}, bf16[1,2,256,1024]{3,2,1,0:T(8,128)(2,1)S(1)}, u32[]{:S(2)}, u32[]{:S(2)}) collective-permute-start(bf16[1,2,256,1024]{3,2,1,0:T(8,128)(2,1)S(1)} %bitcast.56), channel_id=1, source_target_pairs={{16,0},{32,16},{48,32},{64,48},{80,64},{96,80},{112,96},{128,112},... | collective-permute-start | bytes 3145736 | tf_op jit(solution)/shard_map/ppermute | solution.py:338
  12.5 0.0 copy-done.3
  12.5 0.0 copy-done.5
  12.5 3.5 %split_spectra.3 = (bf16[3,128,1024]{2,1,0:T(8,128)(2,1)S(1)}, bf16[3,128,1024]{2,1,0:T(8,128)(2,1)S(1)}) custom-call(s32[2]{0:T(128)S(1)} %pad_add_fusion.1.refs_0_, bf16[3,8,2,2,8,2,1024]{6,5,4,3,2,1,0:T(2,128)(2,1)S(1)} %bitcast.71, bf16[1024,1024]{1,0:T(8,128)(2,1)S(1)} %copy-done.5), custom_call_target="tpu_custom_call" | custom-call | flops 1610612736 | bytes 8388608 | tf_op jit(solution)/shard_map/split_spectra/pallas_call | solution.py:207
  16.0 1.9 %collective-permute-start.5 = (bf16[3,128,1024]{2,1,0:T(8,128)(2,1)S(1)}, bf16[3,128,1024]{2,1,0:T(8,128)(2,1)S(1)}, u32[]{:S(2)}, u32[]{:S(2)}) collective-permute-start(bf16[3,128,1024]{2,1,0:T(8,128)(2,1)S(1)} %get-tuple-element.62), channel_id=1, source_target_pairs={{0,1},{1,0},{2,3},{3,2},{4,5},{5,4},{6,7},{7,6},{8,9},{9,8},{10,11... | collective-permute-start | bytes 2359304 | tf_op jit(solution)/shard_map/ppermute | solution.py:342
  17.9 2.3 %collective-permute-done.5.refs_2_ = bf16[3,128,1024]{2,1,0:T(8,128)(2,1)S(1)} collective-permute-done((bf16[3,128,1024]{2,1,0:T(8,128)(2,1)S(1)}, bf16[3,128,1024]{2,1,0:T(8,128)(2,1)S(1)}, u32[]{:S(2)}, u32[]{:S(2)}) %collective-permute-start.5) | collective-permute-done | bytes 786464 | tf_op jit(solution)/shard_map/ppermute | solution.py:342
  20.2 2.0 %lanes.3 = (bf16[2,2,128,1024]{3,2,1,0:T(8,128)(2,1)}, bf16[2,2,128,1024]{3,2,1,0:T(8,128)(2,1)}) custom-call(s32[18]{0:T(128)S(1)} %get-tuple-element.59.refs_0_, bf16[3,128,1024]{2,1,0:T(8,128)(2,1)S(1)} %get-tuple-element.61.refs_1_, bf16[3,128,1024]{2,1,0:T(8,128)(2,1)S(1)} %collective-permute-done.5.refs_2_), custom_call_target="tpu_custom_call" | custom-call | bytes 4194304 | tf_op jit(solution)/shard_map/lanes/pallas_call | solution.py:243
  22.2 5.9 %collective-permute-start.8 = (bf16[2,2,128,1024]{3,2,1,0:T(8,128)(2,1)}, bf16[2,2,128,1024]{3,2,1,0:T(8,128)(2,1)S(1)}, u32[]{:S(2)}, u32[]{:S(2)}) collective-permute-start(bf16[2,2,128,1024]{3,2,1,0:T(8,128)(2,1)} %get-tuple-element.67), channel_id=1, source_target_pairs={{0,16},{16,32},{32,48},{48,64},{64,80},{80,96},{96,112},{112,128},... | collective-permute-start | bytes 3145736 | tf_op jit(solution)/shard_map/ppermute | solution.py:345
  28.0 1.9 %collective-permute-start.9 = (bf16[2,2,128,1024]{3,2,1,0:T(8,128)(2,1)}, bf16[2,2,128,1024]{3,2,1,0:T(8,128)(2,1)}, u32[]{:S(2)}, u32[]{:S(2)}) collective-permute-start(bf16[2,2,128,1024]{3,2,1,0:T(8,128)(2,1)} %get-tuple-element.68), channel_id=1, source_target_pairs={{16,0},{32,16},{48,32},{64,48},{80,64},{96,80},{112,96},{128,112},... | collective-permute-start | bytes 3145736 | tf_op jit(solution)/shard_map/ppermute | solution.py:346
  30.0 4.6 %collective-permute-done.6.refs_2_ = bf16[1,2,256,1024]{3,2,1,0:T(8,128)(2,1)S(1)} collective-permute-done((bf16[1,2,256,1024]{3,2,1,0:T(8,128)(2,1)S(1)}, bf16[1,2,256,1024]{3,2,1,0:T(8,128)(2,1)S(1)}, u32[]{:S(2)}, u32[]{:S(2)}) %collective-permute-start.6) | collective-permute-done | bytes 1048608 | tf_op jit(solution)/shard_map/ppermute | solution.py:337
  34.6 5.9 %collective-permute-done.7.refs_3_ = bf16[1,2,256,1024]{3,2,1,0:T(8,128)(2,1)S(1)} collective-permute-done((bf16[1,2,256,1024]{3,2,1,0:T(8,128)(2,1)S(1)}, bf16[1,2,256,1024]{3,2,1,0:T(8,128)(2,1)S(1)}, u32[]{:S(2)}, u32[]{:S(2)}) %collective-permute-start.7) | collective-permute-done | bytes 1048608 | tf_op jit(solution)/shard_map/ppermute | solution.py:338
  40.5 2.7 %products.6 = bf16[8,4,16,1024]{3,2,1,0:T(8,128)(2,1)} custom-call(s32[18]{0:T(128)S(1)} %get-tuple-element.59.refs_0_, bf16[3,256,1024]{2,1,0:T(8,128)(2,1)S(1)} %get-tuple-element.64.refs_1_, bf16[1,2,256,1024]{3,2,1,0:T(8,128)(2,1)S(1)} %collective-permute-done.6.refs_2_, bf16[1,2,256,1024]{3,2,1,0:T(8,128)(2,1)S(1)} %collective-permute-done.7.refs_3_), custom_call_target="tpu_custom_call" | custom-call | flops 33554432 | bytes 8388608 | tf_op jit(solution)/shard_map/products/pallas_call | solution.py:311
  43.2 4.5 %all-to-all-start.2 = ((bf16[8,4,16,1024]{3,2,1,0:T(8,128)(2,1)}), bf16[8,4,16,1024]{3,2,1,0:T(8,128)(2,1)}, u32[]{:S(2)}, u32[]{:S(2)}) async-start(bf16[8,4,16,1024]{3,2,1,0:T(8,128)(2,1)} %products.6), calls=%async_computation.2 | async-start | bytes 2097152 | tf_op jit(solution)/shard_map/all_to_all | solution.py:359
  47.7 8.3 %collective-permute-done.8.refs_3_ = bf16[2,2,128,1024]{3,2,1,0:T(8,128)(2,1)S(1)} collective-permute-done((bf16[2,2,128,1024]{3,2,1,0:T(8,128)(2,1)}, bf16[2,2,128,1024]{3,2,1,0:T(8,128)(2,1)S(1)}, u32[]{:S(2)}, u32[]{:S(2)}) %collective-permute-start.8) | collective-permute-done | bytes 1048608 | tf_op jit(solution)/shard_map/ppermute | solution.py:345
  55.9 5.7 %collective-permute-done.9.refs_4_ = bf16[2,2,128,1024]{3,2,1,0:T(8,128)(2,1)} collective-permute-done((bf16[2,2,128,1024]{3,2,1,0:T(8,128)(2,1)}, bf16[2,2,128,1024]{3,2,1,0:T(8,128)(2,1)}, u32[]{:S(2)}, u32[]{:S(2)}) %collective-permute-start.9) | collective-permute-done | bytes 1048608 | tf_op jit(solution)/shard_map/ppermute | solution.py:346
  61.6 3.4 %products.7 = bf16[4,4,16,1024]{3,2,1,0:T(8,128)(2,1)} custom-call(s32[18]{0:T(128)S(1)} %get-tuple-element.59.refs_0_, bf16[3,128,1024]{2,1,0:T(8,128)(2,1)S(1)} %get-tuple-element.61.refs_1_, bf16[3,128,1024]{2,1,0:T(8,128)(2,1)S(1)} %collective-permute-done.5.refs_2_, bf16[2,2,128,1024]{3,2,1,0:T(8,128)(2,1)S(1)} %collective-permute-done.8.refs_3_, ...), custom_call_target="tpu_custom_call" | custom-call | flops 33554432 | bytes 8388608 | tf_op jit(solution)/shard_map/products/pallas_call | solution.py:311
  65.0 0.0 all-to-all-done.2
  65.0 4.5 %all-to-all-start.3 = ((bf16[4,4,16,1024]{3,2,1,0:T(8,128)(2,1)}), bf16[4,4,16,1024]{3,2,1,0:T(8,128)(2,1)S(1)}, u32[]{:S(2)}, u32[]{:S(2)}) async-start(bf16[4,4,16,1024]{3,2,1,0:T(8,128)(2,1)} %products.7), calls=%async_computation.3 | async-start | bytes 1048576 | tf_op jit(solution)/shard_map/all_to_all | solution.py:362
  69.5 0.0 copy-start.1
  69.5 0.0 copy-start.2
  69.5 1.4 %convert_reduce_fusion.2 = f32[4,16,1024]{2,1,0:T(8,128)S(1)} fusion(bf16[8,4,16,1024]{3,2,1,0:T(8,128)(2,1)} %all-to-all-done.2), kind=kLoop, calls=%fused_computation.12 | loop fusion | flops 983040 | bytes 1310720 | tf_op jit(solution)/shard_map/reduce_sum | solution.py:353
  70.9 0.0 copy-start.6
  70.9 6.8 %all-to-all-done.3 = bf16[4,4,16,1024]{3,2,1,0:T(8,128)(2,1)S(1)} async-done(((bf16[4,4,16,1024]{3,2,1,0:T(8,128)(2,1)}), bf16[4,4,16,1024]{3,2,1,0:T(8,128)(2,1)S(1)}, u32[]{:S(2)}, u32[]{:S(2)}) %all-to-all-start.3) | async-done | bytes 524320 | tf_op jit(solution)/shard_map/all_to_all | solution.py:362
  77.7 0.1 convert_reduce_fusion.3
  77.9 0.0 copy-done.1
  77.9 0.0 copy-done.2
  77.9 0.1 fusion.5
  78.0 0.1 stack.30
  78.1 0.1 copy.15
  78.2 0.1 stack.31
  78.3 0.1 copy.16
  78.5 0.6 reduce_max.9
  79.8 22.1 %all-gather.1 = bf16[8,16,1024]{2,1,0:T(8,128)(2,1)S(1)} all-gather(bf16[4,16,1024]{2,1,0:T(8,128)(2,1)S(1)} %pad_maximum_fusion.2), channel_id=3, replica_groups={{0,8},{1,9},{2,10},{3,11},{4,12},{5,13},{6,14},{7,15},{16,24},{17,25},{..., dimensions={0}, use_global_device_ids=true | all-gather | bytes 393216 | tf_op jit(solution)/shard_map/all_gather | solution.py:366
  102.0 0.0 copy-done.6
  102.0 0.1 conditional.1
  102.0 0.0 copy-start
  102.0 0.7 copy-done
  (8 shorter events, 0.2 us)
Async XLA Ops:
  0.1 12.4 %copy-start.3 = (bf16[3,256,2,1024]{3,2,1,0:T(2,128)(2,1)S(1)}, bf16[3,256,2,1024]{3,2,1,0:T(2,128)(2,1)}, u32[]{:S(2)}) copy-start(bf16[3,256,2,1024]{3,2,1,0:T(2,128)(2,1)} %param.7) | copy-start | bytes 9437188
  0.1 12.4 %copy-start.5 = (bf16[1024,1024]{1,0:T(8,128)(2,1)S(1)}, bf16[1024,1024]{1,0:T(8,128)(2,1)}, u32[]{:S(2)}) copy-start(bf16[1024,1024]{1,0:T(8,128)(2,1)} %constant.120.clone.refs_4_.refs_2_) | copy-start | bytes 6291460
  6.6 27.9 %collective-permute-start.6 = (bf16[1,2,256,1024]{3,2,1,0:T(8,128)(2,1)S(1)}, bf16[1,2,256,1024]{3,2,1,0:T(8,128)(2,1)S(1)}, u32[]{:S(2)}, u32[]{:S(2)}) collective-permute-start(bf16[1,2,256,1024]{3,2,1,0:T(8,128)(2,1)S(1)} %bitcast.57), channel_id=1, source_target_pairs={{0,16},{16,32},{32,48},{48,64},{64,80},{80,96},{96,112},{112,128},... | collective-permute-start | bytes 3145736 | tf_op jit(solution)/shard_map/ppermute | solution.py:337
  10.4 30.1 %collective-permute-start.7 = (bf16[1,2,256,1024]{3,2,1,0:T(8,128)(2,1)S(1)}, bf16[1,2,256,1024]{3,2,1,0:T(8,128)(2,1)S(1)}, u32[]{:S(2)}, u32[]{:S(2)}) collective-permute-start(bf16[1,2,256,1024]{3,2,1,0:T(8,128)(2,1)S(1)} %bitcast.56), channel_id=1, source_target_pairs={{16,0},{32,16},{48,32},{64,48},{80,64},{96,80},{112,96},{128,112},... | collective-permute-start | bytes 3145736 | tf_op jit(solution)/shard_map/ppermute | solution.py:338
  16.0 4.2 %collective-permute-start.5 = (bf16[3,128,1024]{2,1,0:T(8,128)(2,1)S(1)}, bf16[3,128,1024]{2,1,0:T(8,128)(2,1)S(1)}, u32[]{:S(2)}, u32[]{:S(2)}) collective-permute-start(bf16[3,128,1024]{2,1,0:T(8,128)(2,1)S(1)} %get-tuple-element.62), channel_id=1, source_target_pairs={{0,1},{1,0},{2,3},{3,2},{4,5},{5,4},{6,7},{7,6},{8,9},{9,8},{10,11... | collective-permute-start | bytes 2359304 | tf_op jit(solution)/shard_map/ppermute | solution.py:342
  22.2 33.8 %collective-permute-start.8 = (bf16[2,2,128,1024]{3,2,1,0:T(8,128)(2,1)}, bf16[2,2,128,1024]{3,2,1,0:T(8,128)(2,1)S(1)}, u32[]{:S(2)}, u32[]{:S(2)}) collective-permute-start(bf16[2,2,128,1024]{3,2,1,0:T(8,128)(2,1)} %get-tuple-element.67), channel_id=1, source_target_pairs={{0,16},{16,32},{32,48},{48,64},{64,80},{80,96},{96,112},{112,128},... | collective-permute-start | bytes 3145736 | tf_op jit(solution)/shard_map/ppermute | solution.py:345
  28.0 33.5 %collective-permute-start.9 = (bf16[2,2,128,1024]{3,2,1,0:T(8,128)(2,1)}, bf16[2,2,128,1024]{3,2,1,0:T(8,128)(2,1)}, u32[]{:S(2)}, u32[]{:S(2)}) collective-permute-start(bf16[2,2,128,1024]{3,2,1,0:T(8,128)(2,1)} %get-tuple-element.68), channel_id=1, source_target_pairs={{16,0},{32,16},{48,32},{64,48},{80,64},{96,80},{112,96},{128,112},... | collective-permute-start | bytes 3145736 | tf_op jit(solution)/shard_map/ppermute | solution.py:346
  43.2 21.8 %all-to-all-start.2 = ((bf16[8,4,16,1024]{3,2,1,0:T(8,128)(2,1)}), bf16[8,4,16,1024]{3,2,1,0:T(8,128)(2,1)}, u32[]{:S(2)}, u32[]{:S(2)}) async-start(bf16[8,4,16,1024]{3,2,1,0:T(8,128)(2,1)} %products.6), calls=%async_computation.2 | async-start | bytes 2097152 | tf_op jit(solution)/shard_map/all_to_all | solution.py:359
  65.0 12.7 %all-to-all-start.3 = ((bf16[4,4,16,1024]{3,2,1,0:T(8,128)(2,1)}), bf16[4,4,16,1024]{3,2,1,0:T(8,128)(2,1)S(1)}, u32[]{:S(2)}, u32[]{:S(2)}) async-start(bf16[4,4,16,1024]{3,2,1,0:T(8,128)(2,1)} %products.7), calls=%async_computation.3 | async-start | bytes 1048576 | tf_op jit(solution)/shard_map/all_to_all | solution.py:362
  69.5 8.4 %copy-start.1 = (s32[80,2]{0,1:T(2,128)S(1)}, s32[80,2]{0,1:T(2,128)}, u32[]{:S(2)}) copy-start(s32[80,2]{0,1:T(2,128)} %param.8) | copy-start | bytes 1924
  69.5 8.4 %copy-start.2 = (s32[80]{0:T(128)S(1)}, s32[80]{0:T(128)}, u32[]{:S(2)}) copy-start(s32[80]{0:T(128)} %refs_2_.2) | copy-start | bytes 964
  70.9 31.1 %copy-start.6 = (bf16[1024,1024]{1,0:T(8,128)(2,1)S(1)}, bf16[1024,1024]{1,0:T(8,128)(2,1)}, u32[]{:S(2)}) copy-start(bf16[1024,1024]{1,0:T(8,128)(2,1)} %constant.120.clone.refs_4_.refs_2_) | copy-start | bytes 6291460
  102.0 0.7 copy-start

commit v3 on v0

v3 whole, which is shorter than its diff:
```python
import math

import jax
import jax.numpy as jnp
import ml_dtypes
import numpy as np
from jax import lax
from jax.experimental import pallas as pl
from jax.experimental.pallas import tpu as pltpu
from jax.sharding import PartitionSpec as P

PCAP = 4
BLOCKS = 3
CHAN = 32
CHUNKS = 2
LENGTH = 1024
BINS = 512
HALF = 16 // CHUNKS
ROWS = 512 // CHUNKS
VMEM = pl.BlockSpec(memory_space=pltpu.VMEM)
SMEM = pl.BlockSpec(memory_space=pltpu.SMEM)
ANY = pl.BlockSpec(memory_space=pl.ANY)
HBM = pl.BlockSpec(memory_space=pltpu.HBM)
PARAMS = pltpu.CompilerParams(vmem_limit_bytes=40 << 20)
ALL_VMEM = pltpu.CompilerParams(vmem_limit_bytes=63 << 20)


def basis_table():
    sample_ids = np.arange(LENGTH, dtype=np.int32)
    bin_ids = np.arange(BINS, dtype=np.int32)
    step = np.float32(2.0 * math.pi / LENGTH)
    phases = (sample_ids[:, None] * bin_ids[None, :] % LENGTH).astype(np.float32) * step
    taper = np.float32(0.5) - np.float32(0.5) * np.cos(sample_ids.astype(np.float32) * step)
    table = np.concatenate([taper[:, None] * np.cos(phases), -taper[:, None] * np.sin(phases)], axis=1)
    return table.astype(ml_dtypes.bfloat16)


LANES, FIRST, SECOND, USED, TABLE = 0, 6, 10, 14, 18
SWAPS = [
    [pair for low in range(start, CHAN - 1, 2) for pair in ((low, low + 1), (low + 1, low))] for start in (1, 0)
]


def table_kernel(where, pairs_hbm, owner_hbm, narrow, wide, flag, pairs, owner, rows, sems):
    copies = [
        pltpu.make_async_copy(pairs_hbm, pairs, sems.at[0]),
        pltpu.make_async_copy(owner_hbm, owner, sems.at[1]),
    ]
    for copy in copies:
        copy.start()
    odd = where[0] % 2
    me = where[0].astype(jnp.float32)
    count = owner.shape[1]
    for copy in copies:
        copy.wait()
    rows[...] = jnp.full(rows.shape, -1000.0, jnp.float32)
    rows[0:2, 0:count] = pairs[...].astype(jnp.float32)
    rows[2:3, 0:count] = owner[...].astype(jnp.float32)
    first = rows[0:1, :]
    second = rows[1:2, :]
    holder = rows[2:3, :]

    chan = lax.broadcasted_iota(jnp.int32, (CHAN, 128), 0).astype(jnp.float32)

    def all_three(block, step):
        hits = [
            jnp.max(jnp.where((block == BLOCKS * chan + i) & (holder == chan + step), 1.0, 0.0), axis=1, keepdims=True)
            for i in range(BLOCKS)
        ]
        return hits[0] * hits[1] * hits[2]

    most = jnp.max(jnp.maximum(all_three(first, 1.0), all_three(second, -1.0)))

    def total(hit, value=1.0):
        return jnp.sum(jnp.where(hit, value, 0.0))

    first = first - BLOCKS * me
    second = second - BLOCKS * me
    apart = holder - me
    mine = apart == 0.0

    def needs(hit, block):
        return [(total(hit & (block == float(i))) > 0.0).astype(jnp.int32) for i in range(BLOCKS)]

    to_right = needs(apart == 1.0, first)
    to_left = needs(apart == -1.0, second)
    of_left = needs(mine, first + BLOCKS)
    of_right = needs(mine, second - BLOCKS)
    earlier = lax.broadcasted_iota(jnp.int32, (128, 128), 0) < lax.broadcasted_iota(jnp.int32, (128, 128), 1)
    ranks = jnp.dot(
        jnp.broadcast_to(jnp.where(mine, 1.0, 0.0), (8, 128)).astype(jnp.bfloat16),
        jnp.where(earlier, 1.0, 0.0).astype(jnp.bfloat16),
        preferred_element_type=jnp.float32,
    )[0:1, :]
    number = total(mine).astype(jnp.int32)

    def spot(need, block, width):
        if width == BLOCKS:
            return block
        return jnp.where(block == 0, 0, jnp.where(block == 1, need[0], jnp.minimum(need[0] + need[1], width - 1)))

    def picks(need, width):
        if width == BLOCKS:
            return [jnp.int32(i) for i in range(BLOCKS)]
        n0, n1, n2 = [n > 0 for n in need]
        lowest = jnp.where(n0, 0, jnp.where(n1, 1, jnp.where(n2, 2, 0)))
        after = jnp.where(n0 & n1, 1, jnp.where(n2 & (n0 | n1), 2, 0))
        return [lowest.astype(jnp.int32), after.astype(jnp.int32), jnp.int32(0)]

    flag[0] = most.astype(jnp.int32)
    for info, width in ((narrow, 2), (wide, BLOCKS)):
        for i, (right, left) in enumerate(zip(picks(to_right, width), picks(to_left, width))):
            info[LANES + i] = jnp.where(odd == 1, right, left)
            info[LANES + 3 + i] = jnp.where(odd == 1, left, right)
    for slot in range(PCAP):
        hit = mine & (ranks == float(slot))
        a = total(hit, first).astype(jnp.int32)
        b = total(hit, second).astype(jnp.int32)
        used = (number > slot).astype(jnp.int32)
        for info, width in ((narrow, 2), (wide, BLOCKS)):
            from_left = BLOCKS + odd * width
            from_right = BLOCKS + (1 - odd) * width
            info[FIRST + slot] = jnp.where(a < 0, from_left + spot(of_left, a + BLOCKS, width), a)
            info[SECOND + slot] = jnp.where(b >= BLOCKS, from_right + spot(of_right, b - BLOCKS, width), b)
            info[USED + slot] = used


def tables(where, pairs, owner):
    table = jax.ShapeDtypeStruct((TABLE,), jnp.int32)
    return pl.pallas_call(
        table_kernel,
        out_shape=(table, table, jax.ShapeDtypeStruct((1,), jnp.int32)),
        in_specs=[SMEM, HBM, HBM],
        out_specs=[SMEM] * 3,
        scratch_shapes=[
            pltpu.VMEM((2, pairs.shape[0]), jnp.int32),
            pltpu.VMEM((1, pairs.shape[0]), jnp.int32),
            pltpu.VMEM((8, 128), jnp.float32),
            pltpu.SemaphoreType.DMA((2,)),
        ],
        compiler_params=ALL_VMEM,
        name="tables",
    )(where, pairs.T, owner[None])


def whitened(rows, basis):
    spectrum = jnp.dot(rows, basis, preferred_element_type=jnp.float32)
    power_mean = jnp.mean(spectrum * spectrum, axis=-1, keepdims=True)
    return (spectrum * lax.rsqrt(power_mean + 1e-06)).astype(jnp.bfloat16)


COST = pl.CostEstimate(flops=2 * 3 * ROWS * LENGTH * LENGTH, bytes_accessed=8 << 20, transcendentals=0)


def deal_kernel(x, deal, buf, xsem, dsem):
    loads = [pltpu.make_async_copy(x.at[block, :, 1], buf.at[block], xsem.at[block]) for block in range(BLOCKS)]
    stores = [
        [
            pltpu.make_async_copy(buf.at[block, z * 8 + peer], deal.at[peer, block, z], dsem.at[peer, block, z])
            for peer in range(8)
            for z in range(2)
        ]
        for block in range(BLOCKS)
    ]
    for copy in loads:
        copy.start()
    for load, copies in zip(loads, stores):
        load.wait()
        for copy in copies:
            copy.start()
    for copies in stores:
        for copy in copies:
            copy.wait()


def dealing(x):
    return pl.pallas_call(
        deal_kernel,
        out_shape=jax.ShapeDtypeStruct((8, BLOCKS, 2, HALF, 2, LENGTH), jnp.bfloat16),
        in_specs=[HBM],
        out_specs=ANY,
        scratch_shapes=[
            pltpu.VMEM((BLOCKS, 16, HALF, 2, LENGTH), jnp.bfloat16),
            pltpu.SemaphoreType.DMA((BLOCKS,)),
            pltpu.SemaphoreType.DMA((8, BLOCKS, 2)),
        ],
        compiler_params=PARAMS,
        cost_estimate=pl.CostEstimate(flops=0, bytes_accessed=3 << 20, transcendentals=0),
        name="deal",
    )(x)


def lane_copy(buf, block, lanes, way, spot, lsem):
    return pltpu.make_async_copy(buf.at[block], lanes[way].at[spot], lsem.at[way, spot])


def start_lanes(width, info, buf, block, lanes, lsem):
    for way in range(2):
        for spot in range(width):

            @pl.when(info[LANES + way * 3 + spot] == block)
            def _(way=way, spot=spot):
                lane_copy(buf, block, lanes, way, spot, lsem).start()


def wait_lanes(width, buf, lanes, lsem):
    for way in range(2):
        for spot in range(width):
            lane_copy(buf, 0, lanes, way, spot, lsem).wait()


def raw_lanes_kernel(width, info, x, one, two, buf, xsem, lsem):
    loads = [pltpu.make_async_copy(x.at[block, :, 0], buf.at[block], xsem.at[block]) for block in range(BLOCKS)]
    for copy in loads:
        copy.start()
    for block, copy in enumerate(loads):
        copy.wait()
        start_lanes(width, info, buf, block, (one, two), lsem)
    wait_lanes(width, buf, (one, two), lsem)


def raw_lanes(width, info, x):
    lane = jax.ShapeDtypeStruct((width, 16, HALF, 2, LENGTH), jnp.bfloat16)
    return pl.pallas_call(
        lambda *refs: raw_lanes_kernel(width, *refs),
        out_shape=(lane, lane),
        in_specs=[SMEM, HBM],
        out_specs=[ANY] * 2,
        scratch_shapes=[
            pltpu.VMEM((BLOCKS, 16, HALF, 2, LENGTH), jnp.bfloat16),
            pltpu.SemaphoreType.DMA((BLOCKS,)),
            pltpu.SemaphoreType.DMA((2, width)),
        ],
        compiler_params=PARAMS,
        cost_estimate=pl.CostEstimate(flops=0, bytes_accessed=4 << 20, transcendentals=0),
        name="raw_lanes",
    )(info, x)


def spectra_kernel(count, at, x, basis, own, xbuf, spec, xsem, osem):
    def load(block):
        return pltpu.make_async_copy(x.at[at(block)], xbuf.at[block], xsem.at[block])

    def store(block):
        return pltpu.make_async_copy(spec.at[block], own.at[block], osem.at[block])

    for block in range(count):
        load(block).start()
    for block in range(count):
        load(block).wait()
        spec[block] = whitened(xbuf[block].reshape(ROWS, LENGTH), basis[...])
        store(block).start()
    for block in range(count):
        store(block).wait()


def spectra(count, at, x, basis):
    return pl.pallas_call(
        lambda *refs: spectra_kernel(count, at, *refs),
        out_shape=jax.ShapeDtypeStruct((count, ROWS, LENGTH), jnp.bfloat16),
        in_specs=[HBM, VMEM],
        out_specs=ANY,
        scratch_shapes=[
            pltpu.VMEM((count, 16, HALF, 2, LENGTH), jnp.bfloat16),
            pltpu.VMEM((count, ROWS, LENGTH), jnp.bfloat16),
            pltpu.SemaphoreType.DMA((count,)),
            pltpu.SemaphoreType.DMA((count,)),
        ],
        compiler_params=PARAMS,
        cost_estimate=COST,
        name="spectra",
    )(x, basis)


def dealt_kernel(width, info, x, basis, own, one, two, spec, osem, lsem):
    def store(block):
        return pltpu.make_async_copy(spec.at[block], own.at[block], osem.at[block])

    for block in range(BLOCKS):
        spec[block] = whitened(x[:, block].reshape(ROWS, LENGTH), basis[...])
        start_lanes(width, info, spec, block, (one, two), lsem)
        store(block).start()
    wait_lanes(width, spec, (one, two), lsem)
    for block in range(BLOCKS):
        store(block).wait()


def dealt_spectra(width, info, x, basis):
    own = jax.ShapeDtypeStruct((BLOCKS, ROWS, LENGTH), jnp.bfloat16)
    lane = jax.ShapeDtypeStruct((width, ROWS, LENGTH), jnp.bfloat16)
    return pl.pallas_call(
        lambda *refs: dealt_kernel(width, *refs),
        out_shape=(own, lane, lane),
        in_specs=[SMEM, VMEM, VMEM],
        out_specs=[HBM] * 3,
        scratch_shapes=[
            pltpu.VMEM((BLOCKS, ROWS, LENGTH), jnp.bfloat16),
            pltpu.SemaphoreType.DMA((BLOCKS,)),
            pltpu.SemaphoreType.DMA((2, width)),
        ],
        compiler_params=PARAMS,
        cost_estimate=COST,
        name="dealt_spectra",
    )(info, x, basis)


def parts(read, at, lane):
    a_re, a_im, b_re, b_im = [
        read(operand, at, pl.ds(start + lane * 128, 128)).astype(jnp.float32)
        for operand in range(2)
        for start in (0, BINS)
    ]
    return a_re * b_re + a_im * b_im, a_im * b_re - a_re * b_im


def pair_sums(acc):
    return acc[pl.ds(0, HALF, 2), :] + acc[pl.ds(1, HALF, 2), :]


def tile(index):
    return pl.ds(pl.multiple_of(index * 2 * HALF, 2 * HALF), 2 * HALF)


def raw_products_kernel(width, info, basis, own, one, two, out, xbuf, buf, acc, xsem, osem):
    loads = [pltpu.make_async_copy(two.at[spot], xbuf.at[spot], xsem.at[spot]) for spot in range(width)]
    ready = [
        pltpu.make_async_copy(own, buf.at[pl.ds(0, BLOCKS)], osem.at[0]),
        pltpu.make_async_copy(one, buf.at[pl.ds(BLOCKS, width)], osem.at[1]),
    ]
    for copy in loads + ready:
        copy.start()
    for spot, copy in enumerate(loads):
        copy.wait()
        buf[BLOCKS + width + spot] = whitened(xbuf[spot].reshape(ROWS, LENGTH), basis[...])
    for copy in ready:
        copy.wait()

    @pl.loop(0, PCAP)
    def _(slot):
        spots = info[FIRST + slot], info[SECOND + slot]

        def read(operand, at, part):
            return buf[spots[operand], at, part]

        @pl.when(info[USED + slot] > 0)
        def _():
            @pl.loop(0, 8)
            def _(peer):
                for lane in range(BINS // 128):
                    for z in range(2):
                        acc[lane, z, 0], acc[lane, z, 1] = parts(read, tile(z * 8 + peer), lane)
                    for part in range(2):
                        sums = [pair_sums(acc.at[lane, z, part]) for z in range(2)]
                        out[peer, slot, :, pl.ds(part * BINS + lane * 128, 128)] = jnp.concatenate(
                            sums, axis=0
                        ).astype(jnp.bfloat16)

        @pl.when(info[USED + slot] == 0)
        def _():
            @pl.loop(0, 8)
            def _(peer):
                out[peer, slot] = jnp.zeros((2 * HALF, LENGTH), jnp.bfloat16)


def raw_products(width, info, basis, own, one, two):
    return pl.pallas_call(
        lambda *refs: raw_products_kernel(width, *refs),
        out_shape=jax.ShapeDtypeStruct((8, PCAP, 2 * HALF, LENGTH), jnp.bfloat16),
        in_specs=[SMEM, VMEM, ANY, ANY, HBM],
        out_specs=VMEM,
        scratch_shapes=[
            pltpu.VMEM((width, 16, HALF, 2, LENGTH), jnp.bfloat16),
            pltpu.VMEM((BLOCKS + 2 * width, ROWS, LENGTH), jnp.bfloat16),
            pltpu.VMEM((BINS // 128, 2, 2, 2 * HALF, 128), jnp.float32),
            pltpu.SemaphoreType.DMA((width,)),
            pltpu.SemaphoreType.DMA((2,)),
        ],
        compiler_params=PARAMS,
        cost_estimate=COST,
        name="raw_products",
    )(info, basis, own, one, two)


def dealt_products_kernel(width, info, own, one, two, out, buf, acc, sems):
    def start(slot, operand, spot):
        to, sem = buf.at[slot, operand], sems.at[slot, operand]

        @pl.when(spot < BLOCKS)
        def _():
            pltpu.make_async_copy(own.at[spot], to, sem).start()

        @pl.when((spot >= BLOCKS) & (spot < BLOCKS + width))
        def _():
            pltpu.make_async_copy(one.at[spot - BLOCKS], to, sem).start()

        @pl.when(spot >= BLOCKS + width)
        def _():
            pltpu.make_async_copy(two.at[spot - BLOCKS - width], to, sem).start()

    for slot in range(PCAP):

        @pl.when(info[USED + slot] > 0)
        def _(slot=slot):
            start(slot, 0, info[FIRST + slot])
            start(slot, 1, info[SECOND + slot])

    @pl.loop(0, PCAP)
    def _(slot):
        def read(operand, at, part):
            return buf[slot, operand, at, part]

        @pl.when(info[USED + slot] > 0)
        def _():
            for operand in range(2):
                pltpu.make_async_copy(own.at[0], buf.at[slot, operand], sems.at[slot, operand]).wait()

            @pl.loop(0, 2)
            def _(z):
                for lane in range(BINS // 128):
                    real, imag = parts(read, tile(z), lane)
                    for source in range(1, 8):
                        re, im = parts(read, tile(source * 2 + z), lane)
                        real, imag = real + re, imag + im
                    acc[lane, 0], acc[lane, 1] = real, imag
                    for part in range(2):
                        out[z, slot, :, pl.ds(part * BINS + lane * 128, 128)] = pair_sums(acc.at[lane, part])

        @pl.when(info[USED + slot] == 0)
        def _():
            for z in range(2):
                out[z, slot] = jnp.zeros((HALF, LENGTH), jnp.float32)


def dealt_products(width, info, own, one, two):
    return pl.pallas_call(
        lambda *refs: dealt_products_kernel(width, *refs),
        out_shape=jax.ShapeDtypeStruct((2, PCAP, HALF, LENGTH), jnp.float32),
        in_specs=[SMEM] + [ANY] * 3,
        out_specs=VMEM,
        scratch_shapes=[
            pltpu.VMEM((PCAP, 2, ROWS, LENGTH), jnp.bfloat16),
            pltpu.VMEM((BINS // 128, 2, 2 * HALF, 128), jnp.float32),
            pltpu.SemaphoreType.DMA((PCAP, 2)),
        ],
        compiler_params=PARAMS,
        cost_estimate=pl.CostEstimate(flops=1 << 25, bytes_accessed=8 << 20, transcendentals=0),
        name="dealt_products",
    )(info, own, one, two)


def path(records, info, width):
    far = lax.axis_index("win") // 8
    basis = jnp.asarray(basis_table())
    x = records.reshape(BLOCKS, 16, CHUNKS, HALF, 2, LENGTH)
    chip_groups = [[z * 8 + j for j in range(8)] for z in range(2)]
    far_groups = [[z * 8 + j for z in range(2)] for j in range(8)]

    deal = dealing(x)
    x, deal = lax.optimization_barrier((x, deal))
    dealt = lax.all_to_all(deal, "win", 0, 0, tiled=True, axis_index_groups=chip_groups)
    raw_one, raw_two = [lax.ppermute(lane, "chan", swap) for lane, swap in zip(raw_lanes(width, info, x), SWAPS)]
    dealt_own, *sent = dealt_spectra(width, info, dealt, basis)
    raw_basis, *sent = lax.optimization_barrier((basis, *sent))
    came = [lax.ppermute(lane, "chan", swap) for lane, swap in zip(sent, SWAPS)]
    own = spectra(BLOCKS, lambda block: (block, slice(None), 0), x, basis)
    one = spectra(width, lambda spot: (spot,), raw_one, raw_basis)

    part = raw_products(width, info, raw_basis, own, one, raw_two)
    first = lax.all_to_all(part, "win", 0, 0, tiled=True, axis_index_groups=chip_groups)
    dealt_own, part = lax.optimization_barrier((dealt_own, part))
    second = dealt_products(width, info, dealt_own, *came)
    first, second = lax.optimization_barrier((first, second))
    first = jnp.sum(first.astype(jnp.float32), axis=0).reshape(PCAP, 2, HALF, LENGTH)

    def half(at):
        return jnp.concatenate(
            [
                lax.dynamic_index_in_dim(first, at, axis=1, keepdims=False),
                lax.dynamic_index_in_dim(second, at, axis=0, keepdims=False),
            ],
            axis=1,
        )

    give = half(1 - far).astype(jnp.bfloat16)

    def swapped(slots):
        got = lax.all_gather(give[:slots], "win", axis=0, tiled=True, axis_index_groups=far_groups)
        got = lax.dynamic_slice_in_dim(got, (1 - far) * slots, slots, axis=0).astype(jnp.float32)
        return jnp.concatenate([got, jnp.zeros((PCAP - slots,) + got.shape[1:], jnp.float32)], axis=0)

    got = lax.cond(info[USED + 2] > 0, lambda: swapped(PCAP), lambda: swapped(PCAP // 2))
    return half(far) + got


def local(records, pairs, owner):
    where = lax.axis_index("chan")[None].astype(jnp.int32)
    narrow, wide, three = tables(where, pairs, owner)
    return lax.cond(
        three.reshape(()) == 0,
        lambda: path(records, narrow, 2),
        lambda: path(records, wide, BLOCKS),
    )


def solution(mesh):
    return jax.shard_map(
        local,
        mesh=mesh,
        in_specs=(P("chan", None, "win", None), P(), P()),
        out_specs=P("chan", "win", None),
        check_vma=False,
    )
```

time: 303 us -> 97.2 us (0.32)
  the two profiles are of different devices: /device:TPU:152 before, /device:TPU:2 now
where the time goes in v3:
time: 97.2 us; the launch traced here: 96.6 us
  Pallas kernels  27 us (28%)
  starting transfers between devices  25.3 us (26%)
  blocking collectives  20.9 us (22%)
  waiting for transfers between devices  17.7 us (18%)
  local copies, waits for them, and re-layouts  2.52 us (3%)
  other arithmetic  1.48 us (2%)
  loops' own time  1.05 us (1%)
    all_gather x1, blocking collectives, swapped(): lax.all_gather(give[:slots], 'win', axis=0, tiled=True, axis_index_groups...  20.9 us
    ppermute x2, waiting for transfers between devices, path(): came = [lax.ppermute(lane, 'chan', swap) for lane, swap in zip(sent, SWAPS)]  9.83 us
    ppermute x2, starting transfers between devices, path(): lax.ppermute(lane, 'chan', swap)  8.85 us
    ppermute x2, starting transfers between devices, path(): came = [lax.ppermute(lane, 'chan', swap) for lane, swap in zip(sent, SWAPS)]  7.56 us
    pallas_call x2, Pallas kernels, spectra(): pl.pallas_call(lambda *refs: spectra_kernel(count, at, *refs), out_shape=...  7.1 us
    pallas_call x1, Pallas kernels, dealt_spectra(): pl.pallas_call(lambda *refs: dealt_kernel(width, *refs), out_shape=(own,...  5.11 us
    all_to_all x1, waiting for transfers between devices, path(): lax.all_to_all(deal, 'win', 0, 0, tiled=True, axis_index_groups=chip_groups)  5.11 us
    pallas_call x1, Pallas kernels, raw_products(): pl.pallas_call(lambda *refs: raw_products_kernel(width, *refs), out_shape...  5.1 us
  transfers between devices with their start and end apart: 6, of which 4 were waited for; matrix products, arithmetic and copies ran while one was open for 1% of the time, Pallas kernels for 24%

profile of v3, /device:TPU:2, one launch (start us, length us, event | category | flops | bytes accessed | tf_op | source)
XLA Modules:
  0.0 96.6 jit_solution(13641791746695441690)
XLA Ops:
  0.0 1.6 %tables.1 = (s32[18]{0:T(128)S(1)}, s32[18]{0:T(128)S(1)}, s32[1]{0:T(128)}) custom-call(s32[1]{0:T(128)} %bitcast.14.where, s32[2,80]{1,0:T(2,128)} %bitcast.44, s32[1,80]{1,0:T(1,128)} %bitcast.45), custom_call_target="tpu_custom_call" | custom-call | tf_op jit(solution)/shard_map/tables/pallas_call | solution.py:130
  2.2 93.7 %conditional.3 = (f32[4,16,1024]{2,1,0:T(8,128)S(1)}) conditional(s32[]{:T(128)} %bitcast.17, (bf16[3,256,2,1024]{3,2,1,0:T(2,128)(2,1)}, s32[18]{0:T(128)S(1)}, bf16[1024,1024]{1,0:T(8,128)(2,1)}) %tuple.31, (bf16[3,256,2,1024]{3,2,1,0:T(2,128)(2,1)}, s32[18]{0:T(128)S(1)}, bf16[1024,1024]{1,0:T(8,128)(2,1)}) %tuple.32), branch_computations={%region_0.4_spmd, %region_4.8_spmd} | conditional | flops 6477447168 | bytes 111411912 | solution.py:498
  2.3 2.7 %deal.3 = bf16[8,3,2,8,2,1024]{5,4,3,2,1,0:T(2,128)(2,1)} custom-call(bf16[3,16,2,8,2,1024]{5,4,3,2,1,0:T(2,128)(2,1)} %bitcast.37), custom_call_target="tpu_custom_call" | custom-call | bytes 3145728 | tf_op jit(solution)/shard_map/cond/branch_1_fun/deal/pallas_call | solution.py:177
  4.9 4.5 %all-to-all-start.2 = ((bf16[8,3,2,8,2,1024]{5,4,3,2,1,0:T(2,128)(2,1)}), bf16[8,3,2,8,2,1024]{5,4,3,2,1,0:T(2,128)(2,1)S(1)}, u32[]{:S(2)}, u32[]{:S(2)}) async-start(bf16[8,3,2,8,2,1024]{5,4,3,2,1,0:T(2,128)(2,1)} %deal.3), calls=%async_computation.2 | async-start | bytes 3145728 | tf_op jit(solution)/shard_map/cond/branch_1_fun/all_to_all | solution.py:460
  9.4 0.0 copy-start.3
  9.4 3.3 %raw_lanes.3 = (bf16[2,16,8,2,1024]{4,3,2,1,0:T(2,128)(2,1)}, bf16[2,16,8,2,1024]{4,3,2,1,0:T(2,128)(2,1)}) custom-call(s32[18]{0:T(128)S(1)} %get-tuple-element.66.refs_0_, bf16[3,16,2,8,2,1024]{5,4,3,2,1,0:T(2,128)(2,1)} %bitcast.38), custom_call_target="tpu_custom_call" | custom-call | bytes 4194304 | tf_op jit(solution)/shard_map/cond/branch_1_fun/raw_lanes/pallas_call | solution.py:224
  12.7 3.4 %collective-permute-start.4 = (bf16[2,16,8,2,1024]{4,3,2,1,0:T(2,128)(2,1)}, bf16[2,16,8,2,1024]{4,3,2,1,0:T(2,128)(2,1)}, u32[]{:S(2)}, u32[]{:S(2)}) collective-permute-start(bf16[2,16,8,2,1024]{4,3,2,1,0:T(2,128)(2,1)} %get-tuple-element.74), channel_id=1, source_target_pairs={{16,32},{32,16},{48,64},{64,48},{80,96},{96,80},{112,128},{128,112... | collective-permute-start | bytes 3145736 | tf_op jit(solution)/shard_map/cond/branch_1_fun/ppermute | solution.py:461
  16.1 5.5 %collective-permute-start.5 = (bf16[2,16,8,2,1024]{4,3,2,1,0:T(2,128)(2,1)}, bf16[2,16,8,2,1024]{4,3,2,1,0:T(2,128)(2,1)}, u32[]{:S(2)}, u32[]{:S(2)}) collective-permute-start(bf16[2,16,8,2,1024]{4,3,2,1,0:T(2,128)(2,1)} %get-tuple-element.75), channel_id=1, source_target_pairs={{0,16},{16,0},{32,48},{48,32},{64,80},{80,64},{96,112},{112,96},{1... | collective-permute-start | bytes 3145736 | tf_op jit(solution)/shard_map/cond/branch_1_fun/ppermute | solution.py:461
  21.5 0.0 copy-done.3
  21.6 4.3 %spectra.6.refs_2_ = bf16[3,256,1024]{2,1,0:T(8,128)(2,1)S(1)} custom-call(bf16[3,16,2,8,2,1024]{5,4,3,2,1,0:T(2,128)(2,1)S(1)} %bitcast.39, bf16[1024,1024]{1,0:T(8,128)(2,1)} %get-tuple-element.72.refs_2_.refs_1_), custom_call_target="tpu_custom_call" | custom-call | flops 1610612736 | bytes 8388608 | tf_op jit(solution)/shard_map/cond/branch_1_fun/spectra/pallas_call | solution.py:258
  25.9 5.1 %all-to-all-done.2.refs_1_ = bf16[8,3,2,8,2,1024]{5,4,3,2,1,0:T(2,128)(2,1)S(1)} async-done(((bf16[8,3,2,8,2,1024]{5,4,3,2,1,0:T(2,128)(2,1)}), bf16[8,3,2,8,2,1024]{5,4,3,2,1,0:T(2,128)(2,1)S(1)}, u32[]{:S(2)}, u32[]{:S(2)}) %all-to-all-start.2) | async-done | bytes 1572896 | tf_op jit(solution)/shard_map/cond/branch_1_fun/all_to_all | solution.py:460
  31.0 0.0 copy-start.5
  31.0 5.1 %dealt_spectra.3 = (bf16[3,256,1024]{2,1,0:T(8,128)(2,1)S(1)}, bf16[2,256,1024]{2,1,0:T(8,128)(2,1)}, bf16[2,256,1024]{2,1,0:T(8,128)(2,1)}) custom-call(s32[18]{0:T(128)S(1)} %get-tuple-element.66.refs_0_, bf16[8,3,2,8,2,1024]{5,4,3,2,1,0:T(2,128)(2,1)S(1)} %all-to-all-done.2.refs_1_, bf16[1024,1024]{1,0:T(8,128)(2,1)} %get-tuple-element.72.refs_2_.refs_1_), custom_call_target="tpu_custom_call" | custom-call | flops 1610612736 | bytes 8388608 | tf_op jit(solution)/shard_map/cond/branch_1_fun/dealt_spectra/pallas_call | solution.py:291
  36.1 0.0 copy-start
  36.1 1.2 %copy-done = bf16[3,256,1024]{2,1,0:T(8,128)(2,1)} copy-done((bf16[3,256,1024]{2,1,0:T(8,128)(2,1)}, bf16[3,256,1024]{2,1,0:T(8,128)(2,1)S(1)}, u32[]{:S(2)}) %copy-start) | copy-done | bytes 1572888 | tf_op jit(solution)/shard_map/cond
  37.3 3.6 %collective-permute-start.6 = (bf16[2,256,1024]{2,1,0:T(8,128)(2,1)}, bf16[2,256,1024]{2,1,0:T(8,128)(2,1)S(1)}, u32[]{:S(2)}, u32[]{:S(2)}) collective-permute-start(bf16[2,256,1024]{2,1,0:T(8,128)(2,1)} %get-tuple-element.78), channel_id=1, source_target_pairs={{16,32},{32,16},{48,64},{64,48},{80,96},{96,80},{112,128},{128,112... | collective-permute-start | bytes 3145736 | tf_op jit(solution)/shard_map/cond/branch_1_fun/ppermute | solution.py:464
  40.9 4.0 %collective-permute-start.7 = (bf16[2,256,1024]{2,1,0:T(8,128)(2,1)}, bf16[2,256,1024]{2,1,0:T(8,128)(2,1)}, u32[]{:S(2)}, u32[]{:S(2)}) collective-permute-start(bf16[2,256,1024]{2,1,0:T(8,128)(2,1)} %get-tuple-element.79), channel_id=1, source_target_pairs={{0,16},{16,0},{32,48},{48,32},{64,80},{80,64},{96,112},{112,96},{1... | collective-permute-start | bytes 3145736 | tf_op jit(solution)/shard_map/cond/branch_1_fun/ppermute | solution.py:464
  44.9 0.0 collective-permute-done.4.refs_0_
  44.9 0.0 copy-done.5
  44.9 2.8 %spectra.7.refs_3_ = bf16[2,256,1024]{2,1,0:T(8,128)(2,1)S(1)} custom-call(bf16[2,16,8,2,1024]{4,3,2,1,0:T(2,128)(2,1)} %collective-permute-done.4.refs_0_, bf16[1024,1024]{1,0:T(8,128)(2,1)S(1)} %copy-done.5), custom_call_target="tpu_custom_call" | custom-call | flops 1610612736 | bytes 8388608 | tf_op jit(solution)/shard_map/cond/branch_1_fun/spectra/pallas_call | solution.py:258
  47.7 0.0 collective-permute-done.5.refs_4_
  47.7 5.1 %raw_products.3 = bf16[8,4,16,1024]{3,2,1,0:T(8,128)(2,1)} custom-call(s32[18]{0:T(128)S(1)} %get-tuple-element.66.refs_0_, bf16[1024,1024]{1,0:T(8,128)(2,1)S(1)} %copy-done.5, bf16[3,256,1024]{2,1,0:T(8,128)(2,1)S(1)} %spectra.6.refs_2_, bf16[2,256,1024]{2,1,0:T(8,128)(2,1)S(1)} %spectra.7.refs_3_, bf16[2,16,8,2,1024]{4,3,2,1,0:T(2,128)(2,1)} %collective-permute-done.5.refs_4_), custom_call_target="tpu_custom_call" | custom-call | flops 1610612736 | bytes 8388608 | tf_op jit(solution)/shard_map/cond/branch_1_fun/raw_products/pallas_call | solution.py:366
  52.8 0.0 copy-start.1
  52.8 4.4 %all-to-all-start.3 = ((bf16[8,4,16,1024]{3,2,1,0:T(8,128)(2,1)}), bf16[8,4,16,1024]{3,2,1,0:T(8,128)(2,1)}, u32[]{:S(2)}, u32[]{:S(2)}) async-start(bf16[8,4,16,1024]{3,2,1,0:T(8,128)(2,1)} %raw_products.3), calls=%async_computation.3 | async-start | bytes 2097152 | tf_op jit(solution)/shard_map/cond/branch_1_fun/all_to_all | solution.py:469
  57.2 0.6 slice.11
  58.3 5.8 %collective-permute-done.6.refs_2_ = bf16[2,256,1024]{2,1,0:T(8,128)(2,1)S(1)} collective-permute-done((bf16[2,256,1024]{2,1,0:T(8,128)(2,1)}, bf16[2,256,1024]{2,1,0:T(8,128)(2,1)S(1)}, u32[]{:S(2)}, u32[]{:S(2)}) %collective-permute-start.6) | collective-permute-done | bytes 1048608 | tf_op jit(solution)/shard_map/cond/branch_1_fun/ppermute | solution.py:464
  64.1 4.1 %collective-permute-done.7.refs_3_ = bf16[2,256,1024]{2,1,0:T(8,128)(2,1)} collective-permute-done((bf16[2,256,1024]{2,1,0:T(8,128)(2,1)}, bf16[2,256,1024]{2,1,0:T(8,128)(2,1)}, u32[]{:S(2)}, u32[]{:S(2)}) %collective-permute-start.7) | collective-permute-done | bytes 1048608 | tf_op jit(solution)/shard_map/cond/branch_1_fun/ppermute | solution.py:464
  68.2 0.0 copy-done.1
  68.2 2.2 %dealt_products.3 = f32[2,4,8,1024]{3,2,1,0:T(8,128)S(1)} custom-call(s32[18]{0:T(128)S(1)} %get-tuple-element.66.refs_0_, bf16[3,256,1024]{2,1,0:T(8,128)(2,1)S(1)} %copy-done.1, bf16[2,256,1024]{2,1,0:T(8,128)(2,1)S(1)} %collective-permute-done.6.refs_2_, bf16[2,256,1024]{2,1,0:T(8,128)(2,1)} %collective-permute-done.7.refs_3_), custom_call_target="tpu_custom_call" | custom-call | flops 33554432 | bytes 8388608 | tf_op jit(solution)/shard_map/cond/branch_1_fun/dealt_products/pallas_call | solution.py:435
  70.4 2.8 %all-to-all-done.3 = bf16[8,4,16,1024]{3,2,1,0:T(8,128)(2,1)} async-done(((bf16[8,4,16,1024]{3,2,1,0:T(8,128)(2,1)}), bf16[8,4,16,1024]{3,2,1,0:T(8,128)(2,1)}, u32[]{:S(2)}, u32[]{:S(2)}) %all-to-all-start.3) | async-done | bytes 1048608 | tf_op jit(solution)/shard_map/cond/branch_1_fun/all_to_all | solution.py:469
  73.2 1.4 %convert_reduce_fusion.1 = f32[4,16,1024]{2,1,0:T(8,128)S(1)} fusion(bf16[8,4,16,1024]{3,2,1,0:T(8,128)(2,1)} %all-to-all-done.3), kind=kLoop, calls=%fused_computation.15 | loop fusion | flops 983040 | bytes 1310720 | tf_op jit(solution)/shard_map/cond/branch_1_fun/reduce_sum | solution.py:473
  74.7 20.9 %conditional.1 = (f32[4,16,1024]{2,1,0:T(8,128)S(1)}) conditional(s32[]{:T(128)} %bitcast.11, (bf16[4,16,1024]{2,1,0:T(8,128)(2,1)S(1)}, s32[]{:T(128)}) %tuple.27, (bf16[4,16,1024]{2,1,0:T(8,128)(2,1)S(1)}, s32[]{:T(128)}) %tuple.27), branch_computations={%region_6.6_spmd, %region_7.7_spmd} | conditional | flops 65541 | bytes 786502 | solution.py:491
  74.8 20.9 %all_gather.10 = bf16[4,16,1024]{2,1,0:T(8,128)(2,1)S(1)} all-gather(bf16[2,16,1024]{2,1,0:T(8,128)(2,1)S(1)} %slice.10), channel_id=1, replica_groups={{0,8},{1,9},{2,10},{3,11},{4,12},{5,13},{6,14},{7,15},{16,24},{17,25},{..., dimensions={0}, use_global_device_ids=true | all-gather | bytes 196608 | tf_op jit(solution)/shard_map/cond/branch_1_fun/cond/branch_0_fun/all_gather | solution.py:487
  95.9 0.0 copy-start.6
  95.9 0.7 copy-done.6
  (9 shorter events, 0.1 us)
Async XLA Ops:
  4.9 26.1 %all-to-all-start.2 = ((bf16[8,3,2,8,2,1024]{5,4,3,2,1,0:T(2,128)(2,1)}), bf16[8,3,2,8,2,1024]{5,4,3,2,1,0:T(2,128)(2,1)S(1)}, u32[]{:S(2)}, u32[]{:S(2)}) async-start(bf16[8,3,2,8,2,1024]{5,4,3,2,1,0:T(2,128)(2,1)} %deal.3), calls=%async_computation.2 | async-start | bytes 3145728 | tf_op jit(solution)/shard_map/cond/branch_1_fun/all_to_all | solution.py:460
  9.4 12.1 %copy-start.3 = (bf16[3,256,2,1024]{3,2,1,0:T(2,128)(2,1)S(1)}, bf16[3,256,2,1024]{3,2,1,0:T(2,128)(2,1)}, u32[]{:S(2)}) copy-start(bf16[3,256,2,1024]{3,2,1,0:T(2,128)(2,1)} %get-tuple-element.68) | copy-start | bytes 9437188 | tf_op jit(solution)/shard_map/cond
  12.7 32.2 %collective-permute-start.4 = (bf16[2,16,8,2,1024]{4,3,2,1,0:T(2,128)(2,1)}, bf16[2,16,8,2,1024]{4,3,2,1,0:T(2,128)(2,1)}, u32[]{:S(2)}, u32[]{:S(2)}) collective-permute-start(bf16[2,16,8,2,1024]{4,3,2,1,0:T(2,128)(2,1)} %get-tuple-element.74), channel_id=1, source_target_pairs={{16,32},{32,16},{48,64},{64,48},{80,96},{96,80},{112,128},{128,112... | collective-permute-start | bytes 3145736 | tf_op jit(solution)/shard_map/cond/branch_1_fun/ppermute | solution.py:461
  16.1 31.6 %collective-permute-start.5 = (bf16[2,16,8,2,1024]{4,3,2,1,0:T(2,128)(2,1)}, bf16[2,16,8,2,1024]{4,3,2,1,0:T(2,128)(2,1)}, u32[]{:S(2)}, u32[]{:S(2)}) collective-permute-start(bf16[2,16,8,2,1024]{4,3,2,1,0:T(2,128)(2,1)} %get-tuple-element.75), channel_id=1, source_target_pairs={{0,16},{16,0},{32,48},{48,32},{64,80},{80,64},{96,112},{112,96},{1... | collective-permute-start | bytes 3145736 | tf_op jit(solution)/shard_map/cond/branch_1_fun/ppermute | solution.py:461
  31.0 13.9 %copy-start.5 = (bf16[1024,1024]{1,0:T(8,128)(2,1)S(1)}, bf16[1024,1024]{1,0:T(8,128)(2,1)}, u32[]{:S(2)}) copy-start(bf16[1024,1024]{1,0:T(8,128)(2,1)} %get-tuple-element.72.refs_2_.refs_1_) | copy-start | bytes 6291460 | tf_op jit(solution)/shard_map/cond
  36.1 1.2 %copy-start = (bf16[3,256,1024]{2,1,0:T(8,128)(2,1)}, bf16[3,256,1024]{2,1,0:T(8,128)(2,1)S(1)}, u32[]{:S(2)}) copy-start(bf16[3,256,1024]{2,1,0:T(8,128)(2,1)S(1)} %get-tuple-element.77.refs_1_) | copy-start | bytes 4718596 | tf_op jit(solution)/shard_map/cond
  37.3 26.8 %collective-permute-start.6 = (bf16[2,256,1024]{2,1,0:T(8,128)(2,1)}, bf16[2,256,1024]{2,1,0:T(8,128)(2,1)S(1)}, u32[]{:S(2)}, u32[]{:S(2)}) collective-permute-start(bf16[2,256,1024]{2,1,0:T(8,128)(2,1)} %get-tuple-element.78), channel_id=1, source_target_pairs={{16,32},{32,16},{48,64},{64,48},{80,96},{96,80},{112,128},{128,112... | collective-permute-start | bytes 3145736 | tf_op jit(solution)/shard_map/cond/branch_1_fun/ppermute | solution.py:464
  40.9 27.3 %collective-permute-start.7 = (bf16[2,256,1024]{2,1,0:T(8,128)(2,1)}, bf16[2,256,1024]{2,1,0:T(8,128)(2,1)}, u32[]{:S(2)}, u32[]{:S(2)}) collective-permute-start(bf16[2,256,1024]{2,1,0:T(8,128)(2,1)} %get-tuple-element.79), channel_id=1, source_target_pairs={{0,16},{16,0},{32,48},{48,32},{64,80},{80,64},{96,112},{112,96},{1... | collective-permute-start | bytes 3145736 | tf_op jit(solution)/shard_map/cond/branch_1_fun/ppermute | solution.py:464
  52.8 15.4 %copy-start.1 = (bf16[3,256,1024]{2,1,0:T(8,128)(2,1)S(1)}, bf16[3,256,1024]{2,1,0:T(8,128)(2,1)}, u32[]{:S(2)}) copy-start(bf16[3,256,1024]{2,1,0:T(8,128)(2,1)} %copy-done) | copy-start | bytes 4718596 | tf_op jit(solution)/shard_map/cond
  52.8 20.3 %all-to-all-start.3 = ((bf16[8,4,16,1024]{3,2,1,0:T(8,128)(2,1)}), bf16[8,4,16,1024]{3,2,1,0:T(8,128)(2,1)}, u32[]{:S(2)}, u32[]{:S(2)}) async-start(bf16[8,4,16,1024]{3,2,1,0:T(8,128)(2,1)} %raw_products.3), calls=%async_computation.3 | async-start | bytes 2097152 | tf_op jit(solution)/shard_map/cond/branch_1_fun/all_to_all | solution.py:469
  95.9 0.7 copy-start.6

commit v4 on v3

--- a/solution.py
+++ b/solution.py
@@ -41,7 +41,7 @@
 ]
 
 
-def table_kernel(where, pairs_hbm, owner_hbm, narrow, wide, flag, pairs, owner, rows, sems):
+def fill_tables(where, pairs_hbm, owner_hbm, narrow, wide, flag, pairs, owner, rows, sems):
     copies = [
         pltpu.make_async_copy(pairs_hbm, pairs, sems.at[0]),
         pltpu.make_async_copy(owner_hbm, owner, sems.at[1]),
@@ -104,7 +104,7 @@
             return [jnp.int32(i) for i in range(BLOCKS)]
         n0, n1, n2 = [n > 0 for n in need]
         lowest = jnp.where(n0, 0, jnp.where(n1, 1, jnp.where(n2, 2, 0)))
-        after = jnp.where(n0 & n1, 1, jnp.where(n2 & (n0 | n1), 2, 0))
+        after = jnp.where(n0 & n1, 1, jnp.where(n2 & (n0 | n1), 2, lowest))
         return [lowest.astype(jnp.int32), after.astype(jnp.int32), jnp.int32(0)]
 
     flag[0] = most.astype(jnp.int32)
@@ -125,24 +125,6 @@
             info[USED + slot] = used
 
 
-def tables(where, pairs, owner):
-    table = jax.ShapeDtypeStruct((TABLE,), jnp.int32)
-    return pl.pallas_call(
-        table_kernel,
-        out_shape=(table, table, jax.ShapeDtypeStruct((1,), jnp.int32)),
-        in_specs=[SMEM, HBM, HBM],
-        out_specs=[SMEM] * 3,
-        scratch_shapes=[
-            pltpu.VMEM((2, pairs.shape[0]), jnp.int32),
-            pltpu.VMEM((1, pairs.shape[0]), jnp.int32),
-            pltpu.VMEM((8, 128), jnp.float32),
-            pltpu.SemaphoreType.DMA((2,)),
-        ],
-        compiler_params=ALL_VMEM,
-        name="tables",
-    )(where, pairs.T, owner[None])
-
-
 def whitened(rows, basis):
     spectrum = jnp.dot(rows, basis, preferred_element_type=jnp.float32)
     power_mean = jnp.mean(spectrum * spectrum, axis=-1, keepdims=True)
@@ -150,44 +132,6 @@
 
 
 COST = pl.CostEstimate(flops=2 * 3 * ROWS * LENGTH * LENGTH, bytes_accessed=8 << 20, transcendentals=0)
-
-
-def deal_kernel(x, deal, buf, xsem, dsem):
-    loads = [pltpu.make_async_copy(x.at[block, :, 1], buf.at[block], xsem.at[block]) for block in range(BLOCKS)]
-    stores = [
-        [
-            pltpu.make_async_copy(buf.at[block, z * 8 + peer], deal.at[peer, block, z], dsem.at[peer, block, z])
-            for peer in range(8)
-            for z in range(2)
-        ]
-        for block in range(BLOCKS)
-    ]
-    for copy in loads:
-        copy.start()
-    for load, copies in zip(loads, stores):
-        load.wait()
-        for copy in copies:
-            copy.start()
-    for copies in stores:
-        for copy in copies:
-            copy.wait()
-
-
-def dealing(x):
-    return pl.pallas_call(
-        deal_kernel,
-        out_shape=jax.ShapeDtypeStruct((8, BLOCKS, 2, HALF, 2, LENGTH), jnp.bfloat16),
-        in_specs=[HBM],
-        out_specs=ANY,
-        scratch_shapes=[
-            pltpu.VMEM((BLOCKS, 16, HALF, 2, LENGTH), jnp.bfloat16),
-            pltpu.SemaphoreType.DMA((BLOCKS,)),
-            pltpu.SemaphoreType.DMA((8, BLOCKS, 2)),
-        ],
-        compiler_params=PARAMS,
-        cost_estimate=pl.CostEstimate(flops=0, bytes_accessed=3 << 20, transcendentals=0),
-        name="deal",
-    )(x)
 
 
 def lane_copy(buf, block, lanes, way, spot, lsem):
@@ -235,6 +179,68 @@
         cost_estimate=pl.CostEstimate(flops=0, bytes_accessed=4 << 20, transcendentals=0),
         name="raw_lanes",
     )(info, x)
+
+
+def prepare_kernel(where, pairs, owner, x, narrow, wide, flag, deal, one, two, *scratch):
+    small, (buf, xsem, dsem, lsem) = scratch[:4], scratch[4:]
+    loads = [
+        [pltpu.make_async_copy(x.at[block, :, chunk], buf.at[chunk, block], xsem.at[chunk, block]) for block in range(BLOCKS)]
+        for chunk in range(CHUNKS)
+    ]
+    for copies in reversed(loads):
+        for copy in copies:
+            copy.start()
+    fill_tables(where, pairs, owner, narrow, wide, flag, *small)
+    deals = [
+        [
+            pltpu.make_async_copy(buf.at[1, block, z * 8 + peer], deal.at[peer, block, z], dsem.at[peer, block, z])
+            for peer in range(8)
+            for z in range(2)
+        ]
+        for block in range(BLOCKS)
+    ]
+    for block in range(BLOCKS):
+        loads[1][block].wait()
+        for copy in deals[block]:
+            copy.start()
+    for block in range(BLOCKS):
+        loads[0][block].wait()
+        start_lanes(2, narrow, buf.at[0], block, (one, two), lsem)
+    for copies in deals:
+        for copy in copies:
+            copy.wait()
+    wait_lanes(2, buf.at[0], (one, two), lsem)
+
+
+def prepare(where, pairs, owner, x):
+    table = jax.ShapeDtypeStruct((TABLE,), jnp.int32)
+    lane = jax.ShapeDtypeStruct((2, 16, HALF, 2, LENGTH), jnp.bfloat16)
+    return pl.pallas_call(
+        prepare_kernel,
+        out_shape=(
+            table,
+            table,
+            jax.ShapeDtypeStruct((1,), jnp.int32),
+            jax.ShapeDtypeStruct((8, BLOCKS, 2, HALF, 2, LENGTH), jnp.bfloat16),
+            lane,
+            lane,
+        ),
+        in_specs=[SMEM, HBM, HBM, HBM],
+        out_specs=[SMEM] * 3 + [ANY] * 3,
+        scratch_shapes=[
+            pltpu.VMEM((2, pairs.shape[0]), jnp.int32),
+            pltpu.VMEM((1, pairs.shape[0]), jnp.int32),
+            pltpu.VMEM((8, 128), jnp.float32),
+            pltpu.SemaphoreType.DMA((2,)),
+            pltpu.VMEM((CHUNKS, BLOCKS, 16, HALF, 2, LENGTH), jnp.bfloat16),
+            pltpu.SemaphoreType.DMA((CHUNKS, BLOCKS)),
+            pltpu.SemaphoreType.DMA((8, BLOCKS, 2)),
+            pltpu.SemaphoreType.DMA((2, 2)),
+        ],
+        compiler_params=ALL_VMEM,
+        cost_estimate=pl.CostEstimate(flops=0, bytes_accessed=7 << 20, transcendentals=0),
+        name="prepare",
+    )(where, pairs.T, owner[None], x)
 
 
 def spectra_kernel(count, at, x, basis, own, xbuf, spec, xsem, osem):
@@ -272,36 +278,53 @@
     )(x, basis)
 
 
-def dealt_kernel(width, info, x, basis, own, one, two, spec, osem, lsem):
-    def store(block):
-        return pltpu.make_async_copy(spec.at[block], own.at[block], osem.at[block])
-
+def dealt_kernel(width, info, x, basis, one, two, spec, lsem):
     for block in range(BLOCKS):
-        spec[block] = whitened(x[:, block].reshape(ROWS, LENGTH), basis[...])
-        start_lanes(width, info, spec, block, (one, two), lsem)
-        store(block).start()
+        picks = [info[LANES + way * 3 + spot] == block for way in range(2) for spot in range(width)]
+        wanted = picks[0]
+        for pick in picks[1:]:
+            wanted = wanted | pick
+
+        @pl.when(wanted)
+        def _(block=block):
+            spec[block] = whitened(x[:, block].reshape(ROWS, LENGTH), basis[...])
+            start_lanes(width, info, spec, block, (one, two), lsem)
+
     wait_lanes(width, spec, (one, two), lsem)
-    for block in range(BLOCKS):
-        store(block).wait()
-
-
-def dealt_spectra(width, info, x, basis):
-    own = jax.ShapeDtypeStruct((BLOCKS, ROWS, LENGTH), jnp.bfloat16)
+
+
+def dealt_lanes(width, info, x, basis):
     lane = jax.ShapeDtypeStruct((width, ROWS, LENGTH), jnp.bfloat16)
     return pl.pallas_call(
         lambda *refs: dealt_kernel(width, *refs),
-        out_shape=(own, lane, lane),
+        out_shape=(lane, lane),
         in_specs=[SMEM, VMEM, VMEM],
-        out_specs=[HBM] * 3,
+        out_specs=[HBM] * 2,
         scratch_shapes=[
             pltpu.VMEM((BLOCKS, ROWS, LENGTH), jnp.bfloat16),
-            pltpu.SemaphoreType.DMA((BLOCKS,)),
             pltpu.SemaphoreType.DMA((2, width)),
         ],
         compiler_params=PARAMS,
         cost_estimate=COST,
+        name="dealt_lanes",
+    )(info, x, basis)
+
+
+def dealt_own_kernel(x, basis, own):
+    for block in range(BLOCKS):
+        own[block] = whitened(x[:, block].reshape(ROWS, LENGTH), basis[...])
+
+
+def dealt_spectra(x, basis):
+    return pl.pallas_call(
+        dealt_own_kernel,
+        out_shape=jax.ShapeDtypeStruct((BLOCKS, ROWS, LENGTH), jnp.bfloat16),
+        in_specs=[VMEM, VMEM],
+        out_specs=VMEM,
+        compiler_params=PARAMS,
+        cost_estimate=COST,
         name="dealt_spectra",
-    )(info, x, basis)
+    )(x, basis)
 
 
 def parts(read, at, lane):
@@ -448,18 +471,18 @@
     )(info, own, one, two)
 
 
-def path(records, info, width):
+def path(records, info, deal, raw, width):
     far = lax.axis_index("win") // 8
     basis = jnp.asarray(basis_table())
     x = records.reshape(BLOCKS, 16, CHUNKS, HALF, 2, LENGTH)
     chip_groups = [[z * 8 + j for j in range(8)] for z in range(2)]
     far_groups = [[z * 8 + j for z in range(2)] for j in range(8)]
 
-    deal = dealing(x)
-    x, deal = lax.optimization_barrier((x, deal))
     dealt = lax.all_to_all(deal, "win", 0, 0, tiled=True, axis_index_groups=chip_groups)
-    raw_one, raw_two = [lax.ppermute(lane, "chan", swap) for lane, swap in zip(raw_lanes(width, info, x), SWAPS)]
-    dealt_own, *sent = dealt_spectra(width, info, dealt, basis)
+    if raw is None:
+        raw = raw_lanes(width, info, x)
+    raw_one, raw_two = [lax.ppermute(lane, "chan", swap) for lane, swap in zip(raw, SWAPS)]
+    sent = dealt_lanes(width, info, dealt, basis)
     raw_basis, *sent = lax.optimization_barrier((basis, *sent))
     came = [lax.ppermute(lane, "chan", swap) for lane, swap in zip(sent, SWAPS)]
     own = spectra(BLOCKS, lambda block: (block, slice(None), 0), x, basis)
@@ -467,8 +490,8 @@
 
     part = raw_products(width, info, raw_basis, own, one, raw_two)
     first = lax.all_to_all(part, "win", 0, 0, tiled=True, axis_index_groups=chip_groups)
-    dealt_own, part = lax.optimization_barrier((dealt_own, part))
-    second = dealt_products(width, info, dealt_own, *came)
+    dealt, part = lax.optimization_barrier((dealt, part))
+    second = dealt_products(width, info, dealt_spectra(dealt, basis), *came)
     first, second = lax.optimization_barrier((first, second))
     first = jnp.sum(first.astype(jnp.float32), axis=0).reshape(PCAP, 2, HALF, LENGTH)
 
@@ -494,11 +517,12 @@
 
 def local(records, pairs, owner):
     where = lax.axis_index("chan")[None].astype(jnp.int32)
-    narrow, wide, three = tables(where, pairs, owner)
+    x = records.reshape(BLOCKS, 16, CHUNKS, HALF, 2, LENGTH)
+    narrow, wide, three, deal, *raw = prepare(where, pairs, owner, x)
     return lax.cond(
         three.reshape(()) == 0,
-        lambda: path(records, narrow, 2),
-        lambda: path(records, wide, BLOCKS),
+        lambda: path(records, narrow, deal, raw, 2),
+        lambda: path(records, wide, deal, None, BLOCKS),
     )
 
 

time: 97.2 us -> 94.3 us (0.970)
  the two profiles are of different devices: /device:TPU:2 before, /device:TPU:100 now
where the time goes in v4:
time: 94.3 us; the launch traced here: 93.8 us
  Pallas kernels  29.3 us (31%)
  starting transfers between devices  25 us (27%)
  blocking collectives  19.6 us (21%)
  waiting for transfers between devices  16.6 us (18%)
  local copies, waits for them, and re-layouts  1.42 us (2%)
  loops' own time  1.1 us (1%)
    all_gather x1, blocking collectives, swapped(): lax.all_gather(give[:slots], 'win', axis=0, tiled=True, axis_index_groups...  19.6 us
    ppermute x2, starting transfers between devices, path(): came = [lax.ppermute(lane, 'chan', swap) for lane, swap in zip(sent, SWAPS)]  8.87 us
    all_to_all x1, waiting for transfers between devices, path(): lax.all_to_all(deal, 'win', 0, 0, tiled=True, axis_index_groups=chip_groups)  8.27 us
    ppermute x2, starting transfers between devices, path(): lax.ppermute(lane, 'chan', swap)  8.05 us
    pallas_call x2, Pallas kernels, spectra(): pl.pallas_call(lambda *refs: spectra_kernel(count, at, *refs), out_shape=...  8.02 us
    ppermute x2, waiting for transfers between devices, path(): came = [lax.ppermute(lane, 'chan', swap) for lane, swap in zip(sent, SWAPS)]  6.12 us
    pallas_call x1, Pallas kernels, raw_products(): pl.pallas_call(lambda *refs: raw_products_kernel(width, *refs), out_shape...  5.67 us
    pallas_call x1, Pallas kernels, prepare(): pl.pallas_call(prepare_kernel, out_shape=(table, table, jax.ShapeDtypeStr...  4.93 us
  transfers between devices with their start and end apart: 6, of which 4 were waited for; matrix products, arithmetic and copies ran while one was open for 1% of the time, Pallas kernels for 26%

profile of v4, /device:TPU:100, one launch (start us, length us, event | category | flops | bytes accessed | tf_op | source)
XLA Modules:
  0.0 93.8 jit_solution(17415187690961641558)
XLA Ops:
  0.0 4.9 %prepare.1 = (s32[18]{0:T(128)S(1)}, s32[18]{0:T(128)S(1)}, s32[1]{0:T(128)}, bf16[8,3,2,8,2,1024]{5,4,3,2,1,0:T(2,128)(2,1)}, bf16[2,16,8,2,1024]{4,3,2,1,0:T(2...) custom-call(s32[1]{0:T(128)} %bitcast.14.where, s32[2,80]{1,0:T(2,128)} %bitcast.43, s32[1,80]{1,0:T(1,128)} %bitcast.44, ...), custom_call_target="tpu_custom_call" | custom-call | bytes 7340032 | tf_op jit(solution)/shard_map/prepare/pallas_call | solution.py:218
  5.6 87.5 %conditional.3 = (f32[4,16,1024]{2,1,0:T(8,128)S(1)}) conditional(s32[]{:T(128)} %bitcast.18, (bf16[8,3,2,8,2,1024]{5,4,3,2,1,0:T(2,128)(2,1)}, s32[18]{0:T(128)S(1)}, bf16[1024,1024]{1,0:T(8,128)(2,1)}, bf16[3,256,2,1024]{3,2,1,0:T(2,128)(2,1)}) %tuple.29, (bf16[8,3,2,8,2,1024]{5,4,3,2,1,0:T(2,128)(2,1)}, s32[18]{0:T(128)S(1)}, ...), branch_computations={%region_0.4_spmd, %region_4.8_spmd} | conditional | flops 8088059904 | bytes 125043400 | solution.py:522
  5.8 4.5 %all-to-all-start.2 = ((bf16[8,3,2,8,2,1024]{5,4,3,2,1,0:T(2,128)(2,1)}), bf16[8,3,2,8,2,1024]{5,4,3,2,1,0:T(2,128)(2,1)S(1)}, u32[]{:S(2)}, u32[]{:S(2)}) async-start(bf16[8,3,2,8,2,1024]{5,4,3,2,1,0:T(2,128)(2,1)} %get-tuple-element.74), calls=%async_computation.2 | async-start | bytes 3145728 | tf_op jit(solution)/shard_map/cond/branch_1_fun/all_to_all | solution.py:481
  10.3 2.4 %collective-permute-start.4 = (bf16[2,16,8,2,1024]{4,3,2,1,0:T(2,128)(2,1)}, bf16[2,16,8,2,1024]{4,3,2,1,0:T(2,128)(2,1)}, u32[]{:S(2)}, u32[]{:S(2)}) collective-permute-start(bf16[2,16,8,2,1024]{4,3,2,1,0:T(2,128)(2,1)} %get-tuple-element.79), channel_id=1, source_target_pairs={{16,32},{32,16},{48,64},{64,48},{80,96},{96,80},{112,128},{128,112... | collective-permute-start | bytes 3145736 | tf_op jit(solution)/shard_map/cond/branch_1_fun/ppermute | solution.py:484
  12.7 5.6 %collective-permute-start.5 = (bf16[2,16,8,2,1024]{4,3,2,1,0:T(2,128)(2,1)}, bf16[2,16,8,2,1024]{4,3,2,1,0:T(2,128)(2,1)}, u32[]{:S(2)}, u32[]{:S(2)}) collective-permute-start(bf16[2,16,8,2,1024]{4,3,2,1,0:T(2,128)(2,1)} %get-tuple-element.80), channel_id=1, source_target_pairs={{0,16},{16,0},{32,48},{48,32},{64,80},{80,64},{96,112},{112,96},{1... | collective-permute-start | bytes 3145736 | tf_op jit(solution)/shard_map/cond/branch_1_fun/ppermute | solution.py:484
  18.4 5.2 %spectra.6.refs_2_ = bf16[3,256,1024]{2,1,0:T(8,128)(2,1)S(1)} custom-call(bf16[3,16,2,8,2,1024]{5,4,3,2,1,0:T(2,128)(2,1)} %bitcast.38, bf16[1024,1024]{1,0:T(8,128)(2,1)} %get-tuple-element.77.refs_2_.refs_1_.basis), custom_call_target="tpu_custom_call" | custom-call | flops 1610612736 | bytes 8388608 | tf_op jit(solution)/shard_map/cond/branch_1_fun/spectra/pallas_call | solution.py:264
  23.6 8.3 %all-to-all-done.2.refs_1_.x = bf16[8,3,2,8,2,1024]{5,4,3,2,1,0:T(2,128)(2,1)S(1)} async-done(((bf16[8,3,2,8,2,1024]{5,4,3,2,1,0:T(2,128)(2,1)}), bf16[8,3,2,8,2,1024]{5,4,3,2,1,0:T(2,128)(2,1)S(1)}, u32[]{:S(2)}, u32[]{:S(2)}) %all-to-all-start.2) | async-done | bytes 1572896 | tf_op jit(solution)/shard_map/cond/branch_1_fun/all_to_all | solution.py:481
  31.9 0.0 copy-start.4
  31.9 4.4 %dealt_lanes.3 = (bf16[2,256,1024]{2,1,0:T(8,128)(2,1)}, bf16[2,256,1024]{2,1,0:T(8,128)(2,1)}) custom-call(s32[18]{0:T(128)S(1)} %get-tuple-element.72.refs_0_, bf16[8,3,2,8,2,1024]{5,4,3,2,1,0:T(2,128)(2,1)S(1)} %all-to-all-done.2.refs_1_.x, bf16[1024,1024]{1,0:T(8,128)(2,1)} %get-tuple-element.77.refs_2_.refs_1_.basis), custom_call_target="tpu_custom_call" | custom-call | flops 1610612736 | bytes 8388608 | tf_op jit(solution)/shard_map/cond/branch_1_fun/dealt_lanes/pallas_call | solution.py:298
  36.3 3.3 %collective-permute-start.6 = (bf16[2,256,1024]{2,1,0:T(8,128)(2,1)}, bf16[2,256,1024]{2,1,0:T(8,128)(2,1)}, u32[]{:S(2)}, u32[]{:S(2)}) collective-permute-start(bf16[2,256,1024]{2,1,0:T(8,128)(2,1)} %get-tuple-element.82), channel_id=1, source_target_pairs={{16,32},{32,16},{48,64},{64,48},{80,96},{96,80},{112,128},{128,112... | collective-permute-start | bytes 3145736 | tf_op jit(solution)/shard_map/cond/branch_1_fun/ppermute | solution.py:487
  39.6 5.6 %collective-permute-start.7 = (bf16[2,256,1024]{2,1,0:T(8,128)(2,1)}, bf16[2,256,1024]{2,1,0:T(8,128)(2,1)}, u32[]{:S(2)}, u32[]{:S(2)}) collective-permute-start(bf16[2,256,1024]{2,1,0:T(8,128)(2,1)} %get-tuple-element.83), channel_id=1, source_target_pairs={{0,16},{16,0},{32,48},{48,32},{64,80},{80,64},{96,112},{112,96},{1... | collective-permute-start | bytes 3145736 | tf_op jit(solution)/shard_map/cond/branch_1_fun/ppermute | solution.py:487
  45.2 0.0 collective-permute-done.4.refs_0_
  45.2 0.0 copy-done.4
  45.2 2.8 %spectra.7.refs_3_ = bf16[2,256,1024]{2,1,0:T(8,128)(2,1)S(1)} custom-call(bf16[2,16,8,2,1024]{4,3,2,1,0:T(2,128)(2,1)} %collective-permute-done.4.refs_0_, bf16[1024,1024]{1,0:T(8,128)(2,1)S(1)} %copy-done.4), custom_call_target="tpu_custom_call" | custom-call | flops 1610612736 | bytes 8388608 | tf_op jit(solution)/shard_map/cond/branch_1_fun/spectra/pallas_call | solution.py:264
  48.0 0.0 collective-permute-done.5.refs_4_
  48.0 5.7 %raw_products.3 = bf16[8,4,16,1024]{3,2,1,0:T(8,128)(2,1)} custom-call(s32[18]{0:T(128)S(1)} %get-tuple-element.72.refs_0_, bf16[1024,1024]{1,0:T(8,128)(2,1)S(1)} %copy-done.4, bf16[3,256,1024]{2,1,0:T(8,128)(2,1)S(1)} %spectra.6.refs_2_, bf16[2,256,1024]{2,1,0:T(8,128)(2,1)S(1)} %spectra.7.refs_3_, bf16[2,16,8,2,1024]{4,3,2,1,0:T(2,128)(2,1)} %collective-permute-done.5.refs_4_), custom_call_target="tpu_custom_call" | custom-call | flops 1610612736 | bytes 8388608 | tf_op jit(solution)/shard_map/cond/branch_1_fun/raw_products/pallas_call | solution.py:389
  53.7 3.6 %all-to-all-start.3 = ((bf16[8,4,16,1024]{3,2,1,0:T(8,128)(2,1)}), bf16[8,4,16,1024]{3,2,1,0:T(8,128)(2,1)S(1)}, u32[]{:S(2)}, u32[]{:S(2)}) async-start(bf16[8,4,16,1024]{3,2,1,0:T(8,128)(2,1)} %raw_products.3), calls=%async_computation.3 | async-start | bytes 2097152 | tf_op jit(solution)/shard_map/cond/branch_1_fun/all_to_all | solution.py:492
  57.3 0.7 slice.11
  58.6 3.5 %dealt_spectra.3.refs_1_ = bf16[3,256,1024]{2,1,0:T(8,128)(2,1)S(1)} custom-call(bf16[8,3,2,8,2,1024]{5,4,3,2,1,0:T(2,128)(2,1)S(1)} %all-to-all-done.2.refs_1_.x, bf16[1024,1024]{1,0:T(8,128)(2,1)} %get-tuple-element.77.refs_2_.refs_1_.basis), custom_call_target="tpu_custom_call" | custom-call | flops 1610612736 | bytes 8388608 | tf_op jit(solution)/shard_map/cond/branch_1_fun/dealt_spectra/pallas_call | solution.py:319
  62.2 1.0 %collective-permute-done.6.refs_2_ = bf16[2,256,1024]{2,1,0:T(8,128)(2,1)} collective-permute-done((bf16[2,256,1024]{2,1,0:T(8,128)(2,1)}, bf16[2,256,1024]{2,1,0:T(8,128)(2,1)}, u32[]{:S(2)}, u32[]{:S(2)}) %collective-permute-start.6) | collective-permute-done | bytes 1048608 | tf_op jit(solution)/shard_map/cond/branch_1_fun/ppermute | solution.py:487
  63.2 5.1 %collective-permute-done.7.refs_3_ = bf16[2,256,1024]{2,1,0:T(8,128)(2,1)} collective-permute-done((bf16[2,256,1024]{2,1,0:T(8,128)(2,1)}, bf16[2,256,1024]{2,1,0:T(8,128)(2,1)}, u32[]{:S(2)}, u32[]{:S(2)}) %collective-permute-start.7) | collective-permute-done | bytes 1048608 | tf_op jit(solution)/shard_map/cond/branch_1_fun/ppermute | solution.py:487
  68.3 2.7 %dealt_products.3 = f32[2,4,8,1024]{3,2,1,0:T(8,128)S(1)} custom-call(s32[18]{0:T(128)S(1)} %get-tuple-element.72.refs_0_, bf16[3,256,1024]{2,1,0:T(8,128)(2,1)S(1)} %dealt_spectra.3.refs_1_, bf16[2,256,1024]{2,1,0:T(8,128)(2,1)} %collective-permute-done.6.refs_2_, bf16[2,256,1024]{2,1,0:T(8,128)(2,1)} %collective-permute-done.7.refs_3_), custom_call_target="tpu_custom_call" | custom-call | flops 33554432 | bytes 8388608 | tf_op jit(solution)/shard_map/cond/branch_1_fun/dealt_products/pallas_call | solution.py:458
  71.0 2.2 %all-to-all-done.3 = bf16[8,4,16,1024]{3,2,1,0:T(8,128)(2,1)S(1)} async-done(((bf16[8,4,16,1024]{3,2,1,0:T(8,128)(2,1)}), bf16[8,4,16,1024]{3,2,1,0:T(8,128)(2,1)S(1)}, u32[]{:S(2)}, u32[]{:S(2)}) %all-to-all-start.3) | async-done | bytes 1048608 | tf_op jit(solution)/shard_map/cond/branch_1_fun/all_to_all | solution.py:492
  73.1 0.2 convert_reduce_fusion.1
  73.4 19.6 %conditional.1 = (f32[4,16,1024]{2,1,0:T(8,128)S(1)}) conditional(s32[]{:T(128)} %bitcast.11, (bf16[4,16,1024]{2,1,0:T(8,128)(2,1)S(1)}, s32[]{:T(128)}) %tuple.25, (bf16[4,16,1024]{2,1,0:T(8,128)(2,1)S(1)}, s32[]{:T(128)}) %tuple.25), branch_computations={%region_6.6_spmd, %region_7.7_spmd} | conditional | flops 65541 | bytes 786502 | solution.py:514
  73.5 19.6 %all_gather.11 = bf16[8,16,1024]{2,1,0:T(8,128)(2,1)S(1)} all-gather(bf16[4,16,1024]{2,1,0:T(8,128)(2,1)S(1)} %get-tuple-element.70), channel_id=1, replica_groups={{0,8},{1,9},{2,10},{3,11},{4,12},{5,13},{6,14},{7,15},{16,24},{17,25},{..., dimensions={0}, use_global_device_ids=true | all-gather | bytes 393216 | tf_op jit(solution)/shard_map/cond/branch_1_fun/cond/branch_1_fun/all_gather | solution.py:510
  93.1 0.0 copy-start.5
  93.1 0.7 copy-done.5
  (7 shorter events, 0.1 us)
Async XLA Ops:
  5.8 26.1 %all-to-all-start.2 = ((bf16[8,3,2,8,2,1024]{5,4,3,2,1,0:T(2,128)(2,1)}), bf16[8,3,2,8,2,1024]{5,4,3,2,1,0:T(2,128)(2,1)S(1)}, u32[]{:S(2)}, u32[]{:S(2)}) async-start(bf16[8,3,2,8,2,1024]{5,4,3,2,1,0:T(2,128)(2,1)} %get-tuple-element.74), calls=%async_computation.2 | async-start | bytes 3145728 | tf_op jit(solution)/shard_map/cond/branch_1_fun/all_to_all | solution.py:481
  10.3 34.9 %collective-permute-start.4 = (bf16[2,16,8,2,1024]{4,3,2,1,0:T(2,128)(2,1)}, bf16[2,16,8,2,1024]{4,3,2,1,0:T(2,128)(2,1)}, u32[]{:S(2)}, u32[]{:S(2)}) collective-permute-start(bf16[2,16,8,2,1024]{4,3,2,1,0:T(2,128)(2,1)} %get-tuple-element.79), channel_id=1, source_target_pairs={{16,32},{32,16},{48,64},{64,48},{80,96},{96,80},{112,128},{128,112... | collective-permute-start | bytes 3145736 | tf_op jit(solution)/shard_map/cond/branch_1_fun/ppermute | solution.py:484
  12.7 35.3 %collective-permute-start.5 = (bf16[2,16,8,2,1024]{4,3,2,1,0:T(2,128)(2,1)}, bf16[2,16,8,2,1024]{4,3,2,1,0:T(2,128)(2,1)}, u32[]{:S(2)}, u32[]{:S(2)}) collective-permute-start(bf16[2,16,8,2,1024]{4,3,2,1,0:T(2,128)(2,1)} %get-tuple-element.80), channel_id=1, source_target_pairs={{0,16},{16,0},{32,48},{48,32},{64,80},{80,64},{96,112},{112,96},{1... | collective-permute-start | bytes 3145736 | tf_op jit(solution)/shard_map/cond/branch_1_fun/ppermute | solution.py:484
  31.9 13.3 %copy-start.4 = (bf16[1024,1024]{1,0:T(8,128)(2,1)S(1)}, bf16[1024,1024]{1,0:T(8,128)(2,1)}, u32[]{:S(2)}) copy-start(bf16[1024,1024]{1,0:T(8,128)(2,1)} %get-tuple-element.77.refs_2_.refs_1_.basis) | copy-start | bytes 6291460 | tf_op jit(solution)/shard_map/cond
  36.3 26.9 %collective-permute-start.6 = (bf16[2,256,1024]{2,1,0:T(8,128)(2,1)}, bf16[2,256,1024]{2,1,0:T(8,128)(2,1)}, u32[]{:S(2)}, u32[]{:S(2)}) collective-permute-start(bf16[2,256,1024]{2,1,0:T(8,128)(2,1)} %get-tuple-element.82), channel_id=1, source_target_pairs={{16,32},{32,16},{48,64},{64,48},{80,96},{96,80},{112,128},{128,112... | collective-permute-start | bytes 3145736 | tf_op jit(solution)/shard_map/cond/branch_1_fun/ppermute | solution.py:487
  39.6 28.7 %collective-permute-start.7 = (bf16[2,256,1024]{2,1,0:T(8,128)(2,1)}, bf16[2,256,1024]{2,1,0:T(8,128)(2,1)}, u32[]{:S(2)}, u32[]{:S(2)}) collective-permute-start(bf16[2,256,1024]{2,1,0:T(8,128)(2,1)} %get-tuple-element.83), channel_id=1, source_target_pairs={{0,16},{16,0},{32,48},{48,32},{64,80},{80,64},{96,112},{112,96},{1... | collective-permute-start | bytes 3145736 | tf_op jit(solution)/shard_map/cond/branch_1_fun/ppermute | solution.py:487
  53.7 19.5 %all-to-all-start.3 = ((bf16[8,4,16,1024]{3,2,1,0:T(8,128)(2,1)}), bf16[8,4,16,1024]{3,2,1,0:T(8,128)(2,1)S(1)}, u32[]{:S(2)}, u32[]{:S(2)}) async-start(bf16[8,4,16,1024]{3,2,1,0:T(8,128)(2,1)} %raw_products.3), calls=%async_computation.3 | async-start | bytes 2097152 | tf_op jit(solution)/shard_map/cond/branch_1_fun/all_to_all | solution.py:492
  93.1 0.7 copy-start.5

commit v5 on v4

--- a/solution.py
+++ b/solution.py
@@ -41,18 +41,10 @@
 ]
 
 
-def fill_tables(where, pairs_hbm, owner_hbm, narrow, wide, flag, pairs, owner, rows, sems):
-    copies = [
-        pltpu.make_async_copy(pairs_hbm, pairs, sems.at[0]),
-        pltpu.make_async_copy(owner_hbm, owner, sems.at[1]),
-    ]
-    for copy in copies:
-        copy.start()
+def fill_tables(where, pairs, owner, narrow, wide, flag, rows):
     odd = where[0] % 2
     me = where[0].astype(jnp.float32)
     count = owner.shape[1]
-    for copy in copies:
-        copy.wait()
     rows[...] = jnp.full(rows.shape, -1000.0, jnp.float32)
     rows[0:2, 0:count] = pairs[...].astype(jnp.float32)
     rows[2:3, 0:count] = owner[...].astype(jnp.float32)
@@ -182,7 +174,13 @@
 
 
 def prepare_kernel(where, pairs, owner, x, narrow, wide, flag, deal, one, two, *scratch):
-    small, (buf, xsem, dsem, lsem) = scratch[:4], scratch[4:]
+    pairs_here, owner_here, rows, psem, buf, xsem, dsem, lsem = scratch
+    small = [
+        pltpu.make_async_copy(pairs, pairs_here, psem.at[0]),
+        pltpu.make_async_copy(owner, owner_here, psem.at[1]),
+    ]
+    for copy in small:
+        copy.start()
     loads = [
         [pltpu.make_async_copy(x.at[block, :, chunk], buf.at[chunk, block], xsem.at[chunk, block]) for block in range(BLOCKS)]
         for chunk in range(CHUNKS)
@@ -190,11 +188,9 @@
     for copies in reversed(loads):
         for copy in copies:
             copy.start()
-    fill_tables(where, pairs, owner, narrow, wide, flag, *small)
     deals = [
         [
-            pltpu.make_async_copy(buf.at[1, block, z * 8 + peer], deal.at[peer, block, z], dsem.at[peer, block, z])
-            for peer in range(8)
+            pltpu.make_async_copy(buf.at[1, block, pl.ds(z * 8, 8)], deal.at[:, block, z], dsem.at[block, z])
             for z in range(2)
         ]
         for block in range(BLOCKS)
@@ -203,6 +199,9 @@
         loads[1][block].wait()
         for copy in deals[block]:
             copy.start()
+    for copy in small:
+        copy.wait()
+    fill_tables(where, pairs_here, owner_here, narrow, wide, flag, rows)
     for block in range(BLOCKS):
         loads[0][block].wait()
         start_lanes(2, narrow, buf.at[0], block, (one, two), lsem)
@@ -234,7 +233,7 @@
             pltpu.SemaphoreType.DMA((2,)),
             pltpu.VMEM((CHUNKS, BLOCKS, 16, HALF, 2, LENGTH), jnp.bfloat16),
             pltpu.SemaphoreType.DMA((CHUNKS, BLOCKS)),
-            pltpu.SemaphoreType.DMA((8, BLOCKS, 2)),
+            pltpu.SemaphoreType.DMA((BLOCKS, 2)),
             pltpu.SemaphoreType.DMA((2, 2)),
         ],
         compiler_params=ALL_VMEM,
@@ -243,7 +242,14 @@
     )(where, pairs.T, owner[None], x)
 
 
-def spectra_kernel(count, at, x, basis, own, xbuf, spec, xsem, osem):
+def taken(info, spot):
+    hits = [
+        (info[USED + slot] > 0) & ((info[FIRST + slot] == spot) | (info[SECOND + slot] == spot)) for slot in range(PCAP)
+    ]
+    return hits[0] | hits[1] | hits[2] | hits[3]
+
+
+def spectra_kernel(count, base, at, info, x, basis, own, xbuf, spec, xsem, osem):
     def load(block):
         return pltpu.make_async_copy(x.at[at(block)], xbuf.at[block], xsem.at[block])
 
@@ -254,17 +260,21 @@
         load(block).start()
     for block in range(count):
         load(block).wait()
-        spec[block] = whitened(xbuf[block].reshape(ROWS, LENGTH), basis[...])
+
+        @pl.when(taken(info, base + block))
+        def _(block=block):
+            spec[block] = whitened(xbuf[block].reshape(ROWS, LENGTH), basis[...])
+
         store(block).start()
     for block in range(count):
         store(block).wait()
 
 
-def spectra(count, at, x, basis):
-    return pl.pallas_call(
-        lambda *refs: spectra_kernel(count, at, *refs),
+def spectra(count, base, at, info, x, basis):
+    return pl.pallas_call(
+        lambda *refs: spectra_kernel(count, base, at, *refs),
         out_shape=jax.ShapeDtypeStruct((count, ROWS, LENGTH), jnp.bfloat16),
-        in_specs=[HBM, VMEM],
+        in_specs=[SMEM, HBM, VMEM],
         out_specs=ANY,
         scratch_shapes=[
             pltpu.VMEM((count, 16, HALF, 2, LENGTH), jnp.bfloat16),
@@ -275,7 +285,7 @@
         compiler_params=PARAMS,
         cost_estimate=COST,
         name="spectra",
-    )(x, basis)
+    )(info, x, basis)
 
 
 def dealt_kernel(width, info, x, basis, one, two, spec, lsem):
@@ -354,7 +364,11 @@
         copy.start()
     for spot, copy in enumerate(loads):
         copy.wait()
-        buf[BLOCKS + width + spot] = whitened(xbuf[spot].reshape(ROWS, LENGTH), basis[...])
+
+        @pl.when(taken(info, BLOCKS + width + spot))
+        def _(spot=spot):
+            buf[BLOCKS + width + spot] = whitened(xbuf[spot].reshape(ROWS, LENGTH), basis[...])
+
     for copy in ready:
         copy.wait()
 
@@ -485,8 +499,8 @@
     sent = dealt_lanes(width, info, dealt, basis)
     raw_basis, *sent = lax.optimization_barrier((basis, *sent))
     came = [lax.ppermute(lane, "chan", swap) for lane, swap in zip(sent, SWAPS)]
-    own = spectra(BLOCKS, lambda block: (block, slice(None), 0), x, basis)
-    one = spectra(width, lambda spot: (spot,), raw_one, raw_basis)
+    own = spectra(BLOCKS, 0, lambda block: (block, slice(None), 0), info, x, basis)
+    one = spectra(width, BLOCKS, lambda spot: (spot,), info, raw_one, raw_basis)
 
     part = raw_products(width, info, raw_basis, own, one, raw_two)
     first = lax.all_to_all(part, "win", 0, 0, tiled=True, axis_index_groups=chip_groups)

time: 94.3 us -> 91.7 us (0.972)
  the two profiles are of different devices: /device:TPU:100 before, /device:TPU:34 now
where the time goes in v5:
time: 91.7 us; the launch traced here: 91.3 us
  Pallas kernels  24.9 us (27%)
  blocking collectives  21.9 us (24%)
  starting transfers between devices  21.6 us (24%)
  waiting for transfers between devices  19.3 us (21%)
  local copies, waits for them, and re-layouts  1.44 us (2%)
  loops' own time  1.15 us (1%)
    all_gather x1, blocking collectives, swapped(): lax.all_gather(give[:slots], 'win', axis=0, tiled=True, axis_index_groups...  21.9 us
    all_to_all x1, waiting for transfers between devices, path(): lax.all_to_all(deal, 'win', 0, 0, tiled=True, axis_index_groups=chip_groups)  10.6 us
    ppermute x2, waiting for transfers between devices, path(): came = [lax.ppermute(lane, 'chan', swap) for lane, swap in zip(sent, SWAPS)]  8.03 us
    ppermute x2, starting transfers between devices, path(): came = [lax.ppermute(lane, 'chan', swap) for lane, swap in zip(sent, SWAPS)]  7.05 us
    pallas_call x2, Pallas kernels, spectra(): pl.pallas_call(lambda *refs: spectra_kernel(count, base, at, *refs), out_...  6.99 us
    ppermute x2, starting transfers between devices, path(): lax.ppermute(lane, 'chan', swap)  6.54 us
    all_to_all x1, starting transfers between devices, path(): lax.all_to_all(deal, 'win', 0, 0, tiled=True, axis_index_groups=chip_groups)  4.48 us
    pallas_call x1, Pallas kernels, raw_products(): pl.pallas_call(lambda *refs: raw_products_kernel(width, *refs), out_shape...  4.28 us
  transfers between devices with their start and end apart: 6, of which 4 were waited for; matrix products, arithmetic and copies ran while one was open for 1% of the time, Pallas kernels for 23%

profile of v5, /device:TPU:34, one launch (start us, length us, event | category | flops | bytes accessed | tf_op | source)
XLA Modules:
  0.0 91.3 jit_solution(11399864272350539305)
XLA Ops:
  0.0 3.9 %prepare.1 = (s32[18]{0:T(128)S(1)}, s32[18]{0:T(128)S(1)}, s32[1]{0:T(128)}, bf16[8,3,2,8,2,1024]{5,4,3,2,1,0:T(2,128)(2,1)}, bf16[2,16,8,2,1024]{4,3,2,1,0:T(2...) custom-call(s32[1]{0:T(128)} %bitcast.14.where, s32[2,80]{1,0:T(2,128)} %bitcast.43, s32[1,80]{1,0:T(1,128)} %bitcast.44, ...), custom_call_target="tpu_custom_call" | custom-call | bytes 7340032 | tf_op jit(solution)/shard_map/prepare/pallas_call | solution.py:217
  4.6 85.9 %conditional.3 = (f32[4,16,1024]{2,1,0:T(8,128)S(1)}) conditional(s32[]{:T(128)} %bitcast.18, (bf16[8,3,2,8,2,1024]{5,4,3,2,1,0:T(2,128)(2,1)}, s32[18]{0:T(128)S(1)}, bf16[1024,1024]{1,0:T(8,128)(2,1)}, bf16[3,256,2,1024]{3,2,1,0:T(2,128)(2,1)}) %tuple.29, (bf16[8,3,2,8,2,1024]{5,4,3,2,1,0:T(2,128)(2,1)}, s32[18]{0:T(128)S(1)}, ...), branch_computations={%region_0.4_spmd, %region_4.8_spmd} | conditional | flops 8088059904 | bytes 125043400 | solution.py:536
  4.6 4.5 %all-to-all-start.2 = ((bf16[8,3,2,8,2,1024]{5,4,3,2,1,0:T(2,128)(2,1)}), bf16[8,3,2,8,2,1024]{5,4,3,2,1,0:T(2,128)(2,1)S(1)}, u32[]{:S(2)}, u32[]{:S(2)}) async-start(bf16[8,3,2,8,2,1024]{5,4,3,2,1,0:T(2,128)(2,1)} %get-tuple-element.74), calls=%async_computation.2 | async-start | bytes 3145728 | tf_op jit(solution)/shard_map/cond/branch_1_fun/all_to_all | solution.py:495
  9.1 3.3 %collective-permute-start.4 = (bf16[2,16,8,2,1024]{4,3,2,1,0:T(2,128)(2,1)}, bf16[2,16,8,2,1024]{4,3,2,1,0:T(2,128)(2,1)}, u32[]{:S(2)}, u32[]{:S(2)}) collective-permute-start(bf16[2,16,8,2,1024]{4,3,2,1,0:T(2,128)(2,1)} %get-tuple-element.79), channel_id=1, source_target_pairs={{16,32},{32,16},{48,64},{64,48},{80,96},{96,80},{112,128},{128,112... | collective-permute-start | bytes 3145736 | tf_op jit(solution)/shard_map/cond/branch_1_fun/ppermute | solution.py:498
  12.4 3.3 %collective-permute-start.5 = (bf16[2,16,8,2,1024]{4,3,2,1,0:T(2,128)(2,1)}, bf16[2,16,8,2,1024]{4,3,2,1,0:T(2,128)(2,1)}, u32[]{:S(2)}, u32[]{:S(2)}) collective-permute-start(bf16[2,16,8,2,1024]{4,3,2,1,0:T(2,128)(2,1)} %get-tuple-element.80), channel_id=1, source_target_pairs={{0,16},{16,0},{32,48},{48,32},{64,80},{80,64},{96,112},{112,96},{1... | collective-permute-start | bytes 3145736 | tf_op jit(solution)/shard_map/cond/branch_1_fun/ppermute | solution.py:498
  15.7 4.5 %spectra.6.refs_2_ = bf16[3,256,1024]{2,1,0:T(8,128)(2,1)S(1)} custom-call(s32[18]{0:T(128)S(1)} %get-tuple-element.72.refs_0_, bf16[3,16,2,8,2,1024]{5,4,3,2,1,0:T(2,128)(2,1)} %bitcast.38, bf16[1024,1024]{1,0:T(8,128)(2,1)} %get-tuple-element.77.refs_2_.refs_1_.basis), custom_call_target="tpu_custom_call" | custom-call | flops 1610612736 | bytes 8388608 | tf_op jit(solution)/shard_map/cond/branch_1_fun/spectra/pallas_call | solution.py:274
  20.1 10.6 %all-to-all-done.2.refs_1_.x = bf16[8,3,2,8,2,1024]{5,4,3,2,1,0:T(2,128)(2,1)S(1)} async-done(((bf16[8,3,2,8,2,1024]{5,4,3,2,1,0:T(2,128)(2,1)}), bf16[8,3,2,8,2,1024]{5,4,3,2,1,0:T(2,128)(2,1)S(1)}, u32[]{:S(2)}, u32[]{:S(2)}) %all-to-all-start.2) | async-done | bytes 1572896 | tf_op jit(solution)/shard_map/cond/branch_1_fun/all_to_all | solution.py:495
  30.7 0.0 copy-start.4
  30.7 3.9 %dealt_lanes.3 = (bf16[2,256,1024]{2,1,0:T(8,128)(2,1)}, bf16[2,256,1024]{2,1,0:T(8,128)(2,1)}) custom-call(s32[18]{0:T(128)S(1)} %get-tuple-element.72.refs_0_, bf16[8,3,2,8,2,1024]{5,4,3,2,1,0:T(2,128)(2,1)S(1)} %all-to-all-done.2.refs_1_.x, bf16[1024,1024]{1,0:T(8,128)(2,1)} %get-tuple-element.77.refs_2_.refs_1_.basis), custom_call_target="tpu_custom_call" | custom-call | flops 1610612736 | bytes 8388608 | tf_op jit(solution)/shard_map/cond/branch_1_fun/dealt_lanes/pallas_call | solution.py:308
  34.6 3.8 %collective-permute-start.6 = (bf16[2,256,1024]{2,1,0:T(8,128)(2,1)}, bf16[2,256,1024]{2,1,0:T(8,128)(2,1)}, u32[]{:S(2)}, u32[]{:S(2)}) collective-permute-start(bf16[2,256,1024]{2,1,0:T(8,128)(2,1)} %get-tuple-element.82), channel_id=1, source_target_pairs={{16,32},{32,16},{48,64},{64,48},{80,96},{96,80},{112,128},{128,112... | collective-permute-start | bytes 3145736 | tf_op jit(solution)/shard_map/cond/branch_1_fun/ppermute | solution.py:501
  38.4 3.3 %collective-permute-start.7 = (bf16[2,256,1024]{2,1,0:T(8,128)(2,1)}, bf16[2,256,1024]{2,1,0:T(8,128)(2,1)}, u32[]{:S(2)}, u32[]{:S(2)}) collective-permute-start(bf16[2,256,1024]{2,1,0:T(8,128)(2,1)} %get-tuple-element.83), channel_id=1, source_target_pairs={{0,16},{16,0},{32,48},{48,32},{64,80},{80,64},{96,112},{112,96},{1... | collective-permute-start | bytes 3145736 | tf_op jit(solution)/shard_map/cond/branch_1_fun/ppermute | solution.py:501
  41.7 0.0 collective-permute-done.4.refs_1_
  41.7 0.0 copy-done.4
  41.7 2.5 %spectra.7.refs_3_ = bf16[2,256,1024]{2,1,0:T(8,128)(2,1)S(1)} custom-call(s32[18]{0:T(128)S(1)} %get-tuple-element.72.refs_0_, bf16[2,16,8,2,1024]{4,3,2,1,0:T(2,128)(2,1)} %collective-permute-done.4.refs_1_, bf16[1024,1024]{1,0:T(8,128)(2,1)S(1)} %copy-done.4), custom_call_target="tpu_custom_call" | custom-call | flops 1610612736 | bytes 8388608 | tf_op jit(solution)/shard_map/cond/branch_1_fun/spectra/pallas_call | solution.py:274
  44.2 0.0 collective-permute-done.5.refs_4_
  44.2 4.3 %raw_products.3 = bf16[8,4,16,1024]{3,2,1,0:T(8,128)(2,1)} custom-call(s32[18]{0:T(128)S(1)} %get-tuple-element.72.refs_0_, bf16[1024,1024]{1,0:T(8,128)(2,1)S(1)} %copy-done.4, bf16[3,256,1024]{2,1,0:T(8,128)(2,1)S(1)} %spectra.6.refs_2_, bf16[2,256,1024]{2,1,0:T(8,128)(2,1)S(1)} %spectra.7.refs_3_, bf16[2,16,8,2,1024]{4,3,2,1,0:T(2,128)(2,1)} %collective-permute-done.5.refs_4_), custom_call_target="tpu_custom_call" | custom-call | flops 1610612736 | bytes 8388608 | tf_op jit(solution)/shard_map/cond/branch_1_fun/raw_products/pallas_call | solution.py:403
  48.5 3.6 %all-to-all-start.3 = ((bf16[8,4,16,1024]{3,2,1,0:T(8,128)(2,1)}), bf16[8,4,16,1024]{3,2,1,0:T(8,128)(2,1)S(1)}, u32[]{:S(2)}, u32[]{:S(2)}) async-start(bf16[8,4,16,1024]{3,2,1,0:T(8,128)(2,1)} %raw_products.3), calls=%async_computation.3 | async-start | bytes 2097152 | tf_op jit(solution)/shard_map/cond/branch_1_fun/all_to_all | solution.py:506
  52.1 0.7 slice.11
  53.5 3.5 %dealt_spectra.3.refs_1_ = bf16[3,256,1024]{2,1,0:T(8,128)(2,1)S(1)} custom-call(bf16[8,3,2,8,2,1024]{5,4,3,2,1,0:T(2,128)(2,1)S(1)} %all-to-all-done.2.refs_1_.x, bf16[1024,1024]{1,0:T(8,128)(2,1)} %get-tuple-element.77.refs_2_.refs_1_.basis), custom_call_target="tpu_custom_call" | custom-call | flops 1610612736 | bytes 8388608 | tf_op jit(solution)/shard_map/cond/branch_1_fun/dealt_spectra/pallas_call | solution.py:329
  57.0 4.7 %collective-permute-done.6.refs_2_ = bf16[2,256,1024]{2,1,0:T(8,128)(2,1)} collective-permute-done((bf16[2,256,1024]{2,1,0:T(8,128)(2,1)}, bf16[2,256,1024]{2,1,0:T(8,128)(2,1)}, u32[]{:S(2)}, u32[]{:S(2)}) %collective-permute-start.6) | collective-permute-done | bytes 1048608 | tf_op jit(solution)/shard_map/cond/branch_1_fun/ppermute | solution.py:501
  61.7 3.4 %collective-permute-done.7.refs_3_ = bf16[2,256,1024]{2,1,0:T(8,128)(2,1)} collective-permute-done((bf16[2,256,1024]{2,1,0:T(8,128)(2,1)}, bf16[2,256,1024]{2,1,0:T(8,128)(2,1)}, u32[]{:S(2)}, u32[]{:S(2)}) %collective-permute-start.7) | collective-permute-done | bytes 1048608 | tf_op jit(solution)/shard_map/cond/branch_1_fun/ppermute | solution.py:501
  65.0 2.2 %dealt_products.3 = f32[2,4,8,1024]{3,2,1,0:T(8,128)S(1)} custom-call(s32[18]{0:T(128)S(1)} %get-tuple-element.72.refs_0_, bf16[3,256,1024]{2,1,0:T(8,128)(2,1)S(1)} %dealt_spectra.3.refs_1_, bf16[2,256,1024]{2,1,0:T(8,128)(2,1)} %collective-permute-done.6.refs_2_, bf16[2,256,1024]{2,1,0:T(8,128)(2,1)} %collective-permute-done.7.refs_3_), custom_call_target="tpu_custom_call" | custom-call | flops 33554432 | bytes 8388608 | tf_op jit(solution)/shard_map/cond/branch_1_fun/dealt_products/pallas_call | solution.py:472
  67.3 0.7 all-to-all-done.3
  68.0 0.2 convert_reduce_fusion.1
  68.3 22.0 %conditional.1 = (f32[4,16,1024]{2,1,0:T(8,128)S(1)}) conditional(s32[]{:T(128)} %bitcast.11, (bf16[4,16,1024]{2,1,0:T(8,128)(2,1)S(1)}, s32[]{:T(128)}) %tuple.25, (bf16[4,16,1024]{2,1,0:T(8,128)(2,1)S(1)}, s32[]{:T(128)}) %tuple.25), branch_computations={%region_6.6_spmd, %region_7.7_spmd} | conditional | flops 65541 | bytes 786502 | solution.py:528
  68.3 21.9 %all_gather.10 = bf16[4,16,1024]{2,1,0:T(8,128)(2,1)S(1)} all-gather(bf16[2,16,1024]{2,1,0:T(8,128)(2,1)S(1)} %slice.10), channel_id=1, replica_groups={{0,8},{1,9},{2,10},{3,11},{4,12},{5,13},{6,14},{7,15},{16,24},{17,25},{..., dimensions={0}, use_global_device_ids=true | all-gather | bytes 196608 | tf_op jit(solution)/shard_map/cond/branch_1_fun/cond/branch_0_fun/all_gather | solution.py:524
  90.5 0.0 copy-start.5
  90.6 0.7 copy-done.5
  (9 shorter events, 0.1 us)
Async XLA Ops:
  4.6 26.1 %all-to-all-start.2 = ((bf16[8,3,2,8,2,1024]{5,4,3,2,1,0:T(2,128)(2,1)}), bf16[8,3,2,8,2,1024]{5,4,3,2,1,0:T(2,128)(2,1)S(1)}, u32[]{:S(2)}, u32[]{:S(2)}) async-start(bf16[8,3,2,8,2,1024]{5,4,3,2,1,0:T(2,128)(2,1)} %get-tuple-element.74), calls=%async_computation.2 | async-start | bytes 3145728 | tf_op jit(solution)/shard_map/cond/branch_1_fun/all_to_all | solution.py:495
  9.1 32.6 %collective-permute-start.4 = (bf16[2,16,8,2,1024]{4,3,2,1,0:T(2,128)(2,1)}, bf16[2,16,8,2,1024]{4,3,2,1,0:T(2,128)(2,1)}, u32[]{:S(2)}, u32[]{:S(2)}) collective-permute-start(bf16[2,16,8,2,1024]{4,3,2,1,0:T(2,128)(2,1)} %get-tuple-element.79), channel_id=1, source_target_pairs={{16,32},{32,16},{48,64},{64,48},{80,96},{96,80},{112,128},{128,112... | collective-permute-start | bytes 3145736 | tf_op jit(solution)/shard_map/cond/branch_1_fun/ppermute | solution.py:498
  12.4 31.8 %collective-permute-start.5 = (bf16[2,16,8,2,1024]{4,3,2,1,0:T(2,128)(2,1)}, bf16[2,16,8,2,1024]{4,3,2,1,0:T(2,128)(2,1)}, u32[]{:S(2)}, u32[]{:S(2)}) collective-permute-start(bf16[2,16,8,2,1024]{4,3,2,1,0:T(2,128)(2,1)} %get-tuple-element.80), channel_id=1, source_target_pairs={{0,16},{16,0},{32,48},{48,32},{64,80},{80,64},{96,112},{112,96},{1... | collective-permute-start | bytes 3145736 | tf_op jit(solution)/shard_map/cond/branch_1_fun/ppermute | solution.py:498
  30.7 11.0 %copy-start.4 = (bf16[1024,1024]{1,0:T(8,128)(2,1)S(1)}, bf16[1024,1024]{1,0:T(8,128)(2,1)}, u32[]{:S(2)}) copy-start(bf16[1024,1024]{1,0:T(8,128)(2,1)} %get-tuple-element.77.refs_2_.refs_1_.basis) | copy-start | bytes 6291460 | tf_op jit(solution)/shard_map/cond
  34.6 27.0 %collective-permute-start.6 = (bf16[2,256,1024]{2,1,0:T(8,128)(2,1)}, bf16[2,256,1024]{2,1,0:T(8,128)(2,1)}, u32[]{:S(2)}, u32[]{:S(2)}) collective-permute-start(bf16[2,256,1024]{2,1,0:T(8,128)(2,1)} %get-tuple-element.82), channel_id=1, source_target_pairs={{16,32},{32,16},{48,64},{64,48},{80,96},{96,80},{112,128},{128,112... | collective-permute-start | bytes 3145736 | tf_op jit(solution)/shard_map/cond/branch_1_fun/ppermute | solution.py:501
  38.4 26.6 %collective-permute-start.7 = (bf16[2,256,1024]{2,1,0:T(8,128)(2,1)}, bf16[2,256,1024]{2,1,0:T(8,128)(2,1)}, u32[]{:S(2)}, u32[]{:S(2)}) collective-permute-start(bf16[2,256,1024]{2,1,0:T(8,128)(2,1)} %get-tuple-element.83), channel_id=1, source_target_pairs={{0,16},{16,0},{32,48},{48,32},{64,80},{80,64},{96,112},{112,96},{1... | collective-permute-start | bytes 3145736 | tf_op jit(solution)/shard_map/cond/branch_1_fun/ppermute | solution.py:501
  48.5 19.5 %all-to-all-start.3 = ((bf16[8,4,16,1024]{3,2,1,0:T(8,128)(2,1)}), bf16[8,4,16,1024]{3,2,1,0:T(8,128)(2,1)S(1)}, u32[]{:S(2)}, u32[]{:S(2)}) async-start(bf16[8,4,16,1024]{3,2,1,0:T(8,128)(2,1)} %raw_products.3), calls=%async_computation.3 | async-start | bytes 2097152 | tf_op jit(solution)/shard_map/cond/branch_1_fun/all_to_all | solution.py:506
  90.5 0.7 copy-start.5

commit v6 on v5

--- a/solution.py
+++ b/solution.py
@@ -385,7 +385,7 @@
             def _(peer):
                 for lane in range(BINS // 128):
                     for z in range(2):
-                        acc[lane, z, 0], acc[lane, z, 1] = parts(read, tile(z * 8 + peer), lane)
+                        acc[lane, z, 0], acc[lane, z, 1] = parts(read, tile(z * 8 + (peer + 4) % 8), lane)
                     for part in range(2):
                         sums = [pair_sums(acc.at[lane, z, part]) for z in range(2)]
                         out[peer, slot, :, pl.ds(part * BINS + lane * 128, 128)] = jnp.concatenate(
@@ -490,6 +490,7 @@
     basis = jnp.asarray(basis_table())
     x = records.reshape(BLOCKS, 16, CHUNKS, HALF, 2, LENGTH)
     chip_groups = [[z * 8 + j for j in range(8)] for z in range(2)]
+    turned_groups = [[z * 8 + (j + 4) % 8 for j in range(8)] for z in range(2)]
     far_groups = [[z * 8 + j for z in range(2)] for j in range(8)]
 
     dealt = lax.all_to_all(deal, "win", 0, 0, tiled=True, axis_index_groups=chip_groups)
@@ -503,7 +504,7 @@
     one = spectra(width, BLOCKS, lambda spot: (spot,), info, raw_one, raw_basis)
 
     part = raw_products(width, info, raw_basis, own, one, raw_two)
-    first = lax.all_to_all(part, "win", 0, 0, tiled=True, axis_index_groups=chip_groups)
+    first = lax.all_to_all(part, "win", 0, 0, tiled=True, axis_index_groups=turned_groups)
     dealt, part = lax.optimization_barrier((dealt, part))
     second = dealt_products(width, info, dealt_spectra(dealt, basis), *came)
     first, second = lax.optimization_barrier((first, second))

time: 91.7 us -> 115 us (1.25)
  the two profiles are of different devices: /device:TPU:34 before, /device:TPU:2 now
where the time goes in v6:
time: 115 us; the launch traced here: 114 us
  waiting for transfers between devices  32.9 us (29%)
  starting transfers between devices  28.4 us (25%)
  Pallas kernels  26.6 us (23%)
  blocking collectives  20.3 us (18%)
  local copies, waits for them, and re-layouts  2.8 us (2%)
  other arithmetic  1.49 us (1%)
    all_gather x1, blocking collectives, swapped(): lax.all_gather(give[:slots], 'win', axis=0, tiled=True, axis_index_groups...  20.3 us
    ppermute x2, waiting for transfers between devices, path(): came = [lax.ppermute(lane, 'chan', swap) for lane, swap in zip(sent, SWAPS)]  15.1 us
    all_to_all x1, waiting for transfers between devices, path(): lax.all_to_all(deal, 'win', 0, 0, tiled=True, axis_index_groups=chip_groups)  9.45 us
    ppermute x2, starting transfers between devices, path(): lax.ppermute(lane, 'chan', swap)  8.75 us
    ppermute x2, waiting for transfers between devices, path(): lax.ppermute(lane, 'chan', swap)  8.31 us
    ppermute x2, starting transfers between devices, path(): came = [lax.ppermute(lane, 'chan', swap) for lane, swap in zip(sent, SWAPS)]  7.64 us
    all_to_all x1, starting transfers between devices, path(): lax.all_to_all(part, 'win', 0, 0, tiled=True, axis_index_groups=turned_gr...  7.52 us
    pallas_call x1, Pallas kernels, dealt_lanes(): pl.pallas_call(lambda *refs: dealt_kernel(width, *refs), out_shape=(lane,...  5.68 us
  transfers between devices with their start and end apart: 6, of which 5 were waited for; matrix products, arithmetic and copies ran while one was open for 1% of the time, Pallas kernels for 20%

profile of v6, /device:TPU:2, one launch (start us, length us, event | category | flops | bytes accessed | tf_op | source)
XLA Modules:
  0.0 114.3 jit_solution(17838241854267719528)
XLA Ops:
  0.0 3.8 %prepare.1 = (s32[18]{0:T(128)S(1)}, s32[18]{0:T(128)S(1)}, s32[1]{0:T(128)}, bf16[8,3,2,8,2,1024]{5,4,3,2,1,0:T(2,128)(2,1)}, bf16[2,16,8,2,1024]{4,3,2,1,0:T(2...) custom-call(s32[1]{0:T(128)} %bitcast.14.where, s32[2,80]{1,0:T(2,128)} %bitcast.43, s32[1,80]{1,0:T(1,128)} %bitcast.44, ...), custom_call_target="tpu_custom_call" | custom-call | bytes 7340032 | tf_op jit(solution)/shard_map/prepare/pallas_call | solution.py:217
  4.5 109.0 %conditional.3 = (f32[4,16,1024]{2,1,0:T(8,128)S(1)}) conditional(s32[]{:T(128)} %bitcast.18, (bf16[8,3,2,8,2,1024]{5,4,3,2,1,0:T(2,128)(2,1)}, s32[18]{0:T(128)S(1)}, bf16[1024,1024]{1,0:T(8,128)(2,1)}, bf16[3,256,2,1024]{3,2,1,0:T(2,128)(2,1)}) %tuple.29, (bf16[8,3,2,8,2,1024]{5,4,3,2,1,0:T(2,128)(2,1)}, s32[18]{0:T(128)S(1)}, ...), branch_computations={%region_0.4_spmd, %region_4.8_spmd} | conditional | flops 8088059904 | bytes 125043400 | solution.py:537
  4.5 4.5 %all-to-all-start = ((bf16[8,3,2,8,2,1024]{5,4,3,2,1,0:T(2,128)(2,1)}), bf16[8,3,2,8,2,1024]{5,4,3,2,1,0:T(2,128)(2,1)S(1)}, u32[]{:S(2)}, u32[]{:S(2)}) async-start(bf16[8,3,2,8,2,1024]{5,4,3,2,1,0:T(2,128)(2,1)} %get-tuple-element.56), calls=%async_computation | async-start | bytes 3145728 | tf_op jit(solution)/shard_map/cond/branch_0_fun/all_to_all | solution.py:496
  9.0 3.4 %raw_lanes.1 = (bf16[3,16,8,2,1024]{4,3,2,1,0:T(2,128)(2,1)}, bf16[3,16,8,2,1024]{4,3,2,1,0:T(2,128)(2,1)}) custom-call(s32[18]{0:T(128)S(1)} %get-tuple-element.54.refs_0_, bf16[3,16,2,8,2,1024]{5,4,3,2,1,0:T(2,128)(2,1)} %bitcast.36), custom_call_target="tpu_custom_call" | custom-call | bytes 4194304 | tf_op jit(solution)/shard_map/cond/branch_0_fun/raw_lanes/pallas_call | solution.py:160
  12.4 3.4 %collective-permute-start = (bf16[3,16,8,2,1024]{4,3,2,1,0:T(2,128)(2,1)}, bf16[3,16,8,2,1024]{4,3,2,1,0:T(2,128)(2,1)}, u32[]{:S(2)}, u32[]{:S(2)}) collective-permute-start(bf16[3,16,8,2,1024]{4,3,2,1,0:T(2,128)(2,1)} %get-tuple-element.61), channel_id=1, source_target_pairs={{16,32},{32,16},{48,64},{64,48},{80,96},{96,80},{112,128},{128,112... | collective-permute-start | bytes 4718600 | tf_op jit(solution)/shard_map/cond/branch_0_fun/ppermute | solution.py:499
  15.8 5.3 %collective-permute-start.1 = (bf16[3,16,8,2,1024]{4,3,2,1,0:T(2,128)(2,1)}, bf16[3,16,8,2,1024]{4,3,2,1,0:T(2,128)(2,1)}, u32[]{:S(2)}, u32[]{:S(2)}) collective-permute-start(bf16[3,16,8,2,1024]{4,3,2,1,0:T(2,128)(2,1)} %get-tuple-element.62), channel_id=1, source_target_pairs={{0,16},{16,0},{32,48},{48,32},{64,80},{80,64},{96,112},{112,96},{1... | collective-permute-start | bytes 4718600 | tf_op jit(solution)/shard_map/cond/branch_0_fun/ppermute | solution.py:499
  21.1 9.4 %all-to-all-done.refs_1_.x = bf16[8,3,2,8,2,1024]{5,4,3,2,1,0:T(2,128)(2,1)S(1)} async-done(((bf16[8,3,2,8,2,1024]{5,4,3,2,1,0:T(2,128)(2,1)}), bf16[8,3,2,8,2,1024]{5,4,3,2,1,0:T(2,128)(2,1)S(1)}, u32[]{:S(2)}, u32[]{:S(2)}) %all-to-all-start) | async-done | bytes 1572896 | tf_op jit(solution)/shard_map/cond/branch_0_fun/all_to_all | solution.py:496
  30.6 0.0 copy-start
  30.6 0.0 copy-start.2
  30.6 0.0 copy-start.3
  30.6 5.7 %dealt_lanes.2 = (bf16[3,256,1024]{2,1,0:T(8,128)(2,1)}, bf16[3,256,1024]{2,1,0:T(8,128)(2,1)}) custom-call(s32[18]{0:T(128)S(1)} %get-tuple-element.54.refs_0_, bf16[8,3,2,8,2,1024]{5,4,3,2,1,0:T(2,128)(2,1)S(1)} %all-to-all-done.refs_1_.x, bf16[1024,1024]{1,0:T(8,128)(2,1)} %get-tuple-element.59.refs_2_.refs_1_.basis), custom_call_target="tpu_custom_call" | custom-call | flops 1610612736 | bytes 8388608 | tf_op jit(solution)/shard_map/cond/branch_0_fun/dealt_lanes/pallas_call | solution.py:308
  36.3 0.0 copy-done
  36.3 3.4 %collective-permute-start.2 = (bf16[3,256,1024]{2,1,0:T(8,128)(2,1)}, bf16[3,256,1024]{2,1,0:T(8,128)(2,1)S(1)}, u32[]{:S(2)}, u32[]{:S(2)}) collective-permute-start(bf16[3,256,1024]{2,1,0:T(8,128)(2,1)} %get-tuple-element.64), channel_id=1, source_target_pairs={{16,32},{32,16},{48,64},{64,48},{80,96},{96,80},{112,128},{128,112... | collective-permute-start | bytes 4718600 | tf_op jit(solution)/shard_map/cond/branch_0_fun/ppermute | solution.py:502
  39.7 4.2 %collective-permute-start.3 = (bf16[3,256,1024]{2,1,0:T(8,128)(2,1)}, bf16[3,256,1024]{2,1,0:T(8,128)(2,1)S(1)}, u32[]{:S(2)}, u32[]{:S(2)}) collective-permute-start(bf16[3,256,1024]{2,1,0:T(8,128)(2,1)} %get-tuple-element.65), channel_id=1, source_target_pairs={{0,16},{16,0},{32,48},{48,32},{64,80},{80,64},{96,112},{112,96},{1... | collective-permute-start | bytes 4718600 | tf_op jit(solution)/shard_map/cond/branch_0_fun/ppermute | solution.py:502
  43.9 0.0 copy-done.2
  43.9 0.0 copy-done.3
  44.0 1.7 %spectra.4.refs_2_ = bf16[3,256,1024]{2,1,0:T(8,128)(2,1)S(1)} custom-call(s32[18]{0:T(128)S(1)} %get-tuple-element.54.refs_0_, bf16[3,16,2,8,2,1024]{5,4,3,2,1,0:T(2,128)(2,1)S(1)} %bitcast.37, bf16[1024,1024]{1,0:T(8,128)(2,1)S(1)} %copy-done.3), custom_call_target="tpu_custom_call" | custom-call | flops 1610612736 | bytes 8388608 | tf_op jit(solution)/shard_map/cond/branch_0_fun/spectra/pallas_call | solution.py:274
  45.7 6.1 %collective-permute-done.refs_1_ = bf16[3,16,8,2,1024]{4,3,2,1,0:T(2,128)(2,1)} collective-permute-done((bf16[3,16,8,2,1024]{4,3,2,1,0:T(2,128)(2,1)}, bf16[3,16,8,2,1024]{4,3,2,1,0:T(2,128)(2,1)}, u32[]{:S(2)}, u32[]{:S(2)}) %collective-permute-start) | collective-permute-done | bytes 1572896 | tf_op jit(solution)/shard_map/cond/branch_0_fun/ppermute | solution.py:499
  51.8 2.7 %spectra.5.refs_3_ = bf16[3,256,1024]{2,1,0:T(8,128)(2,1)S(1)} custom-call(s32[18]{0:T(128)S(1)} %get-tuple-element.54.refs_0_, bf16[3,16,8,2,1024]{4,3,2,1,0:T(2,128)(2,1)} %collective-permute-done.refs_1_, bf16[1024,1024]{1,0:T(8,128)(2,1)S(1)} %copy-done.3), custom_call_target="tpu_custom_call" | custom-call | flops 1610612736 | bytes 8388608 | tf_op jit(solution)/shard_map/cond/branch_0_fun/spectra/pallas_call | solution.py:274
  54.5 2.2 %collective-permute-done.1.refs_4_ = bf16[3,16,8,2,1024]{4,3,2,1,0:T(2,128)(2,1)} collective-permute-done((bf16[3,16,8,2,1024]{4,3,2,1,0:T(2,128)(2,1)}, bf16[3,16,8,2,1024]{4,3,2,1,0:T(2,128)(2,1)}, u32[]{:S(2)}, u32[]{:S(2)}) %collective-permute-start.1) | collective-permute-done | bytes 1572896 | tf_op jit(solution)/shard_map/cond/branch_0_fun/ppermute | solution.py:499
  56.7 4.4 %raw_products.2 = bf16[8,4,16,1024]{3,2,1,0:T(8,128)(2,1)} custom-call(s32[18]{0:T(128)S(1)} %get-tuple-element.54.refs_0_, bf16[1024,1024]{1,0:T(8,128)(2,1)S(1)} %copy-done.3, bf16[3,256,1024]{2,1,0:T(8,128)(2,1)S(1)} %spectra.4.refs_2_, bf16[3,256,1024]{2,1,0:T(8,128)(2,1)S(1)} %spectra.5.refs_3_, bf16[3,16,8,2,1024]{4,3,2,1,0:T(2,128)(2,1)} %collective-permute-done.1.refs_4_), custom_call_target="tpu_custom_call" | custom-call | flops 1610612736 | bytes 8388608 | tf_op jit(solution)/shard_map/cond/branch_0_fun/raw_products/pallas_call | solution.py:403
  61.1 7.5 %all-to-all-start.1 = ((bf16[8,4,16,1024]{3,2,1,0:T(8,128)(2,1)}), bf16[8,4,16,1024]{3,2,1,0:T(8,128)(2,1)}, u32[]{:S(2)}, u32[]{:S(2)}) async-start(bf16[8,4,16,1024]{3,2,1,0:T(8,128)(2,1)} %raw_products.2), calls=%async_computation.1 | async-start | bytes 2097152 | tf_op jit(solution)/shard_map/cond/branch_0_fun/all_to_all | solution.py:507
  68.6 0.6 slice.9
  69.9 0.0 copy-start.1
  69.9 1.4 %copy-done.1 = bf16[8,3,2,8,2,1024]{5,4,3,2,1,0:T(2,128)(2,1)S(1)} copy-done((bf16[8,3,2,8,2,1024]{5,4,3,2,1,0:T(2,128)(2,1)S(1)}, bf16[8,3,2,8,2,1024]{5,4,3,2,1,0:T(2,128)(2,1)}, u32[]{:S(2)}) %copy-start.1) | copy-done | bytes 1572888 | tf_op jit(solution)/shard_map/cond
  71.3 3.5 %dealt_spectra.2.refs_1_ = bf16[3,256,1024]{2,1,0:T(8,128)(2,1)S(1)} custom-call(bf16[8,3,2,8,2,1024]{5,4,3,2,1,0:T(2,128)(2,1)S(1)} %copy-done.1, bf16[1024,1024]{1,0:T(8,128)(2,1)} %get-tuple-element.59.refs_2_.refs_1_.basis), custom_call_target="tpu_custom_call" | custom-call | flops 1610612736 | bytes 8388608 | tf_op jit(solution)/shard_map/cond/branch_0_fun/dealt_spectra/pallas_call | solution.py:329
  74.9 10.1 %collective-permute-done.2.refs_2_ = bf16[3,256,1024]{2,1,0:T(8,128)(2,1)S(1)} collective-permute-done((bf16[3,256,1024]{2,1,0:T(8,128)(2,1)}, bf16[3,256,1024]{2,1,0:T(8,128)(2,1)S(1)}, u32[]{:S(2)}, u32[]{:S(2)}) %collective-permute-start.2) | collective-permute-done | bytes 1572896 | tf_op jit(solution)/shard_map/cond/branch_0_fun/ppermute | solution.py:502
  85.0 5.0 %collective-permute-done.3.refs_3_ = bf16[3,256,1024]{2,1,0:T(8,128)(2,1)S(1)} collective-permute-done((bf16[3,256,1024]{2,1,0:T(8,128)(2,1)}, bf16[3,256,1024]{2,1,0:T(8,128)(2,1)S(1)}, u32[]{:S(2)}, u32[]{:S(2)}) %collective-permute-start.3) | collective-permute-done | bytes 1572896 | tf_op jit(solution)/shard_map/cond/branch_0_fun/ppermute | solution.py:502
  90.0 1.4 %dealt_products.2 = f32[2,4,8,1024]{3,2,1,0:T(8,128)S(1)} custom-call(s32[18]{0:T(128)S(1)} %get-tuple-element.54.refs_0_, bf16[3,256,1024]{2,1,0:T(8,128)(2,1)S(1)} %dealt_spectra.2.refs_1_, bf16[3,256,1024]{2,1,0:T(8,128)(2,1)S(1)} %collective-permute-done.2.refs_2_, bf16[3,256,1024]{2,1,0:T(8,128)(2,1)S(1)} %collective-permute-done.3.refs_3_), custom_call_target="tpu_custom_call" | custom-call | flops 33554432 | bytes 8388608 | tf_op jit(solution)/shard_map/cond/branch_0_fun/dealt_products/pallas_call | solution.py:472
  91.4 0.0 all-to-all-done.1
  91.4 1.4 %convert_reduce_fusion = f32[4,16,1024]{2,1,0:T(8,128)S(1)} fusion(bf16[8,4,16,1024]{3,2,1,0:T(8,128)(2,1)} %all-to-all-done.1), kind=kLoop, calls=%fused_computation.3 | loop fusion | flops 983040 | bytes 1310720 | tf_op jit(solution)/shard_map/cond/branch_0_fun/reduce_sum | solution.py:511
  92.9 20.3 %conditional = (f32[4,16,1024]{2,1,0:T(8,128)S(1)}) conditional(s32[]{:T(128)} %bitcast.4, (bf16[4,16,1024]{2,1,0:T(8,128)(2,1)S(1)}, s32[]{:T(128)}) %tuple.20, (bf16[4,16,1024]{2,1,0:T(8,128)(2,1)S(1)}, s32[]{:T(128)}) %tuple.20), branch_computations={%region_2.2_spmd, %region_3.3_spmd} | conditional | flops 65541 | bytes 786502 | solution.py:529
  93.0 20.3 %all_gather.8 = bf16[4,16,1024]{2,1,0:T(8,128)(2,1)S(1)} all-gather(bf16[2,16,1024]{2,1,0:T(8,128)(2,1)S(1)} %slice.8), channel_id=1, replica_groups={{0,8},{1,9},{2,10},{3,11},{4,12},{5,13},{6,14},{7,15},{16,24},{17,25},{..., dimensions={0}, use_global_device_ids=true | all-gather | bytes 196608 | tf_op jit(solution)/shard_map/cond/branch_0_fun/cond/branch_0_fun/all_gather | solution.py:525
  113.5 0.0 copy-start.5
  113.6 0.7 copy-done.5
  (9 shorter events, 0.1 us)
Async XLA Ops:
  4.5 26.1 %all-to-all-start = ((bf16[8,3,2,8,2,1024]{5,4,3,2,1,0:T(2,128)(2,1)}), bf16[8,3,2,8,2,1024]{5,4,3,2,1,0:T(2,128)(2,1)S(1)}, u32[]{:S(2)}, u32[]{:S(2)}) async-start(bf16[8,3,2,8,2,1024]{5,4,3,2,1,0:T(2,128)(2,1)} %get-tuple-element.56), calls=%async_computation | async-start | bytes 3145728 | tf_op jit(solution)/shard_map/cond/branch_0_fun/all_to_all | solution.py:496
  12.4 39.4 %collective-permute-start = (bf16[3,16,8,2,1024]{4,3,2,1,0:T(2,128)(2,1)}, bf16[3,16,8,2,1024]{4,3,2,1,0:T(2,128)(2,1)}, u32[]{:S(2)}, u32[]{:S(2)}) collective-permute-start(bf16[3,16,8,2,1024]{4,3,2,1,0:T(2,128)(2,1)} %get-tuple-element.61), channel_id=1, source_target_pairs={{16,32},{32,16},{48,64},{64,48},{80,96},{96,80},{112,128},{128,112... | collective-permute-start | bytes 4718600 | tf_op jit(solution)/shard_map/cond/branch_0_fun/ppermute | solution.py:499
  15.8 40.9 %collective-permute-start.1 = (bf16[3,16,8,2,1024]{4,3,2,1,0:T(2,128)(2,1)}, bf16[3,16,8,2,1024]{4,3,2,1,0:T(2,128)(2,1)}, u32[]{:S(2)}, u32[]{:S(2)}) collective-permute-start(bf16[3,16,8,2,1024]{4,3,2,1,0:T(2,128)(2,1)} %get-tuple-element.62), channel_id=1, source_target_pairs={{0,16},{16,0},{32,48},{48,32},{64,80},{80,64},{96,112},{112,96},{1... | collective-permute-start | bytes 4718600 | tf_op jit(solution)/shard_map/cond/branch_0_fun/ppermute | solution.py:499
  30.6 5.7 %copy-start = (bf16[8,3,2,8,2,1024]{5,4,3,2,1,0:T(2,128)(2,1)}, bf16[8,3,2,8,2,1024]{5,4,3,2,1,0:T(2,128)(2,1)S(1)}, u32[]{:S(2)}) copy-start(bf16[8,3,2,8,2,1024]{5,4,3,2,1,0:T(2,128)(2,1)S(1)} %all-to-all-done.refs_1_.x) | copy-start | bytes 4718596 | tf_op jit(solution)/shard_map/cond
  30.6 13.4 %copy-start.2 = (bf16[3,256,2,1024]{3,2,1,0:T(2,128)(2,1)S(1)}, bf16[3,256,2,1024]{3,2,1,0:T(2,128)(2,1)}, u32[]{:S(2)}) copy-start(bf16[3,256,2,1024]{3,2,1,0:T(2,128)(2,1)} %get-tuple-element.60) | copy-start | bytes 9437188 | tf_op jit(solution)/shard_map/cond
  30.6 13.4 %copy-start.3 = (bf16[1024,1024]{1,0:T(8,128)(2,1)S(1)}, bf16[1024,1024]{1,0:T(8,128)(2,1)}, u32[]{:S(2)}) copy-start(bf16[1024,1024]{1,0:T(8,128)(2,1)} %get-tuple-element.59.refs_2_.refs_1_.basis) | copy-start | bytes 6291460 | tf_op jit(solution)/shard_map/cond
  36.3 48.7 %collective-permute-start.2 = (bf16[3,256,1024]{2,1,0:T(8,128)(2,1)}, bf16[3,256,1024]{2,1,0:T(8,128)(2,1)S(1)}, u32[]{:S(2)}, u32[]{:S(2)}) collective-permute-start(bf16[3,256,1024]{2,1,0:T(8,128)(2,1)} %get-tuple-element.64), channel_id=1, source_target_pairs={{16,32},{32,16},{48,64},{64,48},{80,96},{96,80},{112,128},{128,112... | collective-permute-start | bytes 4718600 | tf_op jit(solution)/shard_map/cond/branch_0_fun/ppermute | solution.py:502
  39.7 50.3 %collective-permute-start.3 = (bf16[3,256,1024]{2,1,0:T(8,128)(2,1)}, bf16[3,256,1024]{2,1,0:T(8,128)(2,1)S(1)}, u32[]{:S(2)}, u32[]{:S(2)}) collective-permute-start(bf16[3,256,1024]{2,1,0:T(8,128)(2,1)} %get-tuple-element.65), channel_id=1, source_target_pairs={{0,16},{16,0},{32,48},{48,32},{64,80},{80,64},{96,112},{112,96},{1... | collective-permute-start | bytes 4718600 | tf_op jit(solution)/shard_map/cond/branch_0_fun/ppermute | solution.py:502
  61.1 30.3 %all-to-all-start.1 = ((bf16[8,4,16,1024]{3,2,1,0:T(8,128)(2,1)}), bf16[8,4,16,1024]{3,2,1,0:T(8,128)(2,1)}, u32[]{:S(2)}, u32[]{:S(2)}) async-start(bf16[8,4,16,1024]{3,2,1,0:T(8,128)(2,1)} %raw_products.2), calls=%async_computation.1 | async-start | bytes 2097152 | tf_op jit(solution)/shard_map/cond/branch_0_fun/all_to_all | solution.py:507
  69.9 1.4 %copy-start.1 = (bf16[8,3,2,8,2,1024]{5,4,3,2,1,0:T(2,128)(2,1)S(1)}, bf16[8,3,2,8,2,1024]{5,4,3,2,1,0:T(2,128)(2,1)}, u32[]{:S(2)}) copy-start(bf16[8,3,2,8,2,1024]{5,4,3,2,1,0:T(2,128)(2,1)} %copy-done) | copy-start | bytes 4718596 | tf_op jit(solution)/shard_map/cond
  113.5 0.7 copy-start.5

commit v7 on v6

--- a/solution.py
+++ b/solution.py
@@ -174,7 +174,7 @@
 
 
 def prepare_kernel(where, pairs, owner, x, narrow, wide, flag, deal, one, two, *scratch):
-    pairs_here, owner_here, rows, psem, buf, xsem, dsem, lsem = scratch
+    pairs_here, owner_here, rows, psem, buf, laid, xsem, dsem, lsem = scratch
     small = [
         pltpu.make_async_copy(pairs, pairs_here, psem.at[0]),
         pltpu.make_async_copy(owner, owner_here, psem.at[1]),
@@ -190,13 +190,14 @@
             copy.start()
     deals = [
         [
-            pltpu.make_async_copy(buf.at[1, block, pl.ds(z * 8, 8)], deal.at[:, block, z], dsem.at[block, z])
+            pltpu.make_async_copy(laid.at[block, z], deal.at[:, block, z], dsem.at[block, z])
             for z in range(2)
         ]
         for block in range(BLOCKS)
     ]
     for block in range(BLOCKS):
         loads[1][block].wait()
+        laid[block] = buf[1, block].reshape(2, 8, 2 * HALF, LENGTH)
         for copy in deals[block]:
             copy.start()
     for copy in small:
@@ -220,7 +221,7 @@
             table,
             table,
             jax.ShapeDtypeStruct((1,), jnp.int32),
-            jax.ShapeDtypeStruct((8, BLOCKS, 2, HALF, 2, LENGTH), jnp.bfloat16),
+            jax.ShapeDtypeStruct((8, BLOCKS, 2, 2 * HALF, LENGTH), jnp.bfloat16),
             lane,
             lane,
         ),
@@ -232,6 +233,7 @@
             pltpu.VMEM((8, 128), jnp.float32),
             pltpu.SemaphoreType.DMA((2,)),
             pltpu.VMEM((CHUNKS, BLOCKS, 16, HALF, 2, LENGTH), jnp.bfloat16),
+            pltpu.VMEM((BLOCKS, 2, 8, 2 * HALF, LENGTH), jnp.bfloat16),
             pltpu.SemaphoreType.DMA((CHUNKS, BLOCKS)),
             pltpu.SemaphoreType.DMA((BLOCKS, 2)),
             pltpu.SemaphoreType.DMA((2, 2)),

time: 115 us -> 117 us (1.017)
  the two profiles are of different devices: /device:TPU:2 before, /device:TPU:32 now
where the time goes in v7:
time: 117 us
  waiting for transfers between devices  33.7 us (29%)
  Pallas kernels  27.5 us (24%)
  starting transfers between devices  25.7 us (22%)
  blocking collectives  23.8 us (20%)
  local copies, waits for them, and re-layouts  2.8 us (2%)
  other arithmetic  1.49 us (1%)
    all_gather x1, blocking collectives, swapped(): lax.all_gather(give[:slots], 'win', axis=0, tiled=True, axis_index_groups...  23.8 us
    ppermute x2, waiting for transfers between devices, path(): came = [lax.ppermute(lane, 'chan', swap) for lane, swap in zip(sent, SWAPS)]  13.9 us
    all_to_all x1, waiting for transfers between devices, path(): lax.all_to_all(deal, 'win', 0, 0, tiled=True, axis_index_groups=chip_groups)  11.4 us
    ppermute x2, waiting for transfers between devices, path(): lax.ppermute(lane, 'chan', swap)  8.32 us
    all_to_all x1, starting transfers between devices, path(): lax.all_to_all(part, 'win', 0, 0, tiled=True, axis_index_groups=turned_gr...  7.73 us
    ppermute x2, starting transfers between devices, path(): lax.ppermute(lane, 'chan', swap)  6.76 us
    ppermute x2, starting transfers between devices, path(): came = [lax.ppermute(lane, 'chan', swap) for lane, swap in zip(sent, SWAPS)]  6.75 us
    pallas_call x1, Pallas kernels, dealt_lanes(): pl.pallas_call(lambda *refs: dealt_kernel(width, *refs), out_shape=(lane,...  5.68 us
  transfers between devices with their start and end apart: 6, of which 4 were waited for; matrix products, arithmetic and copies ran while one was open for 1% of the time, Pallas kernels for 20%

profile of v7, /device:TPU:32, one launch (start us, length us, event | category | flops | bytes accessed | tf_op | source)
XLA Modules:
  0.0 116.8 jit_solution(6272711334846732913)
XLA Ops:
  0.0 3.9 %prepare.1 = (s32[18]{0:T(128)S(1)}, s32[18]{0:T(128)S(1)}, s32[1]{0:T(128)}, bf16[8,3,2,16,1024]{4,3,2,1,0:T(8,128)(2,1)}, bf16[2,16,8,2,1024]{4,3,2,1,0:T(2,128)(2,1)}, /*index=5*/bf16[2,16,8,2,1024]{4,3,2,1,0:T(2,128)(2,1)}) custom-call(s32[1]{0:T(128)} %bitcast.14.where, s32[2,80]{1,0:T(2,128)} %bitcast.43, s32[1,80]{1,0:T(1,128)} %bitcast.44, ...), custom_call_target="tpu_custom_call" | custom-call | bytes 7340032 | tf_op jit(solution)/shard_map/prepare/pallas_call | solution.py:218
  4.5 111.5 %conditional.3 = (f32[4,16,1024]{2,1,0:T(8,128)S(1)}) conditional(s32[]{:T(128)} %bitcast.18, (bf16[8,3,2,16,1024]{4,3,2,1,0:T(8,128)(2,1)}, s32[18]{0:T(128)S(1)}, bf16[1024,1024]{1,0:T(8,128)(2,1)}, bf16[3,256,2,1024]{3,2,1,0:T(2,128)(2,1)}) %tuple.29, (bf16[8,3,2,16,1024]{4,3,2,1,0:T(8,128)(2,1)}, s32[18]{0:T(128)S(1)}, ...), branch_computations={%region_0.4_spmd, %region_4.8_spmd} | conditional | flops 8088059904 | bytes 125043400 | solution.py:539
  4.6 4.5 %all-to-all-start = ((bf16[8,3,2,16,1024]{4,3,2,1,0:T(8,128)(2,1)}), bf16[8,3,2,16,1024]{4,3,2,1,0:T(8,128)(2,1)S(1)}, u32[]{:S(2)}, u32[]{:S(2)}) async-start(bf16[8,3,2,16,1024]{4,3,2,1,0:T(8,128)(2,1)} %get-tuple-element.56), calls=%async_computation | async-start | bytes 3145728 | tf_op jit(solution)/shard_map/cond/branch_0_fun/all_to_all | solution.py:498
  9.0 3.4 %raw_lanes.1 = (bf16[3,16,8,2,1024]{4,3,2,1,0:T(2,128)(2,1)}, bf16[3,16,8,2,1024]{4,3,2,1,0:T(2,128)(2,1)}) custom-call(s32[18]{0:T(128)S(1)} %get-tuple-element.54.refs_0_, bf16[3,16,2,8,2,1024]{5,4,3,2,1,0:T(2,128)(2,1)} %bitcast.36), custom_call_target="tpu_custom_call" | custom-call | bytes 4194304 | tf_op jit(solution)/shard_map/cond/branch_0_fun/raw_lanes/pallas_call | solution.py:160
  12.4 4.3 %collective-permute-start = (bf16[3,16,8,2,1024]{4,3,2,1,0:T(2,128)(2,1)}, bf16[3,16,8,2,1024]{4,3,2,1,0:T(2,128)(2,1)}, u32[]{:S(2)}, u32[]{:S(2)}) collective-permute-start(bf16[3,16,8,2,1024]{4,3,2,1,0:T(2,128)(2,1)} %get-tuple-element.61), channel_id=1, source_target_pairs={{16,32},{32,16},{48,64},{64,48},{80,96},{96,80},{112,128},{128,112... | collective-permute-start | bytes 4718600 | tf_op jit(solution)/shard_map/cond/branch_0_fun/ppermute | solution.py:501
  16.7 2.5 %collective-permute-start.1 = (bf16[3,16,8,2,1024]{4,3,2,1,0:T(2,128)(2,1)}, bf16[3,16,8,2,1024]{4,3,2,1,0:T(2,128)(2,1)}, u32[]{:S(2)}, u32[]{:S(2)}) collective-permute-start(bf16[3,16,8,2,1024]{4,3,2,1,0:T(2,128)(2,1)} %get-tuple-element.62), channel_id=1, source_target_pairs={{0,16},{16,0},{32,48},{48,32},{64,80},{80,64},{96,112},{112,96},{1... | collective-permute-start | bytes 4718600 | tf_op jit(solution)/shard_map/cond/branch_0_fun/ppermute | solution.py:501
  19.2 11.4 %all-to-all-done.refs_1_.x = bf16[8,3,2,16,1024]{4,3,2,1,0:T(8,128)(2,1)S(1)} async-done(((bf16[8,3,2,16,1024]{4,3,2,1,0:T(8,128)(2,1)}), bf16[8,3,2,16,1024]{4,3,2,1,0:T(8,128)(2,1)S(1)}, u32[]{:S(2)}, u32[]{:S(2)}) %all-to-all-start) | async-done | bytes 1572896 | tf_op jit(solution)/shard_map/cond/branch_0_fun/all_to_all | solution.py:498
  30.6 0.0 copy-start
  30.6 0.0 copy-start.2
  30.6 0.0 copy-start.3
  30.6 5.7 %dealt_lanes.2 = (bf16[3,256,1024]{2,1,0:T(8,128)(2,1)}, bf16[3,256,1024]{2,1,0:T(8,128)(2,1)}) custom-call(s32[18]{0:T(128)S(1)} %get-tuple-element.54.refs_0_, bf16[8,3,2,16,1024]{4,3,2,1,0:T(8,128)(2,1)S(1)} %all-to-all-done.refs_1_.x, bf16[1024,1024]{1,0:T(8,128)(2,1)} %get-tuple-element.59.refs_2_.refs_1_.basis), custom_call_target="tpu_custom_call" | custom-call | flops 1610612736 | bytes 8388608 | tf_op jit(solution)/shard_map/cond/branch_0_fun/dealt_lanes/pallas_call | solution.py:310
  36.3 0.0 copy-done
  36.3 4.3 %collective-permute-start.2 = (bf16[3,256,1024]{2,1,0:T(8,128)(2,1)}, bf16[3,256,1024]{2,1,0:T(8,128)(2,1)S(1)}, u32[]{:S(2)}, u32[]{:S(2)}) collective-permute-start(bf16[3,256,1024]{2,1,0:T(8,128)(2,1)} %get-tuple-element.64), channel_id=1, source_target_pairs={{16,32},{32,16},{48,64},{64,48},{80,96},{96,80},{112,128},{128,112... | collective-permute-start | bytes 4718600 | tf_op jit(solution)/shard_map/cond/branch_0_fun/ppermute | solution.py:504
  40.6 2.5 %collective-permute-start.3 = (bf16[3,256,1024]{2,1,0:T(8,128)(2,1)}, bf16[3,256,1024]{2,1,0:T(8,128)(2,1)S(1)}, u32[]{:S(2)}, u32[]{:S(2)}) collective-permute-start(bf16[3,256,1024]{2,1,0:T(8,128)(2,1)} %get-tuple-element.65), channel_id=1, source_target_pairs={{0,16},{16,0},{32,48},{48,32},{64,80},{80,64},{96,112},{112,96},{1... | collective-permute-start | bytes 4718600 | tf_op jit(solution)/shard_map/cond/branch_0_fun/ppermute | solution.py:504
  43.1 0.0 copy-done.2
  43.1 0.0 copy-done.3
  43.1 2.5 %spectra.4.refs_2_ = bf16[3,256,1024]{2,1,0:T(8,128)(2,1)S(1)} custom-call(s32[18]{0:T(128)S(1)} %get-tuple-element.54.refs_0_, bf16[3,16,2,8,2,1024]{5,4,3,2,1,0:T(2,128)(2,1)S(1)} %bitcast.37, bf16[1024,1024]{1,0:T(8,128)(2,1)S(1)} %copy-done.3), custom_call_target="tpu_custom_call" | custom-call | flops 1610612736 | bytes 8388608 | tf_op jit(solution)/shard_map/cond/branch_0_fun/spectra/pallas_call | solution.py:276
  45.6 8.3 %collective-permute-done.refs_1_ = bf16[3,16,8,2,1024]{4,3,2,1,0:T(2,128)(2,1)} collective-permute-done((bf16[3,16,8,2,1024]{4,3,2,1,0:T(2,128)(2,1)}, bf16[3,16,8,2,1024]{4,3,2,1,0:T(2,128)(2,1)}, u32[]{:S(2)}, u32[]{:S(2)}) %collective-permute-start) | collective-permute-done | bytes 1572896 | tf_op jit(solution)/shard_map/cond/branch_0_fun/ppermute | solution.py:501
  53.9 2.8 %spectra.5.refs_3_ = bf16[3,256,1024]{2,1,0:T(8,128)(2,1)S(1)} custom-call(s32[18]{0:T(128)S(1)} %get-tuple-element.54.refs_0_, bf16[3,16,8,2,1024]{4,3,2,1,0:T(2,128)(2,1)} %collective-permute-done.refs_1_, bf16[1024,1024]{1,0:T(8,128)(2,1)S(1)} %copy-done.3), custom_call_target="tpu_custom_call" | custom-call | flops 1610612736 | bytes 8388608 | tf_op jit(solution)/shard_map/cond/branch_0_fun/spectra/pallas_call | solution.py:276
  56.7 0.0 collective-permute-done.1.refs_4_
  56.7 4.4 %raw_products.2 = bf16[8,4,16,1024]{3,2,1,0:T(8,128)(2,1)} custom-call(s32[18]{0:T(128)S(1)} %get-tuple-element.54.refs_0_, bf16[1024,1024]{1,0:T(8,128)(2,1)S(1)} %copy-done.3, bf16[3,256,1024]{2,1,0:T(8,128)(2,1)S(1)} %spectra.4.refs_2_, bf16[3,256,1024]{2,1,0:T(8,128)(2,1)S(1)} %spectra.5.refs_3_, bf16[3,16,8,2,1024]{4,3,2,1,0:T(2,128)(2,1)} %collective-permute-done.1.refs_4_), custom_call_target="tpu_custom_call" | custom-call | flops 1610612736 | bytes 8388608 | tf_op jit(solution)/shard_map/cond/branch_0_fun/raw_products/pallas_call | solution.py:405
  61.2 7.7 %all-to-all-start.1 = ((bf16[8,4,16,1024]{3,2,1,0:T(8,128)(2,1)}), bf16[8,4,16,1024]{3,2,1,0:T(8,128)(2,1)}, u32[]{:S(2)}, u32[]{:S(2)}) async-start(bf16[8,4,16,1024]{3,2,1,0:T(8,128)(2,1)} %raw_products.2), calls=%async_computation.1 | async-start | bytes 2097152 | tf_op jit(solution)/shard_map/cond/branch_0_fun/all_to_all | solution.py:509
  68.9 0.6 slice.9
  70.2 0.0 copy-start.1
  70.2 1.4 %copy-done.1 = bf16[8,3,2,16,1024]{4,3,2,1,0:T(8,128)(2,1)S(1)} copy-done((bf16[8,3,2,16,1024]{4,3,2,1,0:T(8,128)(2,1)S(1)}, bf16[8,3,2,16,1024]{4,3,2,1,0:T(8,128)(2,1)}, u32[]{:S(2)}) %copy-start.1) | copy-done | bytes 1572888 | tf_op jit(solution)/shard_map/cond
  71.6 3.5 %dealt_spectra.2.refs_1_ = bf16[3,256,1024]{2,1,0:T(8,128)(2,1)S(1)} custom-call(bf16[8,3,2,16,1024]{4,3,2,1,0:T(8,128)(2,1)S(1)} %copy-done.1, bf16[1024,1024]{1,0:T(8,128)(2,1)} %get-tuple-element.59.refs_2_.refs_1_.basis), custom_call_target="tpu_custom_call" | custom-call | flops 1610612736 | bytes 8388608 | tf_op jit(solution)/shard_map/cond/branch_0_fun/dealt_spectra/pallas_call | solution.py:331
  75.1 12.0 %collective-permute-done.2.refs_2_ = bf16[3,256,1024]{2,1,0:T(8,128)(2,1)S(1)} collective-permute-done((bf16[3,256,1024]{2,1,0:T(8,128)(2,1)}, bf16[3,256,1024]{2,1,0:T(8,128)(2,1)S(1)}, u32[]{:S(2)}, u32[]{:S(2)}) %collective-permute-start.2) | collective-permute-done | bytes 1572896 | tf_op jit(solution)/shard_map/cond/branch_0_fun/ppermute | solution.py:504
  87.1 1.9 %collective-permute-done.3.refs_3_ = bf16[3,256,1024]{2,1,0:T(8,128)(2,1)S(1)} collective-permute-done((bf16[3,256,1024]{2,1,0:T(8,128)(2,1)}, bf16[3,256,1024]{2,1,0:T(8,128)(2,1)S(1)}, u32[]{:S(2)}, u32[]{:S(2)}) %collective-permute-start.3) | collective-permute-done | bytes 1572896 | tf_op jit(solution)/shard_map/cond/branch_0_fun/ppermute | solution.py:504
  89.0 1.4 %dealt_products.2 = f32[2,4,8,1024]{3,2,1,0:T(8,128)S(1)} custom-call(s32[18]{0:T(128)S(1)} %get-tuple-element.54.refs_0_, bf16[3,256,1024]{2,1,0:T(8,128)(2,1)S(1)} %dealt_spectra.2.refs_1_, bf16[3,256,1024]{2,1,0:T(8,128)(2,1)S(1)} %collective-permute-done.2.refs_2_, bf16[3,256,1024]{2,1,0:T(8,128)(2,1)S(1)} %collective-permute-done.3.refs_3_), custom_call_target="tpu_custom_call" | custom-call | flops 33554432 | bytes 8388608 | tf_op jit(solution)/shard_map/cond/branch_0_fun/dealt_products/pallas_call | solution.py:474
  90.4 0.0 all-to-all-done.1
  90.4 1.4 %convert_reduce_fusion = f32[4,16,1024]{2,1,0:T(8,128)S(1)} fusion(bf16[8,4,16,1024]{3,2,1,0:T(8,128)(2,1)} %all-to-all-done.1), kind=kLoop, calls=%fused_computation.3 | loop fusion | flops 983040 | bytes 1310720 | tf_op jit(solution)/shard_map/cond/branch_0_fun/reduce_sum | solution.py:513
  92.0 23.8 %conditional = (f32[4,16,1024]{2,1,0:T(8,128)S(1)}) conditional(s32[]{:T(128)} %bitcast.4, (bf16[4,16,1024]{2,1,0:T(8,128)(2,1)S(1)}, s32[]{:T(128)}) %tuple.20, (bf16[4,16,1024]{2,1,0:T(8,128)(2,1)S(1)}, s32[]{:T(128)}) %tuple.20), branch_computations={%region_2.2_spmd, %region_3.3_spmd} | conditional | flops 65541 | bytes 786502 | solution.py:531
  92.0 23.8 %all_gather.8 = bf16[4,16,1024]{2,1,0:T(8,128)(2,1)S(1)} all-gather(bf16[2,16,1024]{2,1,0:T(8,128)(2,1)S(1)} %slice.8), channel_id=1, replica_groups={{0,8},{1,9},{2,10},{3,11},{4,12},{5,13},{6,14},{7,15},{16,24},{17,25},{..., dimensions={0}, use_global_device_ids=true | all-gather | bytes 196608 | tf_op jit(solution)/shard_map/cond/branch_0_fun/cond/branch_0_fun/all_gather | solution.py:527
  116.1 0.0 copy-start.5
  116.1 0.7 copy-done.5
  (9 shorter events, 0.1 us)
Async XLA Ops:
  4.6 26.1 %all-to-all-start = ((bf16[8,3,2,16,1024]{4,3,2,1,0:T(8,128)(2,1)}), bf16[8,3,2,16,1024]{4,3,2,1,0:T(8,128)(2,1)S(1)}, u32[]{:S(2)}, u32[]{:S(2)}) async-start(bf16[8,3,2,16,1024]{4,3,2,1,0:T(8,128)(2,1)} %get-tuple-element.56), calls=%async_computation | async-start | bytes 3145728 | tf_op jit(solution)/shard_map/cond/branch_0_fun/all_to_all | solution.py:498
  12.4 41.5 %collective-permute-start = (bf16[3,16,8,2,1024]{4,3,2,1,0:T(2,128)(2,1)}, bf16[3,16,8,2,1024]{4,3,2,1,0:T(2,128)(2,1)}, u32[]{:S(2)}, u32[]{:S(2)}) collective-permute-start(bf16[3,16,8,2,1024]{4,3,2,1,0:T(2,128)(2,1)} %get-tuple-element.61), channel_id=1, source_target_pairs={{16,32},{32,16},{48,64},{64,48},{80,96},{96,80},{112,128},{128,112... | collective-permute-start | bytes 4718600 | tf_op jit(solution)/shard_map/cond/branch_0_fun/ppermute | solution.py:501
  16.7 40.0 %collective-permute-start.1 = (bf16[3,16,8,2,1024]{4,3,2,1,0:T(2,128)(2,1)}, bf16[3,16,8,2,1024]{4,3,2,1,0:T(2,128)(2,1)}, u32[]{:S(2)}, u32[]{:S(2)}) collective-permute-start(bf16[3,16,8,2,1024]{4,3,2,1,0:T(2,128)(2,1)} %get-tuple-element.62), channel_id=1, source_target_pairs={{0,16},{16,0},{32,48},{48,32},{64,80},{80,64},{96,112},{112,96},{1... | collective-permute-start | bytes 4718600 | tf_op jit(solution)/shard_map/cond/branch_0_fun/ppermute | solution.py:501
  30.6 5.7 %copy-start = (bf16[8,3,2,16,1024]{4,3,2,1,0:T(8,128)(2,1)}, bf16[8,3,2,16,1024]{4,3,2,1,0:T(8,128)(2,1)S(1)}, u32[]{:S(2)}) copy-start(bf16[8,3,2,16,1024]{4,3,2,1,0:T(8,128)(2,1)S(1)} %all-to-all-done.refs_1_.x) | copy-start | bytes 4718596 | tf_op jit(solution)/shard_map/cond
  30.6 12.5 %copy-start.2 = (bf16[3,256,2,1024]{3,2,1,0:T(2,128)(2,1)S(1)}, bf16[3,256,2,1024]{3,2,1,0:T(2,128)(2,1)}, u32[]{:S(2)}) copy-start(bf16[3,256,2,1024]{3,2,1,0:T(2,128)(2,1)} %get-tuple-element.60) | copy-start | bytes 9437188 | tf_op jit(solution)/shard_map/cond
  30.6 12.5 %copy-start.3 = (bf16[1024,1024]{1,0:T(8,128)(2,1)S(1)}, bf16[1024,1024]{1,0:T(8,128)(2,1)}, u32[]{:S(2)}) copy-start(bf16[1024,1024]{1,0:T(8,128)(2,1)} %get-tuple-element.59.refs_2_.refs_1_.basis) | copy-start | bytes 6291460 | tf_op jit(solution)/shard_map/cond
  36.3 50.8 %collective-permute-start.2 = (bf16[3,256,1024]{2,1,0:T(8,128)(2,1)}, bf16[3,256,1024]{2,1,0:T(8,128)(2,1)S(1)}, u32[]{:S(2)}, u32[]{:S(2)}) collective-permute-start(bf16[3,256,1024]{2,1,0:T(8,128)(2,1)} %get-tuple-element.64), channel_id=1, source_target_pairs={{16,32},{32,16},{48,64},{64,48},{80,96},{96,80},{112,128},{128,112... | collective-permute-start | bytes 4718600 | tf_op jit(solution)/shard_map/cond/branch_0_fun/ppermute | solution.py:504
  40.6 48.4 %collective-permute-start.3 = (bf16[3,256,1024]{2,1,0:T(8,128)(2,1)}, bf16[3,256,1024]{2,1,0:T(8,128)(2,1)S(1)}, u32[]{:S(2)}, u32[]{:S(2)}) collective-permute-start(bf16[3,256,1024]{2,1,0:T(8,128)(2,1)} %get-tuple-element.65), channel_id=1, source_target_pairs={{0,16},{16,0},{32,48},{48,32},{64,80},{80,64},{96,112},{112,96},{1... | collective-permute-start | bytes 4718600 | tf_op jit(solution)/shard_map/cond/branch_0_fun/ppermute | solution.py:504
  61.2 29.2 %all-to-all-start.1 = ((bf16[8,4,16,1024]{3,2,1,0:T(8,128)(2,1)}), bf16[8,4,16,1024]{3,2,1,0:T(8,128)(2,1)}, u32[]{:S(2)}, u32[]{:S(2)}) async-start(bf16[8,4,16,1024]{3,2,1,0:T(8,128)(2,1)} %raw_products.2), calls=%async_computation.1 | async-start | bytes 2097152 | tf_op jit(solution)/shard_map/cond/branch_0_fun/all_to_all | solution.py:509
  70.2 1.4 %copy-start.1 = (bf16[8,3,2,16,1024]{4,3,2,1,0:T(8,128)(2,1)S(1)}, bf16[8,3,2,16,1024]{4,3,2,1,0:T(8,128)(2,1)}, u32[]{:S(2)}) copy-start(bf16[8,3,2,16,1024]{4,3,2,1,0:T(8,128)(2,1)} %copy-done) | copy-start | bytes 4718596 | tf_op jit(solution)/shard_map/cond
  116.1 0.7 copy-start.5
